TPU v7x, 32 devices: a whole 2x2x4 slice. The times are simulated.
32 devices in a mesh: groups: 2 (over y), ctx: 4 (over z), head: 2 (over x), pair: 2 (over core).
Axes of the slice: x: 2, y: 2, z: 4, core: 2. Of those that a mesh axis runs over, the one named last changes fastest.
Arguments:
- queries: bfloat16 [4096, 16, 128], P(('groups', 'ctx', 'pair'), 'head'), parts along dimension 0, may hold values from -5 to 5
- key_vectors: bfloat16 [4096, 16, 128], P(('groups', 'ctx', 'pair'), 'head'), parts along dimension 0, may hold values from -5 to 5
- value_vectors: bfloat16 [4096, 16, 128], P(('groups', 'ctx', 'pair'), 'head'), parts along dimension 0, may hold values from -6 to 6
- targets: bfloat16 [4096, 16, 128], P(('groups', 'ctx', 'pair'), 'head'), parts along dimension 0, may hold values from -6 to 6
- token_weights: int32 [4096], P(('groups', 'ctx', 'pair')), parts along dimension 0, may hold values from 0 to 3
- sessions: int32 [4096], P(('groups', 'ctx', 'pair')), parts along dimension 0, may hold values from 0 to 5, never falling along the last dimension, each value on 1 to 682 neighbouring positions
- window_size: int32 [16], P('head'), may hold values from 256 to 1024, as said below
Outputs:
- attended: bfloat16 [4096, 16, 128], P(('groups', 'ctx', 'pair'), 'head'), parts along dimension 0
- grad_queries: bfloat16 [4096, 16, 128], P(('groups', 'ctx', 'pair'), 'head'), parts along dimension 0
- grad_keys: bfloat16 [4096, 16, 128], P(('groups', 'ctx', 'pair'), 'head'), parts along dimension 0
- grad_values: bfloat16 [4096, 16, 128], P(('groups', 'ctx', 'pair'), 'head'), parts along dimension 0
There are 2 independent parts, one for each index of `groups`. A program takes and returns all parts, laid end to end along the dimension named above; an argument that names none is the same for every part. Nothing has to cross between parts.
Inputs may be any that keep to these rules, and one draw needn't show every extreme that they name: `window_size`: some head's window equals 1024.
All inputs are finite; a program needn't handle non-finite values.
Results may differ from a plain program's by a relative error of at most 0.02.
Values may be sent and summed in bfloat16 or wider, within the bound.
No kernel may reach another device: no remote copies, remote signals or barrier semaphores. Data moves between devices by JAX's collectives and lax.ppermute only.
A program may use at most 128 MiB of HBM per device.

v0:
```python
import math

import jax
import jax.numpy as jnp
from jax import lax
from jax.sharding import PartitionSpec as P

WIN = 1024
BLOCK = 128


MASKED = -1e30
EPSILON = 1e-06


def carried_in(x, axis, join, neutral, backward):
    count = lax.axis_size(axis)
    place = lax.axis_index(axis)
    ahead = count - 1 - place if backward else place
    gathered = jax.tree.map(
        lambda a, kind: lax.all_gather(a.astype(kind), axis), x, (jnp.int32, jnp.bfloat16)
    )
    state = jax.tree.map(lambda a, e: jnp.zeros_like(a) + jnp.asarray(e, a.dtype), x, neutral)

    def one(hop, state):
        source = count - 1 - hop if backward else hop
        return join(
            state,
            jax.tree.map(
                lambda a, own: lax.dynamic_index_in_dim(a, source, 0, False).astype(own.dtype),
                gathered,
                x,
            ),
        )

    return lax.fori_loop(0, ahead, one, state)


def passed_along(x, axis, by):
    devices = lax.axis_size(axis)
    pairs = [(i, i + by) for i in range(devices) if 0 <= i + by < devices]
    return lax.ppermute(x, axis, pairs)


def contract(form, left, right):
    return jnp.einsum(form, left, right, preferred_element_type=jnp.float32)


def feature(values_in):
    raised = values_in.astype(jnp.float32)
    return jnp.where(raised > 0, raised + 1.0, jnp.exp(jnp.minimum(raised, 0.0)))


def feature_slope(values_in):
    raised = values_in.astype(jnp.float32)
    return jnp.where(raised > 0, 1.0, jnp.exp(jnp.minimum(raised, 0.0)))


def combine_states(early, late):
    session_a, summed_a = early
    session_b, summed_b = late
    keeping = jnp.logical_or(session_b < 0, session_a == session_b)
    factor = jnp.where(keeping, 1.0, 0.0).astype(summed_b.dtype)
    factor = factor.reshape(factor.shape + (1,) * (summed_b.ndim - factor.ndim))
    return (jnp.where(session_b < 0, session_a, session_b), summed_b + factor * summed_a)


def advance(running, incoming):
    return (combine_states(running, incoming), running)


def normalize(numerator):
    inverse_rms = lax.rsqrt(jnp.mean(numerator * numerator, axis=-1, keepdims=True) + EPSILON)
    return (numerator * inverse_rms, inverse_rms)


def linear_local(phi_q, phi_k, value_rows, sessions, block):
    length, head_count, head_width = phi_q.shape
    block_count = length // block
    phi_query = phi_q.reshape(block_count, block, head_count, head_width)
    phi_key = phi_k.reshape(block_count, block, head_count, head_width)
    value_blocks = value_rows.reshape(block_count, block, head_count, head_width)
    session_blocks = sessions.reshape(block_count, block)
    lower_tri = jnp.arange(block)[:, None] >= jnp.arange(block)[None, :]
    same_block = jnp.logical_and(
        lower_tri[None], session_blocks[:, :, None] == session_blocks[:, None, :]
    )[:, None]
    alike_scores = jnp.where(
        same_block, contract("nchk,nshk->nhcs", phi_query, phi_key), 0.0
    ).astype(jnp.bfloat16)
    within = contract("nhcs,nshd->nchd", alike_scores, value_blocks)
    last_session = session_blocks[:, -1]
    owned_rows = (session_blocks == last_session[:, None])[:, :, None, None]
    local_sum = contract(
        "nchk,nchd->nhkd", jnp.where(owned_rows, phi_key, jnp.zeros_like(phi_key)), value_blocks
    )
    identity = (jnp.array(-1, jnp.int32), jnp.zeros(local_sum.shape[1:], jnp.float32))
    summary, starts = lax.scan(advance, identity, (last_session, local_sum))
    cache = (
        phi_query,
        phi_key,
        value_blocks,
        session_blocks,
        same_block,
        alike_scores,
        within,
        starts,
    )
    return (cache, summary)


def linear_finish(cache, prefix):
    phi_query, phi_key, value_blocks, session_blocks, same_block, alike_scores, within, starts = (
        cache
    )
    start_session, start_state = combine_states(prefix, starts)
    rounded_start = start_state.astype(jnp.bfloat16)
    in_state = (session_blocks == start_session[:, None])[:, :, None, None]
    numerator = within + jnp.where(
        in_state, contract("nchk,nhkd->nchd", phi_query, rounded_start), 0.0
    )
    flat_shape = (-1,) + numerator.shape[2:]
    return (numerator.reshape(flat_shape), (start_session, rounded_start))


def linear_back_local(cache, grad_num):
    phi_query = cache[0]
    session_blocks = cache[3]
    grad_blocks = grad_num.reshape(phi_query.shape)
    first_session = session_blocks[:, 0]
    owned_rows = (session_blocks == first_session[:, None])[:, :, None, None]
    local_sum = contract(
        "nchk,nchd->nhkd", jnp.where(owned_rows, phi_query, jnp.zeros_like(phi_query)), grad_blocks
    )
    identity = (jnp.array(-1, jnp.int32), jnp.zeros(local_sum.shape[1:], jnp.float32))
    summary, block_ends = lax.scan(advance, identity, (first_session, local_sum), reverse=True)
    return ((grad_blocks, block_ends), summary)


def linear_back_finish(cache, forward_state, returned, suffix):
    phi_query, phi_key, value_blocks, session_blocks, same_block, alike_scores = (
        cache[0],
        cache[1],
        cache[2],
        cache[3],
        cache[4],
        cache[5],
    )
    start_session, rounded_start = forward_state
    grad_blocks, block_ends = returned
    end_session, end_state = combine_states(suffix, block_ends)
    later_state = end_state.astype(jnp.bfloat16)
    in_state = (session_blocks == start_session[:, None])[:, :, None, None]
    later_use = (session_blocks == end_session[:, None])[:, :, None, None]
    back_scores = jnp.where(
        same_block, contract("nchd,nshd->nhcs", grad_blocks, value_blocks), 0.0
    ).astype(jnp.bfloat16)
    grad_phi_q = contract("nhcs,nshk->nchk", back_scores, phi_key) + jnp.where(
        in_state, contract("nchd,nhkd->nchk", grad_blocks, rounded_start), 0.0
    )
    grad_phi_k = contract("nhcs,nchk->nshk", back_scores, phi_query) + jnp.where(
        later_use, contract("nshd,nhkd->nshk", value_blocks, later_state), 0.0
    )
    grad_v_lin = contract("nhcs,nchd->nshd", alike_scores, grad_blocks) + jnp.where(
        later_use, contract("nshk,nhkd->nshd", phi_key, later_state), 0.0
    )
    flat_shape = (-1,) + grad_phi_q.shape[2:]
    return (
        grad_phi_q.reshape(flat_shape),
        grad_phi_k.reshape(flat_shape),
        grad_v_lin.reshape(flat_shape),
    )


def window_scores(queries, held_block, offset, position, sessions, window_size):
    key_part, value_part, session_part = held_block
    length, head_count, head_width = queries.shape
    offsets_in = jnp.arange(length, dtype=jnp.int32)
    query_pos = position * length + offsets_in
    key_pos = (position - offset) * length + offsets_in
    distance = query_pos[:, None] - key_pos[None, :]
    allowed = (
        (key_pos[None, :] >= 0) & (distance >= 0) & (sessions[:, None] == session_part[None, :])
    )
    allowed = allowed[None] & (distance[None] < window_size[:, None, None])
    raw = contract("qhd,khd->hqk", queries, key_part) * (1.0 / math.sqrt(head_width))
    return jnp.where(allowed, raw, MASKED)


def shards(queries, key_vectors, value_vectors, targets, token_weights, sessions, window_size):
    length, head_count, head_width = queries.shape
    reach_blocks = WIN // length
    factor = 1.0 / math.sqrt(head_width)
    position = lax.axis_index(("ctx", "pair"))
    grad_out = (
        token_weights[:, None, None].astype(jnp.float32) * targets.astype(jnp.float32)
    ).astype(jnp.bfloat16)
    phi_q = feature(queries).astype(jnp.bfloat16)
    phi_k = feature(key_vectors).astype(jnp.bfloat16)
    cache, summary = linear_local(phi_q, phi_k, value_vectors, sessions, BLOCK)
    identity = (jnp.array(-1, jnp.int32), jnp.zeros_like(summary[1]))
    prefix = carried_in((summary[0], summary[1]), ("ctx", "pair"), combine_states, identity, False)
    numerator, forward_state = linear_finish(cache, prefix)
    linear_out, inverse_rms = normalize(numerator)
    key_blocks = [(key_vectors, value_vectors, sessions)]
    for offset in range(1, reach_blocks + 1):
        key_blocks.append(
            passed_along((key_vectors, value_vectors, sessions), ("ctx", "pair"), offset)
        )
    row_peak = jnp.full((head_count, length), MASKED, jnp.float32)
    totals = jnp.zeros((head_count, length), jnp.float32)
    for offset, held_block in enumerate(key_blocks):
        scores = window_scores(queries, held_block, offset, position, sessions, window_size)
        new_peak = jnp.maximum(row_peak, jnp.max(scores, axis=-1))
        totals = totals * jnp.exp(row_peak - new_peak) + jnp.sum(
            jnp.exp(scores - new_peak[..., None]), axis=-1
        )
        row_peak = new_peak
    window_out = jnp.zeros(queries.shape, jnp.float32)
    for offset, held_block in enumerate(key_blocks):
        scores = window_scores(queries, held_block, offset, position, sessions, window_size)
        attn_prob = jnp.exp(scores - row_peak[..., None]) / totals[..., None]
        window_out = window_out + contract(
            "hqk,khd->qhd", attn_prob.astype(jnp.bfloat16), held_block[1]
        )
    attended = (linear_out + window_out).astype(jnp.bfloat16)
    grad_full = grad_out.astype(jnp.float32)
    rowdot = jnp.transpose(jnp.sum(grad_full * window_out, axis=-1))
    grad_q_win = jnp.zeros(queries.shape, jnp.float32)
    grad_k_win = jnp.zeros(queries.shape, jnp.float32)
    grad_v_win = jnp.zeros(queries.shape, jnp.float32)
    for offset, held_block in enumerate(key_blocks):
        scores = window_scores(queries, held_block, offset, position, sessions, window_size)
        attn_prob = jnp.exp(scores - row_peak[..., None]) / totals[..., None]
        rounded = attn_prob.astype(jnp.bfloat16)
        grad_prob = contract("qhd,khd->hqk", grad_out, held_block[1])
        dscore = (attn_prob * (grad_prob - rowdot[..., None])).astype(jnp.bfloat16)
        grad_q_win = grad_q_win + contract("hqk,khd->qhd", dscore, held_block[0]) * factor
        piece_key = (contract("hqk,qhd->khd", dscore, queries) * factor).astype(jnp.bfloat16)
        piece_value = contract("hqk,qhd->khd", rounded, grad_out).astype(jnp.bfloat16)
        if offset == 0:
            kept = lax.optimization_barrier((piece_key, piece_value))
        else:
            kept = passed_along((piece_key, piece_value), ("ctx", "pair"), -offset)
        grad_k_win = grad_k_win + kept[0].astype(jnp.float32)
        grad_v_win = grad_v_win + kept[1].astype(jnp.float32)
    grad_num = inverse_rms * (
        grad_full - linear_out * jnp.mean(grad_full * linear_out, axis=-1, keepdims=True)
    )
    returned, summary_back = linear_back_local(cache, grad_num.astype(jnp.bfloat16))
    suffix = carried_in(
        (summary_back[0], summary_back[1]), ("ctx", "pair"), combine_states, identity, True
    )
    grad_phi_q, grad_phi_k, grad_v_lin = linear_back_finish(cache, forward_state, returned, suffix)
    grad_queries = (feature_slope(queries) * grad_phi_q + grad_q_win).astype(jnp.bfloat16)
    grad_keys = (feature_slope(key_vectors) * grad_phi_k + grad_k_win).astype(jnp.bfloat16)
    grad_values = (grad_v_lin + grad_v_win).astype(jnp.bfloat16)
    return (attended, grad_queries, grad_keys, grad_values)


def solution(mesh):
    return jax.shard_map(
        shards,
        mesh=mesh,
        in_specs=(
            P(("groups", "ctx", "pair"), "head", None),
            P(("groups", "ctx", "pair"), "head", None),
            P(("groups", "ctx", "pair"), "head", None),
            P(("groups", "ctx", "pair"), "head", None),
            P(("groups", "ctx", "pair")),
            P(("groups", "ctx", "pair")),
            P("head"),
        ),
        out_specs=(
            P(("groups", "ctx", "pair"), "head", None),
            P(("groups", "ctx", "pair"), "head", None),
            P(("groups", "ctx", "pair"), "head", None),
            P(("groups", "ctx", "pair"), "head", None),
        ),
        check_vma=False,
    )
```

profile of v0, /device:TPU:9, one launch (start us, length us, event | category | flops | bytes accessed | tf_op | source)
XLA Modules:
  0.0 360.3 jit_solution(13884501624280312621)
XLA Ops:
  7.2 3.3 collective-permute-start.2
  10.6 2.9 collective-permute-start.4
  14.8 3.1 collective-permute-start
  21.9 7.4 %while.66 = (s32[]{:T(128)}, s32[]{:T(128)}, f32[8,128,128]{2,1,0:T(8,128)S(1)}, s32[2]{0:T(128)S(1)}, f32[2,8,128,128]{3,2,1,0:T(8,128)}, /*index=5*/s32[2]{0:T...) while((s32[]{:T(128)}, s32[]{:T(128)}, ...), condition=%wide.region_1.2_spmd.clone, body=%wide.region_0.1_spmd.clone.sunk | while | flops 524296 | bytes 2621659 | solution.py:98
  37.6 40.4 %all-reduce = s32[8]{0:T(128)S(1)} all-reduce(s32[8]{0:T(128)S(1)} %dynamic-update-slice), channel_id=1, replica_groups=mesh['groups'=2,'ctx'=4,'head'=2,'pair'=2] {'ctx','pair'}, use_global_device_ids=true, to_apply=%add | all-reduce | flops 8 | bytes 64
  80.4 5.0 %collective-permute-start.5 = (bf16[256,8,128]{2,0,1:T(8,128)(2,1)}, bf16[256,8,128]{2,0,1:T(8,128)(2,1)S(1)}, u32[]{:S(2)}, u32[]{:S(2)}) collective-permute-start(bf16[256,8,128]{2,0,1:T(8,128)(2,1)} %copy.286), channel_id=1, source_target_pairs={{0,5},{1,8},{4,9},{5,12},{8,13},{2,7},{3,10},{6,11},{7,14},{10,15}... | collective-permute-start | bytes 1572872 | tf_op jit(solution)/shard_map/ppermute | solution.py:42
  97.5 7.8 %collective-permute-start.8 = (bf16[256,8,128]{0,2,1:T(8,128)(2,1)}, bf16[256,8,128]{0,2,1:T(8,128)(2,1)S(1)}, u32[]{:S(2)}, u32[]{:S(2)}) collective-permute-start(bf16[256,8,128]{0,2,1:T(8,128)(2,1)} %copy.308), channel_id=1, source_target_pairs={{0,1},{1,4},{4,5},{5,8},{8,9},{9,12},{12,13},{2,3},{3,6},{6,7},{7,... | collective-permute-start | bytes 1572872 | tf_op jit(solution)/shard_map/ppermute | solution.py:42
  106.1 10.2 %collective-permute-done.3 = bf16[256,8,128]{2,0,1:T(8,128)(2,1)S(1)} collective-permute-done((bf16[256,8,128]{2,0,1:T(8,128)(2,1)}, bf16[256,8,128]{2,0,1:T(8,128)(2,1)S(1)}, u32[]{:S(2)}, u32[]{:S(2)}) %collective-permute-start.3) | collective-permute-done | bytes 524320 | tf_op jit(solution)/shard_map/ppermute | solution.py:42
  116.3 4.2 %collective-permute-start.9 = (bf16[256,8,128]{0,2,1:T(8,128)(2,1)}, bf16[256,8,128]{0,2,1:T(8,128)(2,1)}, u32[]{:S(2)}, u32[]{:S(2)}) collective-permute-start(bf16[256,8,128]{0,2,1:T(8,128)(2,1)} %copy.308), channel_id=1, source_target_pairs={{0,4},{1,5},{4,8},{5,9},{8,12},{9,13},{2,6},{3,7},{6,10},{7,11},{1... | collective-permute-start | bytes 1572872 | tf_op jit(solution)/shard_map/ppermute | solution.py:42
  121.3 15.6 %collective-permute-done.1 = bf16[256,8,128]{2,0,1:T(8,128)(2,1)S(1)} collective-permute-done((bf16[256,8,128]{2,0,1:T(8,128)(2,1)}, bf16[256,8,128]{2,0,1:T(8,128)(2,1)S(1)}, u32[]{:S(2)}, u32[]{:S(2)}) %collective-permute-start.1) | collective-permute-done | bytes 524320 | tf_op jit(solution)/shard_map/ppermute | solution.py:42
  152.0 3.8 %collective-permute-done.10 = bf16[256,8,128]{0,2,1:T(8,128)(2,1)S(1)} collective-permute-done((bf16[256,8,128]{0,2,1:T(8,128)(2,1)}, bf16[256,8,128]{0,2,1:T(8,128)(2,1)S(1)}, u32[]{:S(2)}, u32[]{:S(2)}) %collective-permute-start.10) | collective-permute-done | bytes 524320 | tf_op jit(solution)/shard_map/ppermute | solution.py:42
  158.5 3.0 collective-permute-done.8
  163.9 11.2 %while.64 = (s32[]{:T(128)}, s32[]{:T(128)}, f32[8,128,128]{2,1,0:T(8,128)S(1)}, s32[]{:T(128)}, s32[8]{0:T(128)S(1)}, /*index=5*/bf16[8,8,128,128]{3,2,1,0:T(8,...) while((s32[]{:T(128)}, s32[]{:T(128)}, f32[8,128,128]{2,1,0:T(8,128)S(1)}, ...), condition=%wide.region_3.4_spmd, body=%wide.region_2.3_spmd.sunk | while | flops 393226 | bytes 1310946 | solution.py:36
  183.7 4.6 %fusion.45 = (f32[256,8]{0,1:T(8,128)S(1)}, f32[256,8]{0,1:T(8,128)S(1)}, bf16[256,8,128]{0,2,1:T(8,128)(2,1)}) fusion(f32[256,8,128]{0,2,1:T(8,128)} %copy.296, f32[256,8]{0,1:T(8,128)S(1)} %rsqrt_bitcast_fusion, bf16[256,8,128]{0,2,1:T(8,128)(2,1)S(1)} %copy.317, f32[256]{0:T(256)S(1)} %convert_element_type.213, f32[8,256,128]{1,2,0:T(8,128)} %fusion.99, ...), kind=kOutput, calls=%fused_computation.103 | convolution fusion | flops 139456512 | bytes 7906304 | tf_op jit(solution)/shard_map/hqk,khd->qhd/dot_general | solution.py:46
  205.0 7.4 %while.67 = (s32[]{:T(128)}, s32[]{:T(128)}, f32[8,128,128]{2,1,0:T(8,128)S(1)}, s32[2]{0:T(128)S(1)}, f32[2,8,128,128]{3,2,1,0:T(8,128)}, /*index=5*/s32[2]{0:T...) while((s32[]{:T(128)}, s32[]{:T(128)}, ...), condition=%wide.region_18.19_spmd.clone, body=%wide.region_17.18_spmd.clone.sunk | while | flops 524297 | bytes 2621671 | solution.py:136
  216.3 15.0 %all-reduce.1 = s32[8]{0:T(128)S(1)} all-reduce(s32[8]{0:T(128)S(1)} %dynamic-update-slice.1), channel_id=1, replica_groups=mesh['groups'=2,'ctx'=4,'head'=2,'pair'=2] {'ctx','pair'}, use_global_device_ids=true, to_apply=%add.1 | all-reduce | flops 8 | bytes 64
  249.6 5.6 %collective-permute-start.14 = (bf16[256,8,128]{2,0,1:T(8,128)(2,1)}, bf16[256,8,128]{2,0,1:T(8,128)(2,1)}, u32[]{:S(2)}, u32[]{:S(2)}) collective-permute-start(bf16[256,8,128]{2,0,1:T(8,128)(2,1)} %fusion.29), channel_id=1, source_target_pairs={{5,0},{8,1},{9,4},{12,5},{13,8},{7,2},{10,3},{11,6},{14,7},{15,10}... | collective-permute-start | bytes 1572872 | tf_op jit(solution)/shard_map/ppermute | solution.py:42
  262.8 7.3 %all-gather.7.cloned.1.call-done = bf16[64,128,128]{2,1,0:T(8,128)(2,1)} async-done(((bf16[8,128,128]{2,1,0:T(8,128)(2,1)}), bf16[64,128,128]{2,1,0:T(8,128)(2,1)}) %all-gather.7.cloned.1.call-update) | async-done | bytes 2097168 | tf_op jit(solution)/shard_map/all_gather | solution.py:21
  270.2 15.7 %while.65 = (s32[]{:T(128)}, s32[]{:T(128)}, f32[8,128,128]{2,1,0:T(8,128)S(1)}, s32[]{:T(128)}, s32[8]{0:T(128)S(1)}, /*index=5*/bf16[8,8,128,128]{3,2,1,0:T(8,...) while((s32[]{:T(128)}, s32[]{:T(128)}, ...), condition=%wide.region_20.21_spmd, body=%wide.region_19.20_spmd.sunk | while | flops 393227 | bytes 1310966 | solution.py:36
  289.2 24.0 %collective-permute-start.18 = (bf16[256,8,128]{0,2,1:T(8,128)(2,1)}, bf16[256,8,128]{0,2,1:T(8,128)(2,1)S(1)}, u32[]{:S(2)}, u32[]{:S(2)}) collective-permute-start(bf16[256,8,128]{0,2,1:T(8,128)(2,1)} %fusion.26), channel_id=1, source_target_pairs={{5,0},{8,1},{9,4},{12,5},{13,8},{7,2},{10,3},{11,6},{14,7},{15,10}... | collective-permute-start | bytes 1572872 | tf_op jit(solution)/shard_map/ppermute | solution.py:42
  316.4 3.7 %collective-permute-start.16 = (bf16[256,8,128]{0,2,1:T(8,128)(2,1)}, bf16[256,8,128]{0,2,1:T(8,128)(2,1)}, u32[]{:S(2)}, u32[]{:S(2)}) collective-permute-start(bf16[256,8,128]{0,2,1:T(8,128)(2,1)} %fusion.24), channel_id=1, source_target_pairs={{1,0},{4,1},{5,4},{8,5},{9,8},{12,9},{13,12},{3,2},{6,3},{7,6},{10... | collective-permute-start | bytes 1572872 | tf_op jit(solution)/shard_map/ppermute | solution.py:42
  320.1 8.4 %collective-permute-done.12 = bf16[256,8,128]{2,0,1:T(8,128)(2,1)} collective-permute-done((bf16[256,8,128]{2,0,1:T(8,128)(2,1)}, bf16[256,8,128]{2,0,1:T(8,128)(2,1)}, u32[]{:S(2)}, u32[]{:S(2)}) %collective-permute-start.12) | collective-permute-done | bytes 524320 | tf_op jit(solution)/shard_map/ppermute | solution.py:42
  333.6 6.4 %collective-permute-done.17 = bf16[256,8,128]{0,2,1:T(8,128)(2,1)} collective-permute-done((bf16[256,8,128]{0,2,1:T(8,128)(2,1)}, bf16[256,8,128]{0,2,1:T(8,128)(2,1)}, u32[]{:S(2)}, u32[]{:S(2)}) %collective-permute-start.17) | collective-permute-done | bytes 524320 | tf_op jit(solution)/shard_map/ppermute | solution.py:42
  340.1 10.5 %collective-permute-done.16 = bf16[256,8,128]{0,2,1:T(8,128)(2,1)} collective-permute-done((bf16[256,8,128]{0,2,1:T(8,128)(2,1)}, bf16[256,8,128]{0,2,1:T(8,128)(2,1)}, u32[]{:S(2)}, u32[]{:S(2)}) %collective-permute-start.16) | collective-permute-done | bytes 524320 | tf_op jit(solution)/shard_map/ppermute | solution.py:42
  (268 shorter events, 138.1 us)
Async XLA Ops:
  7.2 156.6 %all-gather.5.cloned.1.call-start = ((), (), s32[]{:S(2)}) async-start(), calls=%async_computation | async-start | bytes 2359296 | tf_op jit(solution)/shard_map/all_gather | solution.py:21
  7.2 73.2 %collective-permute-start.2 = (s32[256]{0:T(256)}, s32[256]{0:T(256)S(1)}, u32[]{:S(2)}, u32[]{:S(2)}) collective-permute-start(s32[256]{0:T(256)} %param.20), channel_id=1, source_target_pairs={{0,4},{1,5},{4,8},{5,9},{8,12},{9,13},{2,6},{3,7},{6,10},{7,11},{1... | collective-permute-start | bytes 3080 | tf_op jit(solution)/shard_map/ppermute | solution.py:42
  10.6 74.8 %collective-permute-start.4 = (s32[256]{0:T(256)}, s32[256]{0:T(256)S(1)}, u32[]{:S(2)}, u32[]{:S(2)}) collective-permute-start(s32[256]{0:T(256)} %param.20), channel_id=1, source_target_pairs={{0,5},{1,8},{4,9},{5,12},{8,13},{2,7},{3,10},{6,11},{7,14},{10,15}... | collective-permute-start | bytes 3080 | tf_op jit(solution)/shard_map/ppermute | solution.py:42
  13.5 73.9 %collective-permute-start.6 = (s32[256]{0:T(256)}, s32[256]{0:T(256)S(1)}, u32[]{:S(2)}, u32[]{:S(2)}) collective-permute-start(s32[256]{0:T(256)} %param.20), channel_id=1, source_target_pairs={{0,8},{1,9},{4,12},{5,13},{2,10},{3,11},{6,14},{7,15},{16,24},{17,... | collective-permute-start | bytes 3080 | tf_op jit(solution)/shard_map/ppermute | solution.py:42
  14.8 74.8 %collective-permute-start = (s32[256]{0:T(256)}, s32[256]{0:T(256)S(1)}, u32[]{:S(2)}, u32[]{:S(2)}) collective-permute-start(s32[256]{0:T(256)} %param.20), channel_id=1, source_target_pairs={{0,1},{1,4},{4,5},{5,8},{8,9},{9,12},{12,13},{2,3},{3,6},{6,7},{7,... | collective-permute-start | bytes 3080 | tf_op jit(solution)/shard_map/ppermute | solution.py:42
  30.0 240.1 %all-gather.7.cloned.1.call-start = ((), (), s32[]{:S(2)}) async-start(), calls=%async_computation.1 | async-start | bytes 2359296 | tf_op jit(solution)/shard_map/all_gather | solution.py:21
  31.0 62.6 %collective-permute-start.7 = (bf16[256,8,128]{2,0,1:T(8,128)(2,1)}, bf16[256,8,128]{2,0,1:T(8,128)(2,1)}, u32[]{:S(2)}, u32[]{:S(2)}) collective-permute-start(bf16[256,8,128]{2,0,1:T(8,128)(2,1)} %copy.286), channel_id=1, source_target_pairs={{0,8},{1,9},{4,12},{5,13},{2,10},{3,11},{6,14},{7,15},{16,24},{17,... | collective-permute-start | bytes 1572872 | tf_op jit(solution)/shard_map/ppermute | solution.py:42
  35.6 56.1 %copy-start.48 = (s32[8]{0:T(128)S(1)}, s32[8]{0:T(128)}, u32[]{:S(2)}) copy-start(s32[8]{0:T(128)} %param.21) | copy-start | bytes 100
  80.4 17.1 %collective-permute-start.5 = (bf16[256,8,128]{2,0,1:T(8,128)(2,1)}, bf16[256,8,128]{2,0,1:T(8,128)(2,1)S(1)}, u32[]{:S(2)}, u32[]{:S(2)}) collective-permute-start(bf16[256,8,128]{2,0,1:T(8,128)(2,1)} %copy.286), channel_id=1, source_target_pairs={{0,5},{1,8},{4,9},{5,12},{8,13},{2,7},{3,10},{6,11},{7,14},{10,15}... | collective-permute-start | bytes 1572872 | tf_op jit(solution)/shard_map/ppermute | solution.py:42
  85.4 30.9 %collective-permute-start.3 = (bf16[256,8,128]{2,0,1:T(8,128)(2,1)}, bf16[256,8,128]{2,0,1:T(8,128)(2,1)S(1)}, u32[]{:S(2)}, u32[]{:S(2)}) collective-permute-start(bf16[256,8,128]{2,0,1:T(8,128)(2,1)} %copy.286), channel_id=1, source_target_pairs={{0,4},{1,5},{4,8},{5,9},{8,12},{9,13},{2,6},{3,7},{6,10},{7,11},{1... | collective-permute-start | bytes 1572872 | tf_op jit(solution)/shard_map/ppermute | solution.py:42
  87.4 49.5 %collective-permute-start.1 = (bf16[256,8,128]{2,0,1:T(8,128)(2,1)}, bf16[256,8,128]{2,0,1:T(8,128)(2,1)S(1)}, u32[]{:S(2)}, u32[]{:S(2)}) collective-permute-start(bf16[256,8,128]{2,0,1:T(8,128)(2,1)} %copy.286), channel_id=1, source_target_pairs={{0,1},{1,4},{4,5},{5,8},{8,9},{9,12},{12,13},{2,3},{3,6},{6,7},{7,... | collective-permute-start | bytes 1572872 | tf_op jit(solution)/shard_map/ppermute | solution.py:42
  89.6 58.5 %collective-permute-start.11 = (bf16[256,8,128]{0,2,1:T(8,128)(2,1)}, bf16[256,8,128]{0,2,1:T(8,128)(2,1)S(1)}, u32[]{:S(2)}, u32[]{:S(2)}) collective-permute-start(bf16[256,8,128]{0,2,1:T(8,128)(2,1)} %copy.308), channel_id=1, source_target_pairs={{0,8},{1,9},{4,12},{5,13},{2,10},{3,11},{6,14},{7,15},{16,24},{17,... | collective-permute-start | bytes 1572872 | tf_op jit(solution)/shard_map/ppermute | solution.py:42
  93.6 45.6 %copy-start.12 = (f32[8,256,256]{1,2,0:T(8,128)}, f32[8,256,256]{1,2,0:T(8,128)S(1)}, u32[]{:S(2)}) copy-start(f32[8,256,256]{1,2,0:T(8,128)S(1)} %get-tuple-element.471) | copy-start | bytes 6291460
  93.6 62.2 %collective-permute-start.10 = (bf16[256,8,128]{0,2,1:T(8,128)(2,1)}, bf16[256,8,128]{0,2,1:T(8,128)(2,1)S(1)}, u32[]{:S(2)}, u32[]{:S(2)}) collective-permute-start(bf16[256,8,128]{0,2,1:T(8,128)(2,1)} %copy.308), channel_id=1, source_target_pairs={{0,5},{1,8},{4,9},{5,12},{8,13},{2,7},{3,10},{6,11},{7,14},{10,15}... | collective-permute-start | bytes 1572872 | tf_op jit(solution)/shard_map/ppermute | solution.py:42
  97.5 63.9 %collective-permute-start.8 = (bf16[256,8,128]{0,2,1:T(8,128)(2,1)}, bf16[256,8,128]{0,2,1:T(8,128)(2,1)S(1)}, u32[]{:S(2)}, u32[]{:S(2)}) collective-permute-start(bf16[256,8,128]{0,2,1:T(8,128)(2,1)} %copy.308), channel_id=1, source_target_pairs={{0,1},{1,4},{4,5},{5,8},{8,9},{9,12},{12,13},{2,3},{3,6},{6,7},{7,... | collective-permute-start | bytes 1572872 | tf_op jit(solution)/shard_map/ppermute | solution.py:42
  116.3 67.4 %collective-permute-start.9 = (bf16[256,8,128]{0,2,1:T(8,128)(2,1)}, bf16[256,8,128]{0,2,1:T(8,128)(2,1)}, u32[]{:S(2)}, u32[]{:S(2)}) collective-permute-start(bf16[256,8,128]{0,2,1:T(8,128)(2,1)} %copy.308), channel_id=1, source_target_pairs={{0,4},{1,5},{4,8},{5,9},{8,12},{9,13},{2,6},{3,7},{6,10},{7,11},{1... | collective-permute-start | bytes 1572872 | tf_op jit(solution)/shard_map/ppermute | solution.py:42
  141.5 192.1 %collective-permute-start.19 = (bf16[256,8,128]{0,2,1:T(8,128)(2,1)}, bf16[256,8,128]{0,2,1:T(8,128)(2,1)}, u32[]{:S(2)}, u32[]{:S(2)}) collective-permute-start(bf16[256,8,128]{0,2,1:T(8,128)(2,1)} %fusion.27), channel_id=1, source_target_pairs={{8,0},{9,1},{12,4},{13,5},{10,2},{11,3},{14,6},{15,7},{24,16},{25,... | collective-permute-start | bytes 1572872 | tf_op jit(solution)/shard_map/ppermute | solution.py:42
  247.1 42.1 %collective-permute-start.15 = (bf16[256,8,128]{2,0,1:T(8,128)(2,1)}, bf16[256,8,128]{2,0,1:T(8,128)(2,1)}, u32[]{:S(2)}, u32[]{:S(2)}) collective-permute-start(bf16[256,8,128]{2,0,1:T(8,128)(2,1)} %fusion.28), channel_id=1, source_target_pairs={{8,0},{9,1},{12,4},{13,5},{10,2},{11,3},{14,6},{15,7},{24,16},{25,... | collective-permute-start | bytes 1572872 | tf_op jit(solution)/shard_map/ppermute | solution.py:42
  249.6 63.5 %collective-permute-start.14 = (bf16[256,8,128]{2,0,1:T(8,128)(2,1)}, bf16[256,8,128]{2,0,1:T(8,128)(2,1)}, u32[]{:S(2)}, u32[]{:S(2)}) collective-permute-start(bf16[256,8,128]{2,0,1:T(8,128)(2,1)} %fusion.29), channel_id=1, source_target_pairs={{5,0},{8,1},{9,4},{12,5},{13,8},{7,2},{10,3},{11,6},{14,7},{15,10}... | collective-permute-start | bytes 1572872 | tf_op jit(solution)/shard_map/ppermute | solution.py:42
  256.5 59.9 %collective-permute-start.13 = (bf16[256,8,128]{2,0,1:T(8,128)(2,1)}, bf16[256,8,128]{2,0,1:T(8,128)(2,1)}, u32[]{:S(2)}, u32[]{:S(2)}) collective-permute-start(bf16[256,8,128]{2,0,1:T(8,128)(2,1)} %fusion.30), channel_id=1, source_target_pairs={{4,0},{5,1},{8,4},{9,5},{12,8},{13,9},{6,2},{7,3},{10,6},{11,7},{1... | collective-permute-start | bytes 1572872 | tf_op jit(solution)/shard_map/ppermute | solution.py:42
  259.7 68.8 %collective-permute-start.12 = (bf16[256,8,128]{2,0,1:T(8,128)(2,1)}, bf16[256,8,128]{2,0,1:T(8,128)(2,1)}, u32[]{:S(2)}, u32[]{:S(2)}) collective-permute-start(bf16[256,8,128]{2,0,1:T(8,128)(2,1)} %fusion.31), channel_id=1, source_target_pairs={{1,0},{4,1},{5,4},{8,5},{9,8},{12,9},{13,12},{3,2},{6,3},{7,6},{10... | collective-permute-start | bytes 1572872 | tf_op jit(solution)/shard_map/ppermute | solution.py:42
  289.2 44.5 %collective-permute-start.18 = (bf16[256,8,128]{0,2,1:T(8,128)(2,1)}, bf16[256,8,128]{0,2,1:T(8,128)(2,1)S(1)}, u32[]{:S(2)}, u32[]{:S(2)}) collective-permute-start(bf16[256,8,128]{0,2,1:T(8,128)(2,1)} %fusion.26), channel_id=1, source_target_pairs={{5,0},{8,1},{9,4},{12,5},{13,8},{7,2},{10,3},{11,6},{14,7},{15,10}... | collective-permute-start | bytes 1572872 | tf_op jit(solution)/shard_map/ppermute | solution.py:42
  313.1 26.9 %collective-permute-start.17 = (bf16[256,8,128]{0,2,1:T(8,128)(2,1)}, bf16[256,8,128]{0,2,1:T(8,128)(2,1)}, u32[]{:S(2)}, u32[]{:S(2)}) collective-permute-start(bf16[256,8,128]{0,2,1:T(8,128)(2,1)} %fusion.25), channel_id=1, source_target_pairs={{4,0},{5,1},{8,4},{9,5},{12,8},{13,9},{6,2},{7,3},{10,6},{11,7},{1... | collective-permute-start | bytes 1572872 | tf_op jit(solution)/shard_map/ppermute | solution.py:42
  316.4 34.2 %collective-permute-start.16 = (bf16[256,8,128]{0,2,1:T(8,128)(2,1)}, bf16[256,8,128]{0,2,1:T(8,128)(2,1)}, u32[]{:S(2)}, u32[]{:S(2)}) collective-permute-start(bf16[256,8,128]{0,2,1:T(8,128)(2,1)} %fusion.24), channel_id=1, source_target_pairs={{1,0},{4,1},{5,4},{8,5},{9,8},{12,9},{13,12},{3,2},{6,3},{7,6},{10... | collective-permute-start | bytes 1572872 | tf_op jit(solution)/shard_map/ppermute | solution.py:42
  (48 other events, 473.3 us)
Sparse Core Ops, SparseCore 0:
  30.2 46.8 all-gather.4
  232.1 37.9 all-gather.6
where the time goes:
time: 362 us; the launch traced here: 360 us
  starting transfers between devices  78.9 us (22%)
  waiting for transfers between devices  69.2 us (19%)
  blocking collectives  55.3 us (15%)
  matrix products  52.8 us (15%)
  local copies, waits for them, and re-layouts  39.5 us (11%)
  other arithmetic  27.2 us (8%)
  loops' own time  22.2 us (6%)
  between operations  15.1 us (4%)
    ppermute x20, starting transfers between devices, passed_along(): return lax.ppermute(x, axis, pairs)  78.8 us
    ppermute x20, waiting for transfers between devices, passed_along(): return lax.ppermute(x, axis, pairs)  61.8 us
    unnamed x2, blocking collectives  55.3 us
    dot_general x42, matrix products, contract(): return jnp.einsum(form, left, right, preferred_element_type=jnp.float32)  52.8 us
    unnamed x112, local copies, waits for them, and re-layouts  16 us
    another operation x2, loops' own time, carried_in(): return lax.fori_loop(0, ahead, one, state)  14.4 us
    add x11, other arithmetic, combine_states(): summed_b + factor * summed_a  8.82 us
    all_gather x2, waiting for transfers between devices, carried_in(): lax.all_gather(a.astype(kind), axis)  7.35 us
  transfers between devices with their start and end apart: 22, of which 11 were waited for; matrix products, arithmetic and copies ran while one was open for 31% of the time, Pallas kernels for 0%

commit v1 on v0

v1 whole, which is shorter than its diff:
```python
import functools
import math

import jax
import jax.numpy as jnp
from jax import lax
from jax.experimental import pallas as pl
from jax.experimental.pallas import tpu as pltpu
from jax.sharding import PartitionSpec as P

WIN = 1024
SESSIONS = 6
EPSILON = 1e-06
MASKED = -1e30
AXES = ("ctx", "pair")
EXTRA = 16
LANES = 128

f32 = jnp.float32
bf16 = jnp.bfloat16


def dot(a, b):
    return lax.dot_general(a, b, (((1,), (0,)), ((), ())), preferred_element_type=f32)


def dot_t(a, b):
    return lax.dot_general(a, b, (((1,), (1,)), ((), ())), preferred_element_type=f32)


def t_dot(a, b):
    return lax.dot_general(a, b, (((0,), (0,)), ((), ())), preferred_element_type=f32)


def feature(x):
    return jnp.where(x > 0, x + 1.0, jnp.exp(jnp.minimum(x, 0.0)))


def slope(x):
    return jnp.where(x > 0, 1.0, jnp.exp(jnp.minimum(x, 0.0)))


def row_of(column):
    n = column.shape[0]
    return jnp.concatenate(
        [
            jnp.transpose(jnp.broadcast_to(column[i : i + LANES], (LANES, LANES)))[0:1]
            for i in range(0, n, LANES)
        ],
        axis=1,
    )


def column_of(rows):
    return jnp.concatenate(
        [
            jnp.transpose(jnp.broadcast_to(rows[i : i + 1], (LANES, LANES)))[:, 0:1]
            for i in range(rows.shape[0])
        ],
        axis=0,
    )


class Plan:
    def __init__(self, length, heads, width, total):
        self.length = length
        self.heads = heads
        self.half = heads // 2
        self.width = width
        self.chip = 2 * length
        longest = total // 3
        reach = min(WIN, longest) - 1
        tail = max(reach - self.chip, 0)
        self.far = longest - 1 > 2 * self.chip or longest - 1 > reach
        self.merged = tail <= length
        self.tail = -(-tail // 16) * 16 if self.merged else length
        self.tail_fill = length if self.merged else self.chip
        self.before = self.tail_fill + self.chip
        self.code_rows = length // LANES
        self.stat_rows = -(-(2 * self.half * self.chip // LANES) // 16) * 16
        self.state_rows = self.half * width
        self.rows = self.half * 2 * length + EXTRA
        self.tail_rows = self.half * 2 * self.tail + EXTRA


def pack_body(p, core_ref, q_ref, k_ref, v_ref, t_ref, w_ref, s_ref, *rest):
    kv_same, kv_cross, qg_same, qg_cross = rest[:4]
    scratch = rest[-1]
    core = core_ref[0]
    L = p.length
    weight = column_of(w_ref[...].astype(f32))
    for n, ref in enumerate((k_ref, v_ref, q_ref, t_ref)):
        x = jnp.swapaxes(ref[...].astype(f32), 0, 1)
        if n == 3:
            x = x * weight[None]
        scratch[n] = x.astype(bf16)
    codes = jnp.concatenate(
        [s_ref[...].astype(f32) + 1.0, jnp.zeros((EXTRA - p.code_rows, LANES), f32)], axis=0
    ).astype(bf16)
    for out, first, which in (
        (kv_same, 0, core),
        (kv_cross, 0, 1 - core),
        (qg_same, 2, core),
        (qg_cross, 2, 1 - core),
    ):
        for h in range(p.half):
            for n in range(2):
                at = (2 * h + n) * L
                out[at : at + L, :] = scratch[first + n, which * p.half + h]
        out[p.rows - EXTRA :, :] = codes
    if p.merged:
        for out, which in ((rest[4], core), (rest[5], 1 - core)):
            for first, wanted, lead in ((0, 1, L - p.tail), (2, 0, 0)):

                @pl.when(core == wanted)
                def _():
                    for h in range(p.half):
                        for n in range(2):
                            at = (2 * h + n) * p.tail
                            out[at : at + p.tail, :] = scratch[
                                first + n, which * p.half + h, lead : lead + p.tail
                            ]

            out[p.tail_rows - EXTRA :, :] = codes


def pack(p, core, q, k, v, targets, weights, sessions):
    big = jax.ShapeDtypeStruct((p.rows, p.width), bf16)
    outs = [big] * 4
    if p.merged:
        outs += [jax.ShapeDtypeStruct((p.tail_rows, p.width), bf16)] * 2
    vmem = pl.BlockSpec(memory_space=pltpu.VMEM)
    return pl.pallas_call(
        functools.partial(pack_body, p),
        out_shape=outs,
        in_specs=[pl.BlockSpec(memory_space=pltpu.SMEM)] + [vmem] * 6,
        out_specs=[vmem] * len(outs),
        scratch_shapes=[pltpu.VMEM((4, p.heads, p.length, p.width), bf16)],
        compiler_params=pltpu.CompilerParams(vmem_limit_bytes=40 << 20),
        name="pack",
    )(core, q, k, v, targets, weights, sessions)


def code_block(p, ref, rows):
    return ref[rows - EXTRA :, :].astype(f32)[: p.code_rows]


def flat(rows):
    return jnp.concatenate([rows[i : i + 1] for i in range(rows.shape[0])], axis=1)


def in_order(core, same, cross):
    first = jnp.where(core == 0, same, cross)
    second = jnp.where(core == 0, cross, same)
    return jnp.concatenate([first, second], axis=0)


def place(p, core, head, same, cross, dst_a, dst_b, start):
    L = p.length
    for ref, which in ((same, core), (cross, 1 - core)):
        to = pl.ds(pl.multiple_of(start + which * L, 16), L)
        for n, dst in ((0, dst_a), (1, dst_b)):
            dst[to, :] = ref[pl.ds(pl.multiple_of((2 * head + n) * L, 16), L), :]


def place_tail(p, flag, head, one, two, dst_a, dst_b, start):
    for n, dst in ((0, dst_a), (1, dst_b)):
        rows = pl.ds(pl.multiple_of((2 * head + n) * p.tail, 16), p.tail)
        dst[start : start + p.tail, :] = jnp.where(flag, one[rows, :], two[rows, :])


def forward_body(p, core_ref, win_ref, *refs):
    kv_own, qg_own, kv_pair, qg_pair, kv_n_same, kv_n_cross, t_a, t_b = refs[:8]
    refs = refs[8:]
    if p.far:
        far_ref, refs = refs[0], refs[1:]
    att_keep, att_send, gn_out, message, ks, vs, qs, gs, atts, dqs, stat, lo_s, code_s = refs
    core = core_ref[0]
    L, C, B, D = p.length, p.chip, p.before, p.width
    scale = 1.0 / math.sqrt(D)
    c2 = scale * math.log2(math.e)

    own_codes = in_order(core, code_block(p, kv_own, p.rows), code_block(p, kv_pair, p.rows))
    near_codes = in_order(
        core, code_block(p, kv_n_same, p.rows), code_block(p, kv_n_cross, p.rows)
    )
    if p.merged:
        far_codes = jnp.where(
            core == 0, code_block(p, t_a, p.tail_rows), code_block(p, t_b, p.tail_rows)
        )
    else:
        far_codes = in_order(core, code_block(p, t_a, p.rows), code_block(p, t_b, p.rows))
    halo_codes = flat(jnp.concatenate([far_codes, near_codes], axis=0))
    own_row = flat(own_codes)
    code = column_of(own_codes)
    last = halo_codes[:, B - 1 : B]
    first_own = own_row[:, 0:1]
    valid = jnp.sum(jnp.where(halo_codes > 0, 1.0, 0.0), axis=1, keepdims=True)
    before_count = jnp.sum(
        jnp.where(jnp.logical_and(halo_codes > 0, halo_codes < code), 1.0, 0.0),
        axis=1,
        keepdims=True,
    ) + jnp.sum(jnp.where(own_row < code, 1.0, 0.0), axis=1, keepdims=True)
    lo_s[...] = (before_count - valid).astype(jnp.int32)
    code_s[...] = code
    cont = jnp.sum(
        jnp.where(jnp.logical_and(halo_codes == last, halo_codes > 0), 1.0, 0.0),
        axis=1,
        keepdims=True,
    ).astype(jnp.int32)
    halo_pos = lax.broadcasted_iota(jnp.int32, (B, 1), 0) - B
    in_start = jnp.broadcast_to(halo_pos >= -cont, (B, D))
    if p.merged and p.tail < p.tail_fill:
        gap = p.tail_fill - p.tail
        ks[0:gap, :] = jnp.zeros((gap, D), bf16)
        vs[0:gap, :] = jnp.zeros((gap, D), bf16)

    @pl.loop(0, p.half)
    def _(h):
        place(p, core, h, kv_own, kv_pair, ks, vs, B)
        place(p, core, h, kv_n_same, kv_n_cross, ks, vs, p.tail_fill)
        place(p, core, h, qg_own, qg_pair, qs, gs, 0)
        if p.merged:
            place_tail(p, core == 0, h, t_a, t_b, ks, vs, p.tail_fill - p.tail)
        else:
            place(p, core, h, t_a, t_b, ks, vs, 0)
        window = win_ref[h]
        if p.far:
            start_state = far_ref[pl.ds(pl.multiple_of(h * D, 16), D), :]
        else:
            halo_phi = jnp.where(in_start, feature(ks[0:B, :].astype(f32)), 0.0).astype(bf16)
            start_state = t_dot(halo_phi, vs[0:B, :]).astype(bf16)
        phi_k = feature(ks[B:, :].astype(f32)).astype(bf16)
        state = jnp.zeros((D, D), f32)
        for r in range(2):
            rows = slice(r * L, (r + 1) * L)
            q = qs[rows, :]
            g = gs[rows, :]
            gf = g.astype(f32)
            lo = lo_s[rows, :]
            mine = code_s[rows, :]
            t_pos = lax.broadcasted_iota(jnp.int32, (L, 1), 0) + r * L
            begin = 0 if not p.merged else r * L
            n_halo = B - begin
            n_own = (r + 1) * L
            wide = n_halo + n_own
            k_part = ks[begin : begin + wide, :]
            v_part = vs[begin : begin + wide, :]
            s_pos = lax.broadcasted_iota(jnp.int32, (L, wide), 1) + (begin - B)
            low = jnp.maximum(lo, t_pos - window + 1)
            allowed = jnp.logical_and(s_pos >= low, s_pos <= t_pos)
            score = jnp.where(allowed, dot_t(q, k_part), MASKED)
            peak = jnp.max(score, axis=1, keepdims=True)
            e = jnp.exp2(score * c2 - peak * c2)
            total = jnp.sum(e, axis=1, keepdims=True)
            inverse = 1.0 / total
            window_out = dot(e.astype(bf16), v_part) * inverse
            rowdot = jnp.sum(gf * window_out, axis=1, keepdims=True)
            ds = (e * (dot_t(g, v_part) - rowdot)).astype(bf16)
            dq = dot(ds, k_part) * (inverse * scale)
            lse = peak * c2 + jnp.log2(total)
            for which, column in ((0, lse), (1, rowdot)):
                base = (which * p.half + h) * (C // LANES) + r * (L // LANES)
                row = row_of(column)
                for j in range(L // LANES):
                    stat[pl.ds(base + j, 1), :] = row[:, j * LANES : (j + 1) * LANES]
            qf = q.astype(f32)
            phi_q = feature(qf).astype(bf16)
            own_pos = lax.broadcasted_iota(jnp.int32, (L, n_own), 1)
            alike = jnp.logical_and(own_pos >= lo, own_pos <= t_pos)
            a = jnp.where(alike, dot_t(phi_q, phi_k[:n_own]), 0.0).astype(bf16)
            reads = mine == last
            numerator = dot(a, vs[B : B + n_own, :]) + jnp.where(
                reads, dot(phi_q, start_state), 0.0
            )
            inverse_rms = lax.rsqrt(
                jnp.mean(numerator * numerator, axis=1, keepdims=True) + EPSILON
            )
            linear_out = numerator * inverse_rms
            grad_num = (
                inverse_rms
                * (gf - linear_out * jnp.mean(gf * linear_out, axis=1, keepdims=True))
            ).astype(bf16)
            b = jnp.where(alike, dot_t(grad_num, vs[B : B + n_own, :]), 0.0).astype(bf16)
            grad_phi_q = dot(b, phi_k[:n_own]) + jnp.where(
                reads, dot_t(grad_num, start_state), 0.0
            )
            atts[h, rows, :] = (linear_out + window_out).astype(bf16)
            dqs[h, rows, :] = (slope(qf) * grad_phi_q + dq).astype(bf16)
            gn_out[h, rows, :] = grad_num
            opening = mine == first_own
            state = state + t_dot(jnp.where(opening, phi_q, jnp.zeros_like(phi_q)), grad_num)
        message[pl.ds(pl.multiple_of(h * D, 16), D), :] = state.astype(bf16)

    values = stat[...]
    if 2 * p.half * C // LANES < p.stat_rows:
        used = lax.broadcasted_iota(jnp.int32, values.shape, 0) < 2 * p.half * C // LANES
        values = jnp.where(used, values, 0.0)
    for n in range(3):
        piece = values.astype(bf16)
        at = p.state_rows + n * p.stat_rows
        message[at : at + p.stat_rows, :] = piece
        values = values - piece.astype(f32)
    for h in range(p.half):
        for n, src in ((0, atts), (1, dqs)):
            att_keep[n, h] = src[h, pl.ds(pl.multiple_of(core * L, 16), L), :]
            att_send[n, h] = src[h, pl.ds(pl.multiple_of((1 - core) * L, 16), L), :]


def forward(p, core, windows, payloads, far_state):
    vmem = pl.BlockSpec(memory_space=pltpu.VMEM)
    smem = pl.BlockSpec(memory_space=pltpu.SMEM)
    half = jax.ShapeDtypeStruct((2, p.half, p.length, p.width), bf16)
    outs = [
        half,
        half,
        jax.ShapeDtypeStruct((p.half, p.chip, p.width), bf16),
        jax.ShapeDtypeStruct((p.state_rows + 3 * p.stat_rows, p.width), bf16),
    ]
    extra = [far_state] if p.far else []
    span = p.before + p.chip
    return pl.pallas_call(
        functools.partial(forward_body, p),
        out_shape=outs,
        in_specs=[smem, smem] + [vmem] * (8 + len(extra)),
        out_specs=[vmem] * 4,
        scratch_shapes=[
            pltpu.VMEM((span, p.width), bf16),
            pltpu.VMEM((span, p.width), bf16),
            pltpu.VMEM((p.chip, p.width), bf16),
            pltpu.VMEM((p.chip, p.width), bf16),
            pltpu.VMEM((p.half, p.chip, p.width), bf16),
            pltpu.VMEM((p.half, p.chip, p.width), bf16),
            pltpu.VMEM((p.stat_rows, p.width), f32),
            pltpu.VMEM((p.chip, 1), jnp.int32),
            pltpu.VMEM((p.chip, 1), f32),
        ],
        compiler_params=pltpu.CompilerParams(vmem_limit_bytes=40 << 20),
        name="forward",
    )(core, windows, *payloads, *extra)


def stats_of(p, ref, head, count):
    result = []
    for which in range(2):
        base = (which * p.half + head) * (p.chip // LANES)
        result.append(flat(ref[pl.ds(base, p.chip // LANES), :])[:, :count])
    return result


def unpack_stats(p, message, dst):
    total = jnp.zeros((p.stat_rows, LANES), f32)
    for n in reversed(range(3)):
        at = p.state_rows + n * p.stat_rows
        total = total + message[at : at + p.stat_rows, :].astype(f32)
    dst[...] = total


def key_side(k, v, q, g, lse, rowdot, allowed, c2, scale):
    score = jnp.where(allowed, dot_t(k, q), MASKED)
    prob = jnp.exp2(score * c2 - lse)
    ds = (prob * (dot_t(v, g) - rowdot)).astype(bf16)
    return dot(ds, q) * scale, dot(prob.astype(bf16), g)


def own_body(p, core_ref, win_ref, kv_own, qg_own, kv_pair, qg_pair, gn, message, dk_o, dv_o, *s):
    ks, vs, qs, gs, stat, hi_s = s
    core = core_ref[0]
    L, C, D = p.length, p.chip, p.width
    scale = 1.0 / math.sqrt(D)
    c2 = scale * math.log2(math.e)
    own_codes = in_order(core, code_block(p, kv_own, p.rows), code_block(p, kv_pair, p.rows))
    own_row = flat(own_codes)
    code = column_of(own_codes)
    hi_s[...] = (
        jnp.sum(jnp.where(own_row <= code, 1.0, 0.0), axis=1, keepdims=True).astype(jnp.int32) - 1
    )
    unpack_stats(p, message, stat)

    @pl.loop(0, p.half)
    def _(h):
        place(p, core, h, kv_own, kv_pair, ks, vs, 0)
        place(p, core, h, qg_own, qg_pair, qs, gs, 0)
        window = win_ref[h]
        lse, rowdot = stats_of(p, stat, h, C)
        phi_q = feature(qs[...].astype(f32)).astype(bf16)
        for r in range(2):
            rows = slice(r * L, (r + 1) * L)
            after = slice(r * L, C)
            wide = C - r * L
            k, v = ks[rows, :], vs[rows, :]
            q, g = qs[after, :], gs[after, :]
            grad_num = gn[h, after, :]
            hi = hi_s[rows, :]
            s_pos = lax.broadcasted_iota(jnp.int32, (L, 1), 0) + r * L
            t_pos = lax.broadcasted_iota(jnp.int32, (L, wide), 1) + r * L
            alike = jnp.logical_and(t_pos >= s_pos, t_pos <= hi)
            allowed = jnp.logical_and(alike, t_pos < s_pos + window)
            dk, dv = key_side(
                k, v, q, g, lse[:, after], rowdot[:, after], allowed, c2, scale
            )
            kf = k.astype(f32)
            a = jnp.where(alike, dot_t(feature(kf).astype(bf16), phi_q[after]), 0.0).astype(bf16)
            b = jnp.where(alike, dot_t(v, grad_num), 0.0).astype(bf16)
            dk_o[h, rows, :] = dk + slope(kf) * dot(b, phi_q[after])
            dv_o[h, rows, :] = dv + dot(a, grad_num)


def own_keys(p, core, windows, kv_own, qg_own, kv_pair, qg_pair, gn, message):
    vmem = pl.BlockSpec(memory_space=pltpu.VMEM)
    smem = pl.BlockSpec(memory_space=pltpu.SMEM)
    full = jax.ShapeDtypeStruct((p.half, p.chip, p.width), f32)
    tile = pltpu.VMEM((p.chip, p.width), bf16)
    return pl.pallas_call(
        functools.partial(own_body, p),
        out_shape=[full, full],
        in_specs=[smem, smem] + [vmem] * 6,
        out_specs=[vmem] * 2,
        scratch_shapes=[tile] * 4
        + [pltpu.VMEM((p.stat_rows, p.width), f32), pltpu.VMEM((p.chip, 1), jnp.int32)],
        compiler_params=pltpu.CompilerParams(vmem_limit_bytes=40 << 20),
        name="own_keys",
    )(core, windows, kv_own, qg_own, kv_pair, qg_pair, gn, message)


def later_body(p, core_ref, win_ref, *refs):
    kv_own, kv_pair, qg_n_same, qg_n_cross, t_a, t_b, message_1, message_2, dk_i, dv_i = refs[:10]
    refs = refs[10:]
    if p.far:
        far_ref, refs = refs[0], refs[1:]
    keep, send, ks, vs, qs, gs, stat_1, stat_2, hi_s, code_s, dks, dvs = refs
    core = core_ref[0]
    L, C, D = p.length, p.chip, p.width
    N = p.tail_fill
    scale = 1.0 / math.sqrt(D)
    c2 = scale * math.log2(math.e)
    own_codes = in_order(core, code_block(p, kv_own, p.rows), code_block(p, kv_pair, p.rows))
    near_codes = in_order(
        core, code_block(p, qg_n_same, p.rows), code_block(p, qg_n_cross, p.rows)
    )
    if p.merged:
        far_codes = jnp.where(
            core == 1, code_block(p, t_a, p.tail_rows), code_block(p, t_b, p.tail_rows)
        )
    else:
        far_codes = in_order(core, code_block(p, t_a, p.rows), code_block(p, t_b, p.rows))
    after_row = flat(jnp.concatenate([near_codes, far_codes], axis=0))
    own_row = flat(own_codes)
    code = column_of(own_codes)
    code_s[...] = code
    hi_s[...] = (
        C
        - 1
        + jnp.sum(
            jnp.where(jnp.logical_and(after_row > 0, after_row <= code), 1.0, 0.0),
            axis=1,
            keepdims=True,
        )
        - jnp.sum(jnp.where(own_row > code, 1.0, 0.0), axis=1, keepdims=True) * (2.0 * (C + N))
    ).astype(jnp.int32)
    first_next = after_row[:, 0:1]
    goes_on = jnp.logical_and(first_next > 0, first_next == after_row[:, C : C + 1])
    unpack_stats(p, message_1, stat_1)
    unpack_stats(p, message_2, stat_2)
    if p.merged and p.tail < p.tail_fill:
        gap = p.tail_fill - p.tail
        qs[C + p.tail :, :] = jnp.zeros((gap, D), bf16)
        gs[C + p.tail :, :] = jnp.zeros((gap, D), bf16)

    @pl.loop(0, p.half)
    def _(h):
        place(p, core, h, kv_own, kv_pair, ks, vs, 0)
        place(p, core, h, qg_n_same, qg_n_cross, qs, gs, 0)
        if p.merged:
            place_tail(p, core == 1, h, t_a, t_b, qs, gs, C)
        else:
            place(p, core, h, t_a, t_b, qs, gs, C)
        window = win_ref[h]
        near_stats = stats_of(p, stat_1, h, C)
        far_stats = stats_of(p, stat_2, h, N)
        lse, rowdot = (
            jnp.concatenate([x, y], axis=1) for x, y in zip(near_stats, far_stats)
        )
        here = pl.ds(pl.multiple_of(h * D, 16), D)
        if p.far:
            later_state = far_ref[here, :]
        else:
            later_state = (
                message_1[here, :].astype(f32)
                + jnp.where(goes_on, message_2[here, :].astype(f32), 0.0)
            ).astype(bf16)
        for r in range(2):
            rows = slice(r * L, (r + 1) * L)
            wide = C + N if (r == 1 or not p.merged) else C
            k, v = ks[rows, :], vs[rows, :]
            q, g = qs[0:wide, :], gs[0:wide, :]
            s_pos = lax.broadcasted_iota(jnp.int32, (L, 1), 0) + r * L
            t_pos = lax.broadcasted_iota(jnp.int32, (L, wide), 1) + C
            allowed = t_pos <= jnp.minimum(hi_s[rows, :], s_pos + window - 1)
            dk, dv = key_side(k, v, q, g, lse[:, :wide], rowdot[:, :wide], allowed, c2, scale)
            kf = k.astype(f32)
            uses = code_s[rows, :] == first_next
            phi_k = feature(kf).astype(bf16)
            grad_phi_k = jnp.where(uses, dot_t(v, later_state), 0.0)
            dks[h, rows, :] = (dk_i[h, rows, :] + dk + slope(kf) * grad_phi_k).astype(bf16)
            dvs[h, rows, :] = (
                dv_i[h, rows, :] + dv + jnp.where(uses, dot(phi_k, later_state), 0.0)
            ).astype(bf16)

    for h in range(p.half):
        for n, src in ((0, dks), (1, dvs)):
            keep[n, h] = src[h, pl.ds(pl.multiple_of(core * L, 16), L), :]
            send[n, h] = src[h, pl.ds(pl.multiple_of((1 - core) * L, 16), L), :]


def later_keys(p, core, windows, payloads, far_state):
    vmem = pl.BlockSpec(memory_space=pltpu.VMEM)
    smem = pl.BlockSpec(memory_space=pltpu.SMEM)
    half = jax.ShapeDtypeStruct((2, p.half, p.length, p.width), bf16)
    extra = [far_state] if p.far else []
    tile = pltpu.VMEM((p.chip, p.width), bf16)
    tall = pltpu.VMEM((p.chip + p.tail_fill, p.width), bf16)
    stat = pltpu.VMEM((p.stat_rows, p.width), f32)
    return pl.pallas_call(
        functools.partial(later_body, p),
        out_shape=[half, half],
        in_specs=[smem, smem] + [vmem] * (10 + len(extra)),
        out_specs=[vmem] * 2,
        scratch_shapes=[
            tile,
            tile,
            tall,
            tall,
            stat,
            stat,
            pltpu.VMEM((p.chip, 1), jnp.int32),
            pltpu.VMEM((p.chip, 1), f32),
            pltpu.VMEM((p.half, p.chip, p.width), bf16),
            pltpu.VMEM((p.half, p.chip, p.width), bf16),
        ],
        compiler_params=pltpu.CompilerParams(vmem_limit_bytes=40 << 20),
        name="later_keys",
    )(core, windows, *payloads, *extra)


def unpack_body(p, core_ref, keep, other, out_a, out_b, scratch):
    core = core_ref[0]
    for n, out in ((0, out_a), (1, out_b)):
        for h in range(p.half):
            scratch[core * p.half + h] = keep[n, h].astype(f32)
            scratch[(1 - core) * p.half + h] = other[n, h].astype(f32)
        out[...] = jnp.swapaxes(scratch[...], 0, 1).astype(bf16)


def unpack(p, core, keep, other):
    vmem = pl.BlockSpec(memory_space=pltpu.VMEM)
    out = jax.ShapeDtypeStruct((p.length, p.heads, p.width), bf16)
    return pl.pallas_call(
        functools.partial(unpack_body, p),
        out_shape=[out, out],
        in_specs=[pl.BlockSpec(memory_space=pltpu.SMEM), vmem, vmem],
        out_specs=[vmem, vmem],
        scratch_shapes=[pltpu.VMEM((p.heads, p.length, p.width), f32)],
        compiler_params=pltpu.CompilerParams(vmem_limit_bytes=40 << 20),
        name="unpack",
    )(core, keep, other)


def folded(session, state, backward):
    sessions = lax.all_gather(session, "ctx")
    states = lax.all_gather(state, "ctx")
    count = lax.axis_size("ctx")
    here = lax.axis_index("ctx")

    def one(hop, carry):
        held, total = carry
        source = count - 1 - hop if backward else hop
        new = lax.dynamic_index_in_dim(sessions, source, 0, False)
        first, last = new[0], new[1]
        part = lax.dynamic_index_in_dim(states, source, 0, False).astype(f32)
        entering, leaving = (last, first) if backward else (first, last)
        whole = jnp.logical_and(entering == held, entering == leaving)
        return leaving, part + jnp.where(whole, total, 0.0)

    steps = count - 1 - here if backward else here
    start = (jnp.zeros((), jnp.int32) - 1, jnp.zeros(state.shape, f32))
    return lax.fori_loop(0, steps, one, start)[1].astype(bf16)


def shards(p, queries, key_vectors, value_vectors, targets, token_weights, sessions, window_size):
    L = p.length
    chips = lax.axis_size("ctx")
    core_id = lax.axis_index("pair").astype(jnp.int32)
    core = core_id.reshape(1)
    windows = lax.dynamic_slice_in_dim(window_size, core_id * p.half, p.half)

    def move(x, target):
        pairs = []
        for c in range(chips):
            for i in range(2):
                to, j = target(c, i)
                if 0 <= to < chips:
                    pairs.append((2 * c + i, 2 * to + j))
        return lax.ppermute(x, AXES, pairs)

    packed = pack(
        p,
        core,
        queries,
        key_vectors,
        value_vectors,
        targets,
        token_weights.reshape(-1, LANES),
        sessions.reshape(-1, LANES),
    )
    kv_same, kv_cross, qg_same, qg_cross = packed[:4]
    kv_pair = move(kv_cross, lambda c, i: (c, 1 - i))
    qg_pair = move(qg_cross, lambda c, i: (c, 1 - i))
    kv_n_same = move(kv_same, lambda c, i: (c + 1, i))
    qg_n_same = move(qg_same, lambda c, i: (c - 1, i))
    kv_n_cross = move(kv_cross, lambda c, i: (c + 1, 1 - i))
    qg_n_cross = move(qg_cross, lambda c, i: (c - 1, 1 - i))
    if p.merged:
        tail_same, tail_cross = packed[4:]
        got_cross = move(tail_cross, lambda c, i: (c + 2, 0) if i == 1 else (c - 2, 1))
        got_same = move(tail_same, lambda c, i: (c + 2, 1) if i == 1 else (c - 2, 0))
        kv_t = qg_t = None
        kv_t = (got_cross, got_same)
        qg_t = (got_cross, got_same)
    else:
        kv_t = (
            move(kv_same, lambda c, i: (c + 2, i)),
            move(kv_cross, lambda c, i: (c + 2, 1 - i)),
        )
        qg_t = (
            move(qg_same, lambda c, i: (c - 2, i)),
            move(qg_cross, lambda c, i: (c - 2, 1 - i)),
        )

    far_before = far_after = None
    if p.far:
        ends = jnp.stack([sessions[0], sessions[-1]])
        both = lax.all_gather(ends, "pair")
        chip_ends = jnp.stack([both[0, 0], both[1, 1]])
        own = kv_same[: p.rows - EXTRA].reshape(p.half, 2, L, p.width)
        pair = kv_pair[: p.rows - EXTRA].reshape(p.half, 2, L, p.width)
        all_sessions = lax.all_gather(sessions, "pair")
        keys_of = []
        total = jnp.zeros((p.half, p.width, p.width), f32)
        for part, owner in ((own, core_id), (pair, 1 - core_id)):
            rows = lax.dynamic_index_in_dim(all_sessions, owner, 0, False)
            phi = feature(part[:, 0].astype(f32))
            phi = jnp.where((rows == chip_ends[1])[None, :, None], phi, 0.0).astype(bf16)
            total = total + jnp.einsum(
                "hsk,hsd->hkd", phi, part[:, 1], preferred_element_type=f32
            )
        far_before = folded(chip_ends, total.astype(bf16), False).reshape(-1, p.width)

    keep, send, grad_num, message = forward(
        p,
        core,
        windows,
        (kv_same, qg_same, kv_pair, qg_pair, kv_n_same, kv_n_cross) + kv_t,
        far_before,
    )
    message_1 = move(message, lambda c, i: (c - 1, i))
    message_2 = move(message, lambda c, i: (c - 2, i))
    other = move(send, lambda c, i: (c, 1 - i))
    if p.far:
        state = message[: p.state_rows].reshape(p.half, p.width, p.width)
        far_after = folded(chip_ends, state, True).reshape(-1, p.width)
    dk, dv = own_keys(p, core, windows, kv_same, qg_same, kv_pair, qg_pair, grad_num, message)
    attended, grad_queries = unpack(p, core, keep, other)
    keep, send = later_keys(
        p,
        core,
        windows,
        (kv_same, kv_pair, qg_n_same, qg_n_cross) + qg_t + (message_1, message_2, dk, dv),
        far_after,
    )
    other = move(send, lambda c, i: (c, 1 - i))
    grad_keys, grad_values = unpack(p, core, keep, other)
    return (attended, grad_queries, grad_keys, grad_values)


def solution(mesh):
    rows = P(("groups", "ctx", "pair"), "head", None)
    events = P(("groups", "ctx", "pair"))

    def run(queries, key_vectors, value_vectors, targets, token_weights, sessions, window_size):
        total = queries.shape[0] // mesh.shape["groups"]
        length = total // (mesh.shape["ctx"] * mesh.shape["pair"])
        heads = queries.shape[1] // mesh.shape["head"]
        p = Plan(length, heads, queries.shape[2], total)
        return jax.shard_map(
            functools.partial(shards, p),
            mesh=mesh,
            in_specs=(rows, rows, rows, rows, events, events, P("head")),
            out_specs=(rows, rows, rows, rows),
            check_vma=False,
        )(queries, key_vectors, value_vectors, targets, token_weights, sessions, window_size)

    return run
```

time: 362 us -> 89.9 us (0.25)
  starting transfers between devices: 78.9 us -> 18.9 us
  blocking collectives: 55.3 us -> 0 us
  matrix products: 52.8 us -> 0 us
  waiting for transfers between devices: 69.2 us -> 29.3 us
  Pallas kernels: 0 us -> 34.5 us
  local copies, waits for them, and re-layouts: 39.5 us -> 5.57 us
  other arithmetic: 27.2 us -> 0 us
  loops' own time: 22.2 us -> 0 us
  between operations: 15.1 us -> 0.81 us
    ppermute x20 -> x12, starting transfers between devices: 78.8 us -> 18.9 us  [move(): return lax.ppermute(x, AXES, pairs)]
    unnamed x2 -> x0, blocking collectives: 55.3 us -> none
    dot_general x42 -> x0, matrix products: 52.8 us -> none  [contract(): return jnp.einsum(form, left, right, preferred_element_type=jnp.float32)]
    pallas_call x0 -> x6, Pallas kernels: none -> 34.5 us  [the longest x1 16.1 us: forward(): pl.pallas_call(functools.partial(forward_body, p), out_shape=outs, in_spe...]
    ppermute x20 -> x12, waiting for transfers between devices: 61.8 us -> 29.3 us  [move(): return lax.ppermute(x, AXES, pairs)]
    another operation x4 -> x0, loops' own time: 22.2 us -> none  [the longest x2 14.4 us: carried_in(): return lax.fori_loop(0, ahead, one, state)]
    convert_element_type x11 -> x0, other arithmetic: 11.2 us -> none  [the longest x1 2.45 us: shards(): (feature_slope(key_vectors) * grad_phi_k + grad_k_win).astype(jnp.bfloat16)]
    unnamed x112 -> x14, local copies, waits for them, and re-layouts: 16 us -> 5.49 us
  transfers between devices with their start and end apart: 22 -> 12, of which waited for: 11 -> 6; matrix products, arithmetic and copies ran while one was open for 31% -> 0% of each run, Pallas kernels for 0% -> 34%
where the time goes in v1:
time: 89.9 us; the launch traced here: 89.1 us
  Pallas kernels  34.5 us (38%)
  waiting for transfers between devices  29.3 us (33%)
  starting transfers between devices  18.9 us (21%)
  local copies, waits for them, and re-layouts  5.57 us (6%)
    ppermute x12, waiting for transfers between devices, move(): return lax.ppermute(x, AXES, pairs)  29.3 us
    ppermute x12, starting transfers between devices, move(): return lax.ppermute(x, AXES, pairs)  18.9 us
    pallas_call x1, Pallas kernels, forward(): pl.pallas_call(functools.partial(forward_body, p), out_shape=outs, in_spe...  16.1 us
    pallas_call x1, Pallas kernels, own_keys(): pl.pallas_call(functools.partial(own_body, p), out_shape=[full, full], in...  7.02 us
    pallas_call x1, Pallas kernels, later_keys(): pl.pallas_call(functools.partial(later_body, p), out_shape=[half, half],...  6.16 us
    unnamed x14, local copies, waits for them, and re-layouts  5.49 us
    pallas_call x2, Pallas kernels, unpack(): pl.pallas_call(functools.partial(unpack_body, p), out_shape=[out, out], i...  2.69 us
    pallas_call x1, Pallas kernels, pack(): pl.pallas_call(functools.partial(pack_body, p), out_shape=outs, in_specs=...  2.55 us
  transfers between devices with their start and end apart: 12, of which 6 were waited for; matrix products, arithmetic and copies ran while one was open for 0% of the time, Pallas kernels for 34%

profile of v1, /device:TPU:9, one launch (start us, length us, event | category | flops | bytes accessed | tf_op | source)
XLA Modules:
  0.0 89.1 jit_solution(14271820752134929480)
XLA Ops:
  1.3 1.0 %copy-done = bf16[256,8,128]{2,1,0:T(8,128)(2,1)S(1)} copy-done((bf16[256,8,128]{2,1,0:T(8,128)(2,1)S(1)}, bf16[256,8,128]{2,1,0:T(8,128)(2,1)}, u32[]{:S(2)}) %copy-start) | copy-done | bytes 524312
  2.4 1.0 %copy-done.1 = bf16[256,8,128]{2,1,0:T(8,128)(2,1)S(1)} copy-done((bf16[256,8,128]{2,1,0:T(8,128)(2,1)S(1)}, bf16[256,8,128]{2,1,0:T(8,128)(2,1)}, u32[]{:S(2)}) %copy-start.1) | copy-done | bytes 524312
  3.4 1.0 %copy-done.2 = bf16[256,8,128]{2,1,0:T(8,128)(2,1)S(1)} copy-done((bf16[256,8,128]{2,1,0:T(8,128)(2,1)S(1)}, bf16[256,8,128]{2,1,0:T(8,128)(2,1)}, u32[]{:S(2)}) %copy-start.2) | copy-done | bytes 524312
  4.5 1.0 %copy-done.3 = bf16[256,8,128]{2,1,0:T(8,128)(2,1)S(1)} copy-done((bf16[256,8,128]{2,1,0:T(8,128)(2,1)S(1)}, bf16[256,8,128]{2,1,0:T(8,128)(2,1)}, u32[]{:S(2)}) %copy-start.3) | copy-done | bytes 524312
  5.5 2.5 %pack.1 = (bf16[2064,128]{1,0:T(8,128)(2,1)S(1)}, bf16[2064,128]{1,0:T(8,128)(2,1)}, bf16[2064,128]{1,0:T(8,128)(2,1)S(1)}, bf16[2064,128]{1,0:T(8,128)(2,1)}, b...) custom-call(s32[1]{0:T(128)} %bitcast.core_ref, bf16[256,8,128]{2,1,0:T(8,128)(2,1)S(1)} %copy-done, ...), custom_call_target="tpu_custom_call" | custom-call | tf_op jit(solution)/shard_map/pack/pallas_call | solution.py:133
  8.1 0.7 collective-permute-start
  8.7 4.1 %collective-permute-start.4 = (bf16[1424,128]{1,0:T(8,128)(2,1)S(1)}, bf16[1424,128]{1,0:T(8,128)(2,1)S(1)}, u32[]{:S(2)}, u32[]{:S(2)}) collective-permute-start(bf16[1424,128]{1,0:T(8,128)(2,1)S(1)} %get-tuple-element.26), channel_id=1, source_target_pairs={{1,8},{5,12},{8,1},{12,5},{3,10},{7,14},{10,3},{14,7},{17,24},{21,... | collective-permute-start | bytes 1093640 | tf_op jit(solution)/shard_map/ppermute | solution.py:604
  12.8 1.3 %collective-permute-start.5 = (bf16[1424,128]{1,0:T(8,128)(2,1)S(1)}, bf16[1424,128]{1,0:T(8,128)(2,1)S(1)}, u32[]{:S(2)}, u32[]{:S(2)}) collective-permute-start(bf16[1424,128]{1,0:T(8,128)(2,1)S(1)} %get-tuple-element.27), channel_id=1, source_target_pairs={{1,9},{5,13},{8,0},{12,4},{3,11},{7,15},{10,2},{14,6},{17,25},{21,... | collective-permute-start | bytes 1093640 | tf_op jit(solution)/shard_map/ppermute | solution.py:604
  14.1 1.9 %collective-permute-start.2 = (bf16[2064,128]{1,0:T(8,128)(2,1)S(1)}, bf16[2064,128]{1,0:T(8,128)(2,1)}, u32[]{:S(2)}, u32[]{:S(2)}) collective-permute-start(bf16[2064,128]{1,0:T(8,128)(2,1)S(1)} %get-tuple-element.22.refs_0_.kv_own), channel_id=1, source_target_pairs={{0,4},{1,5},{4,8},{5,9},{8,12},{9,13},{2,6},{3,7},{6,10},{7,11},{1... | collective-permute-start | bytes 1585160 | tf_op jit(solution)/shard_map/ppermute | solution.py:604
  16.2 11.9 %collective-permute-done.4.refs_6_.refs_4_ = bf16[1424,128]{1,0:T(8,128)(2,1)S(1)} collective-permute-done((bf16[1424,128]{1,0:T(8,128)(2,1)S(1)}, bf16[1424,128]{1,0:T(8,128)(2,1)S(1)}, u32[]{:S(2)}, u32[]{:S(2)}) %collective-permute-start.4) | collective-permute-done | bytes 364576 | tf_op jit(solution)/shard_map/ppermute | solution.py:604
  28.1 1.9 %collective-permute-start.3 = (bf16[2064,128]{1,0:T(8,128)(2,1)}, bf16[2064,128]{1,0:T(8,128)(2,1)}, u32[]{:S(2)}, u32[]{:S(2)}) collective-permute-start(bf16[2064,128]{1,0:T(8,128)(2,1)} %get-tuple-element.24), channel_id=1, source_target_pairs={{0,5},{1,4},{4,9},{5,8},{8,13},{9,12},{2,7},{3,6},{6,11},{7,10},{1... | collective-permute-start | bytes 1585160 | tf_op jit(solution)/shard_map/ppermute | solution.py:604
  30.0 5.9 %collective-permute-done.5.refs_7_.refs_5_ = bf16[1424,128]{1,0:T(8,128)(2,1)S(1)} collective-permute-done((bf16[1424,128]{1,0:T(8,128)(2,1)S(1)}, bf16[1424,128]{1,0:T(8,128)(2,1)S(1)}, u32[]{:S(2)}, u32[]{:S(2)}) %collective-permute-start.5) | collective-permute-done | bytes 364576 | tf_op jit(solution)/shard_map/ppermute | solution.py:604
  35.9 1.9 %collective-permute-start.7 = (bf16[2064,128]{1,0:T(8,128)(2,1)S(1)}, bf16[2064,128]{1,0:T(8,128)(2,1)S(1)}, u32[]{:S(2)}, u32[]{:S(2)}) collective-permute-start(bf16[2064,128]{1,0:T(8,128)(2,1)S(1)} %get-tuple-element.23.refs_1_.qg_own), channel_id=1, source_target_pairs={{4,0},{5,1},{8,4},{9,5},{12,8},{13,9},{6,2},{7,3},{10,6},{11,7},{1... | collective-permute-start | bytes 1585160 | tf_op jit(solution)/shard_map/ppermute | solution.py:604
  37.8 1.9 %collective-permute-start.8 = (bf16[2064,128]{1,0:T(8,128)(2,1)}, bf16[2064,128]{1,0:T(8,128)(2,1)}, u32[]{:S(2)}, u32[]{:S(2)}) collective-permute-start(bf16[2064,128]{1,0:T(8,128)(2,1)} %get-tuple-element.25), channel_id=1, source_target_pairs={{4,1},{5,0},{8,5},{9,4},{12,9},{13,8},{6,3},{7,2},{10,7},{11,6},{1... | collective-permute-start | bytes 1585160 | tf_op jit(solution)/shard_map/ppermute | solution.py:604
  40.5 5.3 %collective-permute-done.2.refs_4_ = bf16[2064,128]{1,0:T(8,128)(2,1)} collective-permute-done((bf16[2064,128]{1,0:T(8,128)(2,1)S(1)}, bf16[2064,128]{1,0:T(8,128)(2,1)}, u32[]{:S(2)}, u32[]{:S(2)}) %collective-permute-start.2) | collective-permute-done | bytes 528416 | tf_op jit(solution)/shard_map/ppermute | solution.py:604
  45.8 5.8 %collective-permute-done.3.refs_5_ = bf16[2064,128]{1,0:T(8,128)(2,1)} collective-permute-done((bf16[2064,128]{1,0:T(8,128)(2,1)}, bf16[2064,128]{1,0:T(8,128)(2,1)}, u32[]{:S(2)}, u32[]{:S(2)}) %collective-permute-start.3) | collective-permute-done | bytes 528416 | tf_op jit(solution)/shard_map/ppermute | solution.py:604
  51.6 16.1 %forward.1 = (bf16[2,4,256,128]{3,2,1,0:T(8,128)(2,1)S(1)}, bf16[2,4,256,128]{3,2,1,0:T(8,128)(2,1)S(1)}, bf16[4,512,128]{2,1,0:T(8,128)(2,1)S(1)}, bf16[608,128]{1,0:T(8,128)(2,1)S(1)}) custom-call(s32[1]{0:T(128)} %bitcast.core_ref, s32[4]{0:T(128)S(1)} %dynamic_slice.3.win_ref, bf16[2064,128]{1,0:T(8,128)(2,1)S(1)} %get-tuple-element.22.refs_0_.kv_own, ...), custom_call_target="tpu_custom_call" | custom-call | tf_op jit(solution)/shard_map/forward/pallas_call | solution.py:322
  67.7 1.3 %collective-permute-start.10 = (bf16[608,128]{1,0:T(8,128)(2,1)S(1)}, bf16[608,128]{1,0:T(8,128)(2,1)S(1)}, u32[]{:S(2)}, u32[]{:S(2)}) collective-permute-start(bf16[608,128]{1,0:T(8,128)(2,1)S(1)} %get-tuple-element.32.message), channel_id=1, source_target_pairs={{8,0},{9,1},{12,4},{13,5},{10,2},{11,3},{14,6},{15,7},{24,16},{25,... | collective-permute-start | bytes 466952 | tf_op jit(solution)/shard_map/ppermute | solution.py:604
  69.0 1.9 %collective-permute-start.9 = (bf16[608,128]{1,0:T(8,128)(2,1)S(1)}, bf16[608,128]{1,0:T(8,128)(2,1)S(1)}, u32[]{:S(2)}, u32[]{:S(2)}) collective-permute-start(bf16[608,128]{1,0:T(8,128)(2,1)S(1)} %get-tuple-element.32.message), channel_id=1, source_target_pairs={{4,0},{5,1},{8,4},{9,5},{12,8},{13,9},{6,2},{7,3},{10,6},{11,7},{1... | collective-permute-start | bytes 466952 | tf_op jit(solution)/shard_map/ppermute | solution.py:604
  71.0 7.0 %own_keys.1 = (f32[4,512,128]{2,1,0:T(8,128)S(1)}, f32[4,512,128]{2,1,0:T(8,128)S(1)}) custom-call(s32[1]{0:T(128)} %bitcast.core_ref, s32[4]{0:T(128)S(1)} %dynamic_slice.3.win_ref, bf16[2064,128]{1,0:T(8,128)(2,1)S(1)} %get-tuple-element.22.refs_0_.kv_own, bf16[2064,128]{1,0:T(8,128)(2,1)S(1)} %get-tuple-element.23.refs_1_.qg_own, ...), custom_call_target="tpu_custom_call" | custom-call | tf_op jit(solution)/shard_map/own_keys/pallas_call | solution.py:414
  78.3 6.2 %later_keys.1 = (bf16[2,4,256,128]{3,2,1,0:T(8,128)(2,1)S(1)}, bf16[2,4,256,128]{3,2,1,0:T(8,128)(2,1)S(1)}) custom-call(s32[1]{0:T(128)} %bitcast.core_ref, s32[4]{0:T(128)S(1)} %dynamic_slice.3.win_ref, bf16[2064,128]{1,0:T(8,128)(2,1)S(1)} %get-tuple-element.22.refs_0_.kv_own, bf16[2064,128]{1,0:T(8,128)(2,1)S(1)} %collective-permute-done.refs_2_.kv_pair.refs_1_, ...), custom_call_target="tpu_custom_call" | custom-call | tf_op jit(solution)/shard_map/later_keys/pallas_call | solution.py:524
  84.4 1.8 %collective-permute-start.11 = (bf16[2,4,256,128]{3,2,1,0:T(8,128)(2,1)S(1)}, bf16[2,4,256,128]{3,2,1,0:T(8,128)(2,1)S(1)}, u32[]{:S(2)}, u32[]{:S(2)}) collective-permute-start(bf16[2,4,256,128]{3,2,1,0:T(8,128)(2,1)S(1)} %get-tuple-element.37), channel_id=1, source_target_pairs={{0,1},{1,0},{4,5},{5,4},{8,9},{9,8},{12,13},{13,12},{2,3},{3,2},{6... | collective-permute-start | bytes 1572872 | tf_op jit(solution)/shard_map/ppermute | solution.py:604
  86.2 1.3 %unpack.2 = (bf16[256,8,128]{2,1,0:T(8,128)(2,1)}, bf16[256,8,128]{2,1,0:T(8,128)(2,1)}) custom-call(s32[1]{0:T(128)} %bitcast.core_ref, bf16[2,4,256,128]{3,2,1,0:T(8,128)(2,1)S(1)} %get-tuple-element.28.keep, bf16[2,4,256,128]{3,2,1,0:T(8,128)(2,1)S(1)} %collective-permute-done.6.other), custom_call_target="tpu_custom_call" | custom-call | tf_op jit(solution)/shard_map/unpack/pallas_call | solution.py:558
  87.8 1.3 %unpack.3 = (bf16[256,8,128]{2,1,0:T(8,128)(2,1)}, bf16[256,8,128]{2,1,0:T(8,128)(2,1)}) custom-call(s32[1]{0:T(128)} %bitcast.core_ref, bf16[2,4,256,128]{3,2,1,0:T(8,128)(2,1)S(1)} %get-tuple-element.36.keep, bf16[2,4,256,128]{3,2,1,0:T(8,128)(2,1)S(1)} %collective-permute-done.11.other), custom_call_target="tpu_custom_call" | custom-call | tf_op jit(solution)/shard_map/unpack/pallas_call | solution.py:558
  (21 shorter events, 2.0 us)
Async XLA Ops:
  0.6 0.7 copy-start.5
  0.6 0.7 copy-start.4
  1.3 1.0 %copy-start = (bf16[256,8,128]{2,1,0:T(8,128)(2,1)S(1)}, bf16[256,8,128]{2,1,0:T(8,128)(2,1)}, u32[]{:S(2)}) copy-start(bf16[256,8,128]{2,1,0:T(8,128)(2,1)} %q_ref.1) | copy-start | bytes 1572868
  2.4 1.0 %copy-start.1 = (bf16[256,8,128]{2,1,0:T(8,128)(2,1)S(1)}, bf16[256,8,128]{2,1,0:T(8,128)(2,1)}, u32[]{:S(2)}) copy-start(bf16[256,8,128]{2,1,0:T(8,128)(2,1)} %k_ref.1) | copy-start | bytes 1572868
  3.4 1.0 %copy-start.2 = (bf16[256,8,128]{2,1,0:T(8,128)(2,1)S(1)}, bf16[256,8,128]{2,1,0:T(8,128)(2,1)}, u32[]{:S(2)}) copy-start(bf16[256,8,128]{2,1,0:T(8,128)(2,1)} %v_ref.1) | copy-start | bytes 1572868
  4.5 1.0 %copy-start.3 = (bf16[256,8,128]{2,1,0:T(8,128)(2,1)S(1)}, bf16[256,8,128]{2,1,0:T(8,128)(2,1)}, u32[]{:S(2)}) copy-start(bf16[256,8,128]{2,1,0:T(8,128)(2,1)} %t_ref.1) | copy-start | bytes 1572868
  8.1 29.8 %collective-permute-start = (bf16[2064,128]{1,0:T(8,128)(2,1)}, bf16[2064,128]{1,0:T(8,128)(2,1)S(1)}, u32[]{:S(2)}, u32[]{:S(2)}) collective-permute-start(bf16[2064,128]{1,0:T(8,128)(2,1)} %get-tuple-element.24), channel_id=1, source_target_pairs={{0,1},{1,0},{4,5},{5,4},{8,9},{9,8},{12,13},{13,12},{2,3},{3,2},{6... | collective-permute-start | bytes 1585160 | tf_op jit(solution)/shard_map/ppermute | solution.py:604
  8.7 19.4 %collective-permute-start.4 = (bf16[1424,128]{1,0:T(8,128)(2,1)S(1)}, bf16[1424,128]{1,0:T(8,128)(2,1)S(1)}, u32[]{:S(2)}, u32[]{:S(2)}) collective-permute-start(bf16[1424,128]{1,0:T(8,128)(2,1)S(1)} %get-tuple-element.26), channel_id=1, source_target_pairs={{1,8},{5,12},{8,1},{12,5},{3,10},{7,14},{10,3},{14,7},{17,24},{21,... | collective-permute-start | bytes 1093640 | tf_op jit(solution)/shard_map/ppermute | solution.py:604
  12.8 23.1 %collective-permute-start.5 = (bf16[1424,128]{1,0:T(8,128)(2,1)S(1)}, bf16[1424,128]{1,0:T(8,128)(2,1)S(1)}, u32[]{:S(2)}, u32[]{:S(2)}) collective-permute-start(bf16[1424,128]{1,0:T(8,128)(2,1)S(1)} %get-tuple-element.27), channel_id=1, source_target_pairs={{1,9},{5,13},{8,0},{12,4},{3,11},{7,15},{10,2},{14,6},{17,25},{21,... | collective-permute-start | bytes 1093640 | tf_op jit(solution)/shard_map/ppermute | solution.py:604
  14.1 31.7 %collective-permute-start.2 = (bf16[2064,128]{1,0:T(8,128)(2,1)S(1)}, bf16[2064,128]{1,0:T(8,128)(2,1)}, u32[]{:S(2)}, u32[]{:S(2)}) collective-permute-start(bf16[2064,128]{1,0:T(8,128)(2,1)S(1)} %get-tuple-element.22.refs_0_.kv_own), channel_id=1, source_target_pairs={{0,4},{1,5},{4,8},{5,9},{8,12},{9,13},{2,6},{3,7},{6,10},{7,11},{1... | collective-permute-start | bytes 1585160 | tf_op jit(solution)/shard_map/ppermute | solution.py:604
  16.1 29.7 %collective-permute-start.1 = (bf16[2064,128]{1,0:T(8,128)(2,1)}, bf16[2064,128]{1,0:T(8,128)(2,1)S(1)}, u32[]{:S(2)}, u32[]{:S(2)}) collective-permute-start(bf16[2064,128]{1,0:T(8,128)(2,1)} %get-tuple-element.25), channel_id=1, source_target_pairs={{0,1},{1,0},{4,5},{5,4},{8,9},{9,8},{12,13},{13,12},{2,3},{3,2},{6... | collective-permute-start | bytes 1585160 | tf_op jit(solution)/shard_map/ppermute | solution.py:604
  28.1 23.5 %collective-permute-start.3 = (bf16[2064,128]{1,0:T(8,128)(2,1)}, bf16[2064,128]{1,0:T(8,128)(2,1)}, u32[]{:S(2)}, u32[]{:S(2)}) collective-permute-start(bf16[2064,128]{1,0:T(8,128)(2,1)} %get-tuple-element.24), channel_id=1, source_target_pairs={{0,5},{1,4},{4,9},{5,8},{8,13},{9,12},{2,7},{3,6},{6,11},{7,10},{1... | collective-permute-start | bytes 1585160 | tf_op jit(solution)/shard_map/ppermute | solution.py:604
  35.9 42.1 %collective-permute-start.7 = (bf16[2064,128]{1,0:T(8,128)(2,1)S(1)}, bf16[2064,128]{1,0:T(8,128)(2,1)S(1)}, u32[]{:S(2)}, u32[]{:S(2)}) collective-permute-start(bf16[2064,128]{1,0:T(8,128)(2,1)S(1)} %get-tuple-element.23.refs_1_.qg_own), channel_id=1, source_target_pairs={{4,0},{5,1},{8,4},{9,5},{12,8},{13,9},{6,2},{7,3},{10,6},{11,7},{1... | collective-permute-start | bytes 1585160 | tf_op jit(solution)/shard_map/ppermute | solution.py:604
  37.8 40.2 %collective-permute-start.8 = (bf16[2064,128]{1,0:T(8,128)(2,1)}, bf16[2064,128]{1,0:T(8,128)(2,1)}, u32[]{:S(2)}, u32[]{:S(2)}) collective-permute-start(bf16[2064,128]{1,0:T(8,128)(2,1)} %get-tuple-element.25), channel_id=1, source_target_pairs={{4,1},{5,0},{8,5},{9,4},{12,9},{13,8},{6,3},{7,2},{10,7},{11,6},{1... | collective-permute-start | bytes 1585160 | tf_op jit(solution)/shard_map/ppermute | solution.py:604
  39.8 0.7 copy-start.6
  67.7 10.4 %collective-permute-start.10 = (bf16[608,128]{1,0:T(8,128)(2,1)S(1)}, bf16[608,128]{1,0:T(8,128)(2,1)S(1)}, u32[]{:S(2)}, u32[]{:S(2)}) collective-permute-start(bf16[608,128]{1,0:T(8,128)(2,1)S(1)} %get-tuple-element.32.message), channel_id=1, source_target_pairs={{8,0},{9,1},{12,4},{13,5},{10,2},{11,3},{14,6},{15,7},{24,16},{25,... | collective-permute-start | bytes 466952 | tf_op jit(solution)/shard_map/ppermute | solution.py:604
  69.0 9.3 %collective-permute-start.9 = (bf16[608,128]{1,0:T(8,128)(2,1)S(1)}, bf16[608,128]{1,0:T(8,128)(2,1)S(1)}, u32[]{:S(2)}, u32[]{:S(2)}) collective-permute-start(bf16[608,128]{1,0:T(8,128)(2,1)S(1)} %get-tuple-element.32.message), channel_id=1, source_target_pairs={{4,0},{5,1},{8,4},{9,5},{12,8},{13,9},{6,2},{7,3},{10,6},{11,7},{1... | collective-permute-start | bytes 466952 | tf_op jit(solution)/shard_map/ppermute | solution.py:604
  70.9 15.4 %collective-permute-start.6 = (bf16[2,4,256,128]{3,2,1,0:T(8,128)(2,1)S(1)}, bf16[2,4,256,128]{3,2,1,0:T(8,128)(2,1)S(1)}, u32[]{:S(2)}, u32[]{:S(2)}) collective-permute-start(bf16[2,4,256,128]{3,2,1,0:T(8,128)(2,1)S(1)} %get-tuple-element.29), channel_id=1, source_target_pairs={{0,1},{1,0},{4,5},{5,4},{8,9},{9,8},{12,13},{13,12},{2,3},{3,2},{6... | collective-permute-start | bytes 1572872 | tf_op jit(solution)/shard_map/ppermute | solution.py:604
  84.4 3.3 %collective-permute-start.11 = (bf16[2,4,256,128]{3,2,1,0:T(8,128)(2,1)S(1)}, bf16[2,4,256,128]{3,2,1,0:T(8,128)(2,1)S(1)}, u32[]{:S(2)}, u32[]{:S(2)}) collective-permute-start(bf16[2,4,256,128]{3,2,1,0:T(8,128)(2,1)S(1)} %get-tuple-element.37), channel_id=1, source_target_pairs={{0,1},{1,0},{4,5},{5,4},{8,9},{9,8},{12,13},{13,12},{2,3},{3,2},{6... | collective-permute-start | bytes 1572872 | tf_op jit(solution)/shard_map/ppermute | solution.py:604

commit v2 on v1

v2 whole, which is shorter than its diff:
```python
import functools
import math

import jax
import jax.numpy as jnp
from jax import lax
from jax.experimental import pallas as pl
from jax.experimental.pallas import tpu as pltpu
from jax.sharding import PartitionSpec as P

WIN = 1024
SESSIONS = 6
EPSILON = 1e-06
MASKED = -1e30
AXES = ("ctx", "pair")
EXTRA = 16
LANES = 128
VMEM_LIMIT = 20 << 20

f32 = jnp.float32
bf16 = jnp.bfloat16


def dot(a, b):
    return lax.dot_general(a, b, (((1,), (0,)), ((), ())), preferred_element_type=f32)


def dot_t(a, b):
    return lax.dot_general(a, b, (((1,), (1,)), ((), ())), preferred_element_type=f32)


def t_dot(a, b):
    return lax.dot_general(a, b, (((0,), (0,)), ((), ())), preferred_element_type=f32)


def feature(x):
    return jnp.where(x > 0, x + 1.0, jnp.exp(jnp.minimum(x, 0.0)))


def slope(x):
    return jnp.where(x > 0, 1.0, jnp.exp(jnp.minimum(x, 0.0)))


def params(micros):
    return dict(
        compiler_params=pltpu.CompilerParams(vmem_limit_bytes=VMEM_LIMIT),
        cost_estimate=pl.CostEstimate(
            flops=int(micros * 1.15e9), bytes_accessed=int(micros * 1e6), transcendentals=0
        ),
    )


def row_of(column):
    n = column.shape[0]
    return jnp.concatenate(
        [
            jnp.transpose(jnp.broadcast_to(column[i : i + LANES], (LANES, LANES)))[0:1]
            for i in range(0, n, LANES)
        ],
        axis=1,
    )


def column_of(rows):
    return jnp.concatenate(
        [
            jnp.transpose(jnp.broadcast_to(rows[i : i + 1], (LANES, LANES)))[:, 0:1]
            for i in range(rows.shape[0])
        ],
        axis=0,
    )


class Plan:
    def __init__(self, length, heads, width, total):
        self.length = length
        self.heads = heads
        self.all = heads // 2
        self.groups = 2 if self.all % 2 == 0 else 1
        self.half = self.all // self.groups
        self.width = width
        self.chip = 2 * length
        longest = total // 3
        reach = min(WIN, longest) - 1
        tail = max(reach - self.chip, 0)
        self.far = longest - 1 > 2 * self.chip or longest - 1 > reach
        self.merged = tail <= length
        self.tail = -(-tail // 16) * 16 if self.merged else length
        self.tail_fill = length if self.merged else self.chip
        self.before = self.tail_fill + self.chip
        self.code_rows = length // LANES
        self.stat_rows = -(-(2 * self.half * self.chip // LANES) // 16) * 16
        self.state_rows = self.half * width
        self.rows = self.half * 2 * length + EXTRA
        self.tail_rows = self.all * 2 * self.tail + EXTRA
        self.far_refs = 2 if self.merged else 4
        self.first_near = 3 if self.merged else 1
        self.pair_rows = self.all * 4 * length + EXTRA


def pack_body(p, core_ref, q_ref, k_ref, v_ref, t_ref, w_ref, s_ref, *rest):
    number = (len(rest) - 4) // 2
    outs, staged = rest[:number], rest[number : 2 * number]
    scratch, landed, sems, out_sems = rest[2 * number :]
    core = core_ref[0]
    L = p.length
    copies = [
        pltpu.make_async_copy(ref, landed.at[n], sems.at[n])
        for n, ref in enumerate((k_ref, v_ref, q_ref, t_ref))
    ]
    for copy in copies:
        copy.start()
    weight = column_of(w_ref[...].astype(f32))
    codes = jnp.concatenate(
        [s_ref[...].astype(f32) + 1.0, jnp.zeros((EXTRA - p.code_rows, LANES), f32)], axis=0
    ).astype(bf16)
    for ref in staged:
        ref[ref.shape[0] - EXTRA :, :] = codes
    for n in range(4):
        copies[n].wait()
        x = jnp.swapaxes(landed[n].astype(f32), 0, 1)
        if n == 3:
            x = x * weight[None]
        scratch[n] = x.astype(bf16)
    leaving = []

    def leave(n):
        leaving.append(pltpu.make_async_copy(staged[n], outs[n], out_sems.at[n]))
        leaving[-1].start()

    other = (1 - core) * p.all
    for n in range(4):
        for h in range(p.all):
            at = (n * p.all + h) * L
            staged[0][at : at + L, :] = scratch[n, other + h]
    leave(0)
    if p.merged:
        first = (1 - core) * 2
        lead = core * (L - p.tail)
        for t, base in ((1, core * p.all), (2, other)):
            for n in range(2):
                for h in range(p.all):
                    at = (n * p.all + h) * p.tail
                    staged[t][at : at + p.tail, :] = scratch[
                        first + n, base + h, pl.ds(pl.multiple_of(lead, 16), p.tail), :
                    ]
            leave(t)
    for g in range(p.groups):
        for x, first, base in (
            (0, core * 2, core * p.all),
            (1, (1 - core) * 2, core * p.all),
            (2, core * 2, other),
            (3, (1 - core) * 2, other),
        ):
            to = p.first_near + 4 * g + x
            for n in range(2):
                for h in range(p.half):
                    at = (n * p.half + h) * L
                    staged[to][at : at + L, :] = scratch[first + n, base + g * p.half + h]
            leave(to)
    for copy in leaving:
        copy.wait()


def pack(p, core, q, k, v, targets, weights, sessions):
    shapes = [(p.pair_rows, p.width)]
    if p.merged:
        shapes += [(p.tail_rows, p.width)] * 2
    shapes += [(p.rows, p.width)] * (4 * p.groups)
    vmem = pl.BlockSpec(memory_space=pltpu.VMEM)
    hbm = pl.BlockSpec(memory_space=pl.ANY)
    return pl.pallas_call(
        functools.partial(pack_body, p),
        out_shape=[jax.ShapeDtypeStruct(x, bf16) for x in shapes],
        in_specs=[pl.BlockSpec(memory_space=pltpu.SMEM)] + [hbm] * 4 + [vmem] * 2,
        out_specs=[hbm] * len(shapes),
        scratch_shapes=[pltpu.VMEM(x, bf16) for x in shapes]
        + [
            pltpu.VMEM((4, p.heads, p.length, p.width), bf16),
            pltpu.VMEM((4, p.length, p.heads, p.width), bf16),
            pltpu.SemaphoreType.DMA((4,)),
            pltpu.SemaphoreType.DMA((len(shapes),)),
        ],
        compiler_params=pltpu.CompilerParams(vmem_limit_bytes=56 << 20),
        name="pack",
    )(core, q, k, v, targets, weights, sessions)


def code_block(p, core, pick):
    one, two = (ref[ref.shape[0] - EXTRA :, :].astype(f32)[: p.code_rows] for ref in pick)
    return jnp.where(core == 0, one, two)


def count(condition):
    return jnp.sum(
        jnp.sum(jnp.where(condition, 1.0, 0.0), axis=1, keepdims=True), axis=0, keepdims=True
    )


def drive(streams):
    streams = list(streams)
    while streams:
        streams = [x for x in streams if next(x, streams) is not streams]


def flat(rows):
    return jnp.concatenate([rows[i : i + 1] for i in range(rows.shape[0])], axis=1)


def in_order(core, same, cross):
    first = jnp.where(core == 0, same, cross)
    second = jnp.where(core == 0, cross, same)
    return jnp.concatenate([first, second], axis=0)


class Chip:
    def __init__(self, p, core, same, cross):
        self.p, self.core, self.same, self.cross = p, core, same, cross

    def codes(self):
        return in_order(
            self.core,
            code_block(self.p, self.core, self.same),
            code_block(self.p, self.core, self.cross),
        )

    def bring(self, targets, start, index=None):
        p = self.p
        L = p.length
        for me in range(2):

            @pl.when(self.core == me)
            def _():
                for ref, which, lead in (
                    (self.same[me], me, None),
                    (self.cross[me], 1 - me, index),
                ):
                    to = start + which * L
                    for n, target in enumerate(targets):
                        for h in range(p.half):
                            at = n * p.half + h
                            if lead is not None:
                                at = (lead[0] + n) * p.all + lead[1] + h
                            target[h, to : to + L, :] = ref[at * L : (at + 1) * L, :]


def bring_tail(p, core, group, pick, targets, start):
    for me in range(2):

        @pl.when(core == me)
        def _():
            for n, target in enumerate(targets):
                for h in range(p.half):
                    at = (n * p.all + group * p.half + h) * p.tail
                    target[h, start : start + p.tail, :] = pick[me][at : at + p.tail, :]


def forward_body(p, group, core_ref, win_ref, *refs):
    (pair, x1, x2, r1, r2, r3, r4), refs = refs[:7], refs[7:]
    far, refs = refs[: p.far_refs], refs[p.far_refs :]
    if p.far:
        far_ref, refs = refs[0], refs[1:]
    att_keep, att_send, gn_out, message, ks, vs, qs, gs, atts, dqs, stat = refs
    core = core_ref[0]
    L, C, B, D = p.length, p.chip, p.before, p.width
    scale = 1.0 / math.sqrt(D)
    c2 = scale * math.log2(math.e)

    head = group * p.half
    own_keys_at = Chip(p, core, (x1, x2), (pair, pair))
    own_queries_at = Chip(p, core, (x2, x1), (pair, pair))
    near_at = Chip(p, core, (r1, r2), (r4, r3))
    own_keys_at.bring((ks, vs), B, (0, head))
    own_queries_at.bring((qs, gs), 0, (2, head))
    near_at.bring((ks, vs), p.tail_fill)
    own_codes = own_keys_at.codes()
    near_codes = near_at.codes()
    if p.merged:
        pick = (far[1], far[0])
        bring_tail(p, core, group, pick, (ks, vs), p.tail_fill - p.tail)
        far_codes = code_block(p, core, pick)
    else:
        far_at = Chip(p, core, (far[0], far[1]), (far[3], far[2]))
        far_at.bring((ks, vs), 0)
        far_codes = far_at.codes()
    halo_codes = jnp.concatenate([far_codes, near_codes], axis=0)
    code = column_of(own_codes)
    last = near_codes[2 * p.code_rows - 1 :, LANES - 1 :]
    first_own = own_codes[0:1, 0:1]
    lo_all = jnp.zeros((C, 1), f32)
    for n in range(1, SESSIONS + 1):
        start = count(own_codes < n) - count(halo_codes >= n)
        lo_all = jnp.where(code == n, start, lo_all)
    lo_all = lo_all.astype(jnp.int32)
    cont = count(jnp.logical_and(halo_codes == last, halo_codes > 0)).astype(jnp.int32)
    halo_pos = lax.broadcasted_iota(jnp.int32, (B, 1), 0) - B
    in_start = jnp.broadcast_to(halo_pos >= -cont, (B, D))
    if p.merged and p.tail < p.tail_fill:
        gap = p.tail_fill - p.tail
        ks[:, 0:gap, :] = jnp.zeros((p.half, gap, D), bf16)
        vs[:, 0:gap, :] = jnp.zeros((p.half, gap, D), bf16)
    phis, starts, states = {}, {}, {}

    def stream(h, r):
        rows = slice(r * L, (r + 1) * L)
        q = qs[h, rows, :]
        g = gs[h, rows, :]
        gf = g.astype(f32)
        qf = q.astype(f32)
        lo = lo_all[rows]
        mine = code[rows]
        t_pos = lax.broadcasted_iota(jnp.int32, (L, 1), 0) + r * L
        window = win_ref[core * p.all + group * p.half + h]
        begin = 0 if not p.merged else r * L
        n_halo = B - begin
        n_own = (r + 1) * L
        wide = n_halo + n_own
        low = jnp.maximum(lo, t_pos - window + 1)
        score = dot_t(q, ks[h, begin : begin + wide, :])
        yield
        if r == 0:
            phis[h] = feature(ks[h, B:, :].astype(f32)).astype(bf16)
            if p.far:
                starts[h] = far_ref[h * D : (h + 1) * D, :]
            else:
                halo_phi = jnp.where(in_start, feature(ks[h, 0:B, :].astype(f32)), 0.0)
                starts[h] = t_dot(halo_phi.astype(bf16), vs[h, 0:B, :]).astype(bf16)
        phi_k, start_state = phis[h], starts[h]
        phi_q = feature(qf).astype(bf16)
        a = dot_t(phi_q, phi_k[:n_own])
        from_start = dot(phi_q, start_state)
        yield
        s_pos = lax.broadcasted_iota(jnp.int32, (L, wide), 1) + (begin - B)
        own_pos = lax.broadcasted_iota(jnp.int32, (L, n_own), 1)
        causal = own_pos <= t_pos
        score = jnp.concatenate(
            [
                jnp.where(s_pos[:, :n_halo] >= low, score[:, :n_halo], MASKED),
                jnp.where(
                    jnp.logical_and(own_pos >= low, causal), score[:, n_halo:], MASKED
                ),
            ],
            axis=1,
        )
        peak = jnp.max(score, axis=1, keepdims=True) * c2
        e = jnp.exp2(score * c2 - peak)
        total = jnp.sum(e, axis=1, keepdims=True)
        yield
        inverse = 1.0 / total
        window_out = dot(e.astype(bf16), vs[h, begin : begin + wide, :]) * inverse
        alike = jnp.logical_and(own_pos >= lo, causal)
        a = jnp.where(alike, a, 0.0).astype(bf16)
        reads = mine == last
        numerator = dot(a, vs[h, B : B + n_own, :]) + jnp.where(reads, from_start, 0.0)
        grad_prob = dot_t(g, vs[h, begin : begin + wide, :])
        yield
        rowdot = jnp.sum(gf * window_out, axis=1, keepdims=True)
        inverse_rms = lax.rsqrt(jnp.mean(numerator * numerator, axis=1, keepdims=True) + EPSILON)
        linear_out = numerator * inverse_rms
        grad_num = (
            inverse_rms * (gf - linear_out * jnp.mean(gf * linear_out, axis=1, keepdims=True))
        ).astype(bf16)
        gn_out[h, rows, :] = grad_num
        atts[h, rows, :] = (linear_out + window_out).astype(bf16)
        b = dot_t(grad_num, vs[h, B : B + n_own, :])
        ds = (e * (grad_prob - rowdot)).astype(bf16)
        yield
        dq = dot(ds, ks[h, begin : begin + wide, :]) * (inverse * scale)
        opening = mine == first_own
        part = t_dot(jnp.where(opening, phi_q, jnp.zeros_like(phi_q)), grad_num)
        lse = peak + jnp.log2(total)
        for which, column in ((0, lse), (1, rowdot)):
            base = (which * p.half + h) * (C // LANES) + r * (L // LANES)
            row = row_of(column)
            for j in range(L // LANES):
                stat[base + j : base + j + 1, :] = row[:, j * LANES : (j + 1) * LANES]
        yield
        b = jnp.where(alike, b, 0.0).astype(bf16)
        grad_phi_q = dot(b, phi_k[:n_own]) + jnp.where(
            reads, dot_t(grad_num, start_state), 0.0
        )
        dqs[h, rows, :] = (slope(qf) * grad_phi_q + dq).astype(bf16)
        states[h] = states[h] + part if r else part
        if r:
            message[h * D : (h + 1) * D, :] = states[h].astype(bf16)

    drive(stream(h, r) for h in range(p.half) for r in range(2))

    values = stat[...]
    if 2 * p.half * C // LANES < p.stat_rows:
        used = lax.broadcasted_iota(jnp.int32, values.shape, 0) < 2 * p.half * C // LANES
        values = jnp.where(used, values, 0.0)
    for n in range(3):
        piece = values.astype(bf16)
        at = p.state_rows + n * p.stat_rows
        message[at : at + p.stat_rows, :] = piece
        values = values - piece.astype(f32)
    for h in range(p.half):
        for n, src in ((0, atts), (1, dqs)):
            att_keep[n, h] = src[h, pl.ds(pl.multiple_of(core * L, 16), L), :]
            att_send[n, h] = src[h, pl.ds(pl.multiple_of((1 - core) * L, 16), L), :]


def forward(p, group, core, windows, payloads, far_state):
    vmem = pl.BlockSpec(memory_space=pltpu.VMEM)
    smem = pl.BlockSpec(memory_space=pltpu.SMEM)
    half = jax.ShapeDtypeStruct((2, p.half, p.length, p.width), bf16)
    outs = [
        half,
        half,
        jax.ShapeDtypeStruct((p.half, p.chip, p.width), bf16),
        jax.ShapeDtypeStruct((p.state_rows + 3 * p.stat_rows, p.width), bf16),
    ]
    extra = [far_state] if p.far else []
    span = p.before + p.chip
    return pl.pallas_call(
        functools.partial(forward_body, p, group),
        out_shape=outs,
        in_specs=[smem, smem] + [vmem] * (7 + p.far_refs + len(extra)),
        out_specs=[vmem] * 4,
        scratch_shapes=[
            pltpu.VMEM((p.half, span, p.width), bf16),
            pltpu.VMEM((p.half, span, p.width), bf16),
            pltpu.VMEM((p.half, p.chip, p.width), bf16),
            pltpu.VMEM((p.half, p.chip, p.width), bf16),
            pltpu.VMEM((p.half, p.chip, p.width), bf16),
            pltpu.VMEM((p.half, p.chip, p.width), bf16),
            pltpu.VMEM((p.stat_rows, p.width), f32),
        ],
        **params(3 * p.half),
        name="forward",
    )(core, windows, *payloads, *extra)


def stats_of(p, values, head, count):
    per = p.chip // LANES
    result = []
    for which in range(2):
        base = (which * p.half + head) * per
        result.append(flat(values[base : base + per])[:, :count])
    return result


def unpack_stats(p, message):
    total = jnp.zeros((p.stat_rows, LANES), f32)
    for n in reversed(range(3)):
        at = p.state_rows + n * p.stat_rows
        total = total + message[at : at + p.stat_rows, :].astype(f32)
    return total


def own_body(p, group, core_ref, win_ref, pair, x1, x2, gn, message, dk_o, dv_o, *s):
    ks, vs, qs, gs = s
    core = core_ref[0]
    L, C, D = p.length, p.chip, p.width
    scale = 1.0 / math.sqrt(D)
    c2 = scale * math.log2(math.e)
    head = group * p.half
    own_keys_at = Chip(p, core, (x1, x2), (pair, pair))
    own_keys_at.bring((ks, vs), 0, (0, head))
    Chip(p, core, (x2, x1), (pair, pair)).bring((qs, gs), 0, (2, head))
    own_codes = own_keys_at.codes()
    code = column_of(own_codes)
    hi_all = jnp.zeros((C, 1), f32)
    for n in range(1, SESSIONS + 1):
        hi_all = jnp.where(code == n, count(own_codes <= n) - 1.0, hi_all)
    hi_all = hi_all.astype(jnp.int32)
    stats = unpack_stats(p, message)

    def stream(h, r):
        window = win_ref[core * p.all + group * p.half + h]
        lse, rowdot = stats_of(p, stats, h, C)
        rows = slice(r * L, (r + 1) * L)
        after = slice(r * L, C)
        wide = C - r * L
        k, v = ks[h, rows, :], vs[h, rows, :]
        q, g = qs[h, after, :], gs[h, after, :]
        score = dot_t(k, q)
        grad_prob = dot_t(v, g)
        yield
        phi_q = feature(q.astype(f32)).astype(bf16)
        kf = k.astype(f32)
        grad_num = gn[h, after, :]
        a = dot_t(feature(kf).astype(bf16), phi_q)
        b = dot_t(v, grad_num)
        yield
        hi = hi_all[rows]
        s_pos = lax.broadcasted_iota(jnp.int32, (L, 1), 0) + r * L
        t_pos = lax.broadcasted_iota(jnp.int32, (L, wide), 1) + r * L
        alike = jnp.logical_and(t_pos >= s_pos, t_pos <= hi)
        allowed = jnp.logical_and(alike, t_pos < s_pos + window)
        prob = jnp.exp2(jnp.where(allowed, score * c2 - lse[:, after], MASKED))
        ds = (prob * (grad_prob - rowdot[:, after])).astype(bf16)
        yield
        dk = dot(ds, q) * scale
        dv = dot(prob.astype(bf16), g)
        a = jnp.where(alike, a, 0.0).astype(bf16)
        b = jnp.where(alike, b, 0.0).astype(bf16)
        yield
        dk_o[h, rows, :] = dk + slope(kf) * dot(b, phi_q)
        dv_o[h, rows, :] = dv + dot(a, grad_num)

    drive(stream(h, r) for h in range(p.half) for r in range(2))


def own_keys(p, group, core, windows, pair, x1, x2, gn, message):
    vmem = pl.BlockSpec(memory_space=pltpu.VMEM)
    smem = pl.BlockSpec(memory_space=pltpu.SMEM)
    full = jax.ShapeDtypeStruct((p.half, p.chip, p.width), f32)
    tile = pltpu.VMEM((p.half, p.chip, p.width), bf16)
    return pl.pallas_call(
        functools.partial(own_body, p, group),
        out_shape=[full, full],
        in_specs=[smem, smem] + [vmem] * 5,
        out_specs=[vmem] * 2,
        scratch_shapes=[tile] * 4,
        **params(1.5 * p.half),
        name="own_keys",
    )(core, windows, pair, x1, x2, gn, message)


def later_body(p, group, core_ref, win_ref, *refs):
    (pair, x1, x2, r1, r2, r3, r4), refs = refs[:7], refs[7:]
    far, refs = refs[: p.far_refs], refs[p.far_refs :]
    (message_1, message_2, dk_i, dv_i), refs = refs[:4], refs[4:]
    if p.far:
        far_ref, refs = refs[0], refs[1:]
    keep, send, ks, vs, qs, gs, dks, dvs = refs
    core = core_ref[0]
    L, C, D = p.length, p.chip, p.width
    N = p.tail_fill
    scale = 1.0 / math.sqrt(D)
    c2 = scale * math.log2(math.e)
    head = group * p.half
    own_keys_at = Chip(p, core, (x1, x2), (pair, pair))
    near_at = Chip(p, core, (r2, r1), (r3, r4))
    own_keys_at.bring((ks, vs), 0, (0, head))
    near_at.bring((qs, gs), 0)
    own_codes = own_keys_at.codes()
    near_codes = near_at.codes()
    if p.merged:
        pick = (far[0], far[1])
        bring_tail(p, core, group, pick, (qs, gs), C)
        far_codes = code_block(p, core, pick)
    else:
        far_at = Chip(p, core, (far[1], far[0]), (far[2], far[3]))
        far_at.bring((qs, gs), C)
        far_codes = far_at.codes()
    after_codes = jnp.concatenate([near_codes, far_codes], axis=0)
    code = column_of(own_codes)
    final = own_codes[2 * p.code_rows - 1 :, LANES - 1 :]
    hi_last = C - 1 + count(after_codes == final)
    hi_all = jnp.where(code == final, hi_last, -1.0).astype(jnp.int32)
    first_next = near_codes[0:1, 0:1]
    goes_on = jnp.logical_and(first_next > 0, first_next == far_codes[0:1, 0:1])
    stats_1 = unpack_stats(p, message_1)
    stats_2 = unpack_stats(p, message_2)
    if p.merged and p.tail < p.tail_fill:
        gap = p.tail_fill - p.tail
        qs[:, C + p.tail :, :] = jnp.zeros((p.half, gap, D), bf16)
        gs[:, C + p.tail :, :] = jnp.zeros((p.half, gap, D), bf16)
    def stream(h, r):
        window = win_ref[core * p.all + group * p.half + h]
        lse, rowdot = (
            jnp.concatenate([x, y], axis=1)
            for x, y in zip(stats_of(p, stats_1, h, C), stats_of(p, stats_2, h, N))
        )
        rows = slice(r * L, (r + 1) * L)
        wide = C + N if (r == 1 or not p.merged) else C
        k, v = ks[h, rows, :], vs[h, rows, :]
        q, g = qs[h, 0:wide, :], gs[h, 0:wide, :]
        score = dot_t(k, q)
        grad_prob = dot_t(v, g)
        yield
        if p.far:
            later_state = far_ref[h * D : (h + 1) * D, :]
        else:
            here = slice(h * D, (h + 1) * D)
            later_state = (
                message_1[here, :].astype(f32)
                + jnp.where(goes_on, message_2[here, :].astype(f32), 0.0)
            ).astype(bf16)
        kf = k.astype(f32)
        uses = code[rows] == first_next
        phi_k = feature(kf).astype(bf16)
        dk_lin = dot_t(v, later_state)
        dv_lin = dot(phi_k, later_state)
        yield
        s_pos = lax.broadcasted_iota(jnp.int32, (L, 1), 0) + r * L
        t_pos = lax.broadcasted_iota(jnp.int32, (L, wide), 1) + C
        allowed = t_pos <= jnp.minimum(hi_all[rows], s_pos + window - 1)
        prob = jnp.exp2(jnp.where(allowed, score * c2 - lse[:, :wide], MASKED))
        ds = (prob * (grad_prob - rowdot[:, :wide])).astype(bf16)
        yield
        dk = dot(ds, q) * scale
        dv = dot(prob.astype(bf16), g)
        yield
        dks[h, rows, :] = (
            dk_i[h, rows, :] + dk + slope(kf) * jnp.where(uses, dk_lin, 0.0)
        ).astype(bf16)
        dvs[h, rows, :] = (dv_i[h, rows, :] + dv + jnp.where(uses, dv_lin, 0.0)).astype(bf16)

    drive(stream(h, r) for h in range(p.half) for r in range(2))

    for h in range(p.half):
        for n, src in ((0, dks), (1, dvs)):
            keep[n, h] = src[h, pl.ds(pl.multiple_of(core * L, 16), L), :]
            send[n, h] = src[h, pl.ds(pl.multiple_of((1 - core) * L, 16), L), :]


def later_keys(p, group, core, windows, payloads, far_state):
    vmem = pl.BlockSpec(memory_space=pltpu.VMEM)
    smem = pl.BlockSpec(memory_space=pltpu.SMEM)
    half = jax.ShapeDtypeStruct((2, p.half, p.length, p.width), bf16)
    extra = [far_state] if p.far else []
    tile = pltpu.VMEM((p.half, p.chip, p.width), bf16)
    tall = pltpu.VMEM((p.half, p.chip + p.tail_fill, p.width), bf16)
    return pl.pallas_call(
        functools.partial(later_body, p, group),
        out_shape=[half, half],
        in_specs=[smem, smem] + [vmem] * (11 + p.far_refs + len(extra)),
        out_specs=[vmem] * 2,
        scratch_shapes=[tile, tile, tall, tall, tile, tile],
        **params(1.5 * p.half),
        name="later_keys",
    )(core, windows, *payloads, *extra)


def unpack_body(p, core_ref, *refs):
    parts, (out_a, out_b, scratch) = refs[: 2 * p.groups], refs[2 * p.groups :]
    core = core_ref[0]
    for n, out in ((0, out_a), (1, out_b)):
        for group in range(p.groups):
            for ref, which in ((parts[2 * group], core), (parts[2 * group + 1], 1 - core)):
                for h in range(p.half):
                    scratch[which * p.all + group * p.half + h] = ref[n, h].astype(f32)
        out[...] = jnp.swapaxes(scratch[...], 0, 1).astype(bf16)


def unpack(p, core, parts):
    vmem = pl.BlockSpec(memory_space=pltpu.VMEM)
    out = jax.ShapeDtypeStruct((p.length, p.heads, p.width), bf16)
    return pl.pallas_call(
        functools.partial(unpack_body, p),
        out_shape=[out, out],
        in_specs=[pl.BlockSpec(memory_space=pltpu.SMEM)] + [vmem] * (2 * p.groups),
        out_specs=[vmem, vmem],
        scratch_shapes=[pltpu.VMEM((p.heads, p.length, p.width), f32)],
        **params(1.4),
        name="unpack",
    )(core, *parts)


def folded(session, state, backward):
    sessions = lax.all_gather(session, "ctx")
    states = lax.all_gather(state, "ctx")
    count = lax.axis_size("ctx")
    here = lax.axis_index("ctx")

    def one(hop, carry):
        held, total = carry
        source = count - 1 - hop if backward else hop
        new = lax.dynamic_index_in_dim(sessions, source, 0, False)
        first, last = new[0], new[1]
        part = lax.dynamic_index_in_dim(states, source, 0, False).astype(f32)
        entering, leaving = (last, first) if backward else (first, last)
        whole = jnp.logical_and(entering == held, entering == leaving)
        return leaving, part + jnp.where(whole, total, 0.0)

    steps = count - 1 - here if backward else here
    start = (jnp.zeros((), jnp.int32) - 1, jnp.zeros(state.shape, f32))
    return lax.fori_loop(0, steps, one, start)[1].astype(bf16)


def shards(p, queries, key_vectors, value_vectors, targets, token_weights, sessions, window_size):
    L = p.length
    chips = lax.axis_size("ctx")
    core_id = lax.axis_index("pair").astype(jnp.int32)
    core = core_id.reshape(1)
    def move(x, target):
        pairs = []
        for c in range(chips):
            for i in range(2):
                to, j = target(c, i)
                if 0 <= to < chips:
                    pairs.append((2 * c + i, 2 * to + j))
        return lax.ppermute(x, AXES, pairs)

    packed = pack(
        p,
        core,
        queries,
        key_vectors,
        value_vectors,
        targets,
        token_weights.reshape(-1, LANES),
        sessions.reshape(-1, LANES),
    )
    def exchange(payloads, by):
        x1, x2, x3, x4 = payloads
        return (
            move(x1, lambda c, i: (c + by, 0) if i == 0 else (c - by, 1)),
            move(x2, lambda c, i: (c + by, 1) if i == 1 else (c - by, 0)),
            move(x3, lambda c, i: (c + by, 1) if i == 0 else (c - by, 0)),
            move(x4, lambda c, i: (c + by, 0) if i == 1 else (c - by, 1)),
        )

    near = [packed[p.first_near + 4 * g : p.first_near + 4 * g + 4] for g in range(p.groups)]
    pair = move(packed[0], lambda c, i: (c, 1 - i))
    got = [exchange(x, 1) for x in near]
    if p.merged:
        first_tail, second_tail, pair = lax.optimization_barrier((packed[1], packed[2], pair))
        tails = (
            move(first_tail, lambda c, i: (c + 2, 1) if i == 1 else (c - 2, 0)),
            move(second_tail, lambda c, i: (c + 2, 0) if i == 1 else (c - 2, 1)),
        )
        far = [tails] * p.groups
    else:
        far = [exchange(x, 2) for x in near]

    if p.far:
        both = lax.all_gather(sessions, "pair")
        chip_ends = jnp.stack([both[0, 0], both[1, -1]])

    query_parts, key_parts = [], []
    for group in range(p.groups):
        x1, x2 = near[group][:2]
        near_by = (pair, x1, x2) + got[group] + far[group]
        far_before = far_after = None
        if p.far:
            total = jnp.zeros((p.half, p.width, p.width), f32)
            keys_here = jnp.where(core_id == 0, x1, x2)[: p.rows - EXTRA].reshape(2, p.half, L, p.width)
            keys_pair = pair[: p.pair_rows - EXTRA].reshape(4, p.all, L, p.width)
            keys_pair = keys_pair[:2, group * p.half : (group + 1) * p.half]
            for part, owner in ((keys_here, core_id), (keys_pair, 1 - core_id)):
                rows = lax.dynamic_index_in_dim(both, owner, 0, False)
                phi = feature(part[0].astype(f32))
                phi = jnp.where((rows == chip_ends[1])[None, :, None], phi, 0.0).astype(bf16)
                total = total + jnp.einsum(
                    "hsk,hsd->hkd", phi, part[1], preferred_element_type=f32
                )
            far_before = folded(chip_ends, total.astype(bf16), False).reshape(-1, p.width)
        keep, send, grad_num, message = forward(
            p,
            group,
            core,
            window_size,
            near_by,
            far_before,
        )
        message_1 = move(message, lambda c, i: (c - 1, i))
        message_2 = move(message, lambda c, i: (c - 2, i))
        query_parts += [keep, move(send, lambda c, i: (c, 1 - i))]
        if p.far:
            state = message[: p.state_rows].reshape(p.half, p.width, p.width)
            far_after = folded(chip_ends, state, True).reshape(-1, p.width)
        dk, dv = own_keys(p, group, core, window_size, pair, x1, x2, grad_num, message)
        keep, send = later_keys(
            p,
            group,
            core,
            window_size,
            near_by + (message_1, message_2, dk, dv),
            far_after,
        )
        key_parts += [keep, move(send, lambda c, i: (c, 1 - i))]
    attended, grad_queries = unpack(p, core, query_parts)
    grad_keys, grad_values = unpack(p, core, key_parts)
    return (attended, grad_queries, grad_keys, grad_values)


def solution(mesh):
    rows = P(("groups", "ctx", "pair"), "head", None)
    events = P(("groups", "ctx", "pair"))

    def run(queries, key_vectors, value_vectors, targets, token_weights, sessions, window_size):
        total = queries.shape[0] // mesh.shape["groups"]
        length = total // (mesh.shape["ctx"] * mesh.shape["pair"])
        heads = queries.shape[1] // mesh.shape["head"]
        p = Plan(length, heads, queries.shape[2], total)
        return jax.shard_map(
            functools.partial(shards, p),
            mesh=mesh,
            in_specs=(rows, rows, rows, rows, events, events, P("head")),
            out_specs=(rows, rows, rows, rows),
            check_vma=False,
        )(queries, key_vectors, value_vectors, targets, token_weights, sessions, window_size)

    return run
```

time: 89.9 us -> 84.9 us (0.944)
  starting transfers between devices: 18.9 us -> 36.6 us
  waiting for transfers between devices: 29.3 us -> 13.3 us
  local copies, waits for them, and re-layouts: 5.57 us -> 1.91 us
  Pallas kernels: 34.5 us -> 30.9 us
    ppermute x12 -> x19, starting transfers between devices: 18.9 us -> 36.6 us  [move(): return lax.ppermute(x, AXES, pairs)]
    ppermute x12 -> x19, waiting for transfers between devices: 29.3 us -> 13.3 us  [move(): return lax.ppermute(x, AXES, pairs)]
    pallas_call x4 -> x7, Pallas kernels: 31.8 us -> 28.2 us  [the longest x2 11.5 us: forward(): pl.pallas_call(functools.partial(forward_body, p, group), out_shape=outs,...]
    unnamed x14 -> x10, local copies, waits for them, and re-layouts: 5.49 us -> 1.91 us
  transfers between devices with their start and end apart: 12 -> 19, of which waited for: 6 -> 2; matrix products, arithmetic and copies ran while one was open for 0% -> 0% of each run, Pallas kernels for 34% -> 29%
where the time goes in v2:
time: 84.9 us; the launch traced here: 83.7 us
  starting transfers between devices  36.6 us (43%)
  Pallas kernels  30.9 us (36%)
  waiting for transfers between devices  13.3 us (16%)
  local copies, waits for them, and re-layouts  1.91 us (2%)
  between operations  0.95 us (1%)
    ppermute x19, starting transfers between devices, move(): return lax.ppermute(x, AXES, pairs)  36.6 us
    ppermute x19, waiting for transfers between devices, move(): return lax.ppermute(x, AXES, pairs)  13.3 us
    pallas_call x2, Pallas kernels, forward(): pl.pallas_call(functools.partial(forward_body, p, group), out_shape=outs,...  11.5 us
    pallas_call x2, Pallas kernels, later_keys(): pl.pallas_call(functools.partial(later_body, p, group), out_shape=[half,...  5.86 us
    pallas_call x2, Pallas kernels, own_keys(): pl.pallas_call(functools.partial(own_body, p, group), out_shape=[full, fu...  5.83 us
    pallas_call x1, Pallas kernels, pack(): pl.pallas_call(functools.partial(pack_body, p), out_shape=[jax.ShapeDtype...  5.01 us
    pallas_call x2, Pallas kernels, unpack(): pl.pallas_call(functools.partial(unpack_body, p), out_shape=[out, out], i...  2.7 us
    unnamed x10, local copies, waits for them, and re-layouts  1.91 us
  transfers between devices with their start and end apart: 19, of which 2 were waited for; matrix products, arithmetic and copies ran while one was open for 0% of the time, Pallas kernels for 29%

profile of v2, /device:TPU:9, one launch (start us, length us, event | category | flops | bytes accessed | tf_op | source)
XLA Modules:
  0.0 83.7 jit_solution(5951783709508615504)
XLA Ops:
  0.6 5.0 %pack.1 = (bf16[4112,128]{1,0:T(8,128)(2,1)}, bf16[1424,128]{1,0:T(8,128)(2,1)}, bf16[1424,128]{1,0:T(8,128)(2,1)}, bf16[1040,128]{1,0:T(8,128)(2,1)}, bf16[1040...) custom-call(s32[1]{0:T(128)} %bitcast.core_ref, ...), custom_call_target="tpu_custom_call" | custom-call | tf_op jit(solution)/shard_map/pack/pallas_call | solution.py:172
  6.4 1.9 %collective-permute-start.8 = (bf16[1040,128]{1,0:T(8,128)(2,1)}, bf16[1040,128]{1,0:T(8,128)(2,1)S(1)}, u32[]{:S(2)}, u32[]{:S(2)}) collective-permute-start(bf16[1040,128]{1,0:T(8,128)(2,1)} %get-tuple-element.50.refs_1_.x1), channel_id=1, source_target_pairs={{0,4},{4,8},{5,1},{8,12},{9,5},{13,9},{2,6},{6,10},{7,3},{10,14},{... | collective-permute-start | bytes 798728 | tf_op jit(solution)/shard_map/ppermute | solution.py:687
  8.9 4.2 %collective-permute-start.5 = (bf16[1424,128]{1,0:T(8,128)(2,1)}, bf16[1424,128]{1,0:T(8,128)(2,1)S(1)}, u32[]{:S(2)}, u32[]{:S(2)}) collective-permute-start(bf16[1424,128]{1,0:T(8,128)(2,1)} %get-tuple-element.46), channel_id=1, source_target_pairs={{1,9},{5,13},{8,0},{12,4},{3,11},{7,15},{10,2},{14,6},{17,25},{21,... | collective-permute-start | bytes 1093640 | tf_op jit(solution)/shard_map/ppermute | solution.py:687
  13.1 3.2 %collective-permute-start.6 = (bf16[1424,128]{1,0:T(8,128)(2,1)}, bf16[1424,128]{1,0:T(8,128)(2,1)S(1)}, u32[]{:S(2)}, u32[]{:S(2)}) collective-permute-start(bf16[1424,128]{1,0:T(8,128)(2,1)} %get-tuple-element.47), channel_id=1, source_target_pairs={{1,8},{5,12},{8,1},{12,5},{3,10},{7,14},{10,3},{14,7},{17,24},{21,... | collective-permute-start | bytes 1093640 | tf_op jit(solution)/shard_map/ppermute | solution.py:687
  16.3 1.9 %collective-permute-start.9 = (bf16[1040,128]{1,0:T(8,128)(2,1)}, bf16[1040,128]{1,0:T(8,128)(2,1)S(1)}, u32[]{:S(2)}, u32[]{:S(2)}) collective-permute-start(bf16[1040,128]{1,0:T(8,128)(2,1)} %get-tuple-element.51.refs_2_.x2), channel_id=1, source_target_pairs={{1,5},{4,0},{5,9},{8,4},{9,13},{12,8},{3,7},{6,2},{7,11},{10,6},{1... | collective-permute-start | bytes 798728 | tf_op jit(solution)/shard_map/ppermute | solution.py:687
  18.2 1.9 %collective-permute-start.10 = (bf16[1040,128]{1,0:T(8,128)(2,1)}, bf16[1040,128]{1,0:T(8,128)(2,1)S(1)}, u32[]{:S(2)}, u32[]{:S(2)}) collective-permute-start(bf16[1040,128]{1,0:T(8,128)(2,1)} %get-tuple-element.52), channel_id=1, source_target_pairs={{0,5},{4,9},{5,0},{8,13},{9,4},{13,8},{2,7},{6,11},{7,2},{10,15},{... | collective-permute-start | bytes 798728 | tf_op jit(solution)/shard_map/ppermute | solution.py:687
  20.2 2.3 %collective-permute-start.11 = (bf16[1040,128]{1,0:T(8,128)(2,1)}, bf16[1040,128]{1,0:T(8,128)(2,1)S(1)}, u32[]{:S(2)}, u32[]{:S(2)}) collective-permute-start(bf16[1040,128]{1,0:T(8,128)(2,1)} %get-tuple-element.53), channel_id=1, source_target_pairs={{1,4},{4,1},{5,8},{8,5},{9,12},{12,9},{3,6},{6,3},{7,10},{10,7},{1... | collective-permute-start | bytes 798728 | tf_op jit(solution)/shard_map/ppermute | solution.py:687
  22.5 12.7 %collective-permute-done.9.refs_4_ = bf16[1040,128]{1,0:T(8,128)(2,1)S(1)} collective-permute-done((bf16[1040,128]{1,0:T(8,128)(2,1)}, bf16[1040,128]{1,0:T(8,128)(2,1)S(1)}, u32[]{:S(2)}, u32[]{:S(2)}) %collective-permute-start.9) | collective-permute-done | bytes 266272 | tf_op jit(solution)/shard_map/ppermute | solution.py:687
  35.2 1.9 %collective-permute-start.1 = (bf16[1040,128]{1,0:T(8,128)(2,1)}, bf16[1040,128]{1,0:T(8,128)(2,1)S(1)}, u32[]{:S(2)}, u32[]{:S(2)}) collective-permute-start(bf16[1040,128]{1,0:T(8,128)(2,1)} %get-tuple-element.42.refs_1_.x1), channel_id=1, source_target_pairs={{0,4},{4,8},{5,1},{8,12},{9,5},{13,9},{2,6},{6,10},{7,3},{10,14},{... | collective-permute-start | bytes 798728 | tf_op jit(solution)/shard_map/ppermute | solution.py:687
  37.1 3.7 %collective-permute-start.2 = (bf16[1040,128]{1,0:T(8,128)(2,1)}, bf16[1040,128]{1,0:T(8,128)(2,1)S(1)}, u32[]{:S(2)}, u32[]{:S(2)}) collective-permute-start(bf16[1040,128]{1,0:T(8,128)(2,1)} %get-tuple-element.43.refs_2_.x2), channel_id=1, source_target_pairs={{1,5},{4,0},{5,9},{8,4},{9,13},{12,8},{3,7},{6,2},{7,11},{10,6},{1... | collective-permute-start | bytes 798728 | tf_op jit(solution)/shard_map/ppermute | solution.py:687
  40.8 2.8 %collective-permute-start.3 = (bf16[1040,128]{1,0:T(8,128)(2,1)}, bf16[1040,128]{1,0:T(8,128)(2,1)S(1)}, u32[]{:S(2)}, u32[]{:S(2)}) collective-permute-start(bf16[1040,128]{1,0:T(8,128)(2,1)} %get-tuple-element.44), channel_id=1, source_target_pairs={{0,5},{4,9},{5,0},{8,13},{9,4},{13,8},{2,7},{6,11},{7,2},{10,15},{... | collective-permute-start | bytes 798728 | tf_op jit(solution)/shard_map/ppermute | solution.py:687
  43.7 2.7 %collective-permute-start.4 = (bf16[1040,128]{1,0:T(8,128)(2,1)}, bf16[1040,128]{1,0:T(8,128)(2,1)S(1)}, u32[]{:S(2)}, u32[]{:S(2)}) collective-permute-start(bf16[1040,128]{1,0:T(8,128)(2,1)} %get-tuple-element.45), channel_id=1, source_target_pairs={{1,4},{4,1},{5,8},{8,5},{9,12},{12,9},{3,6},{6,3},{7,10},{10,7},{1... | collective-permute-start | bytes 798728 | tf_op jit(solution)/shard_map/ppermute | solution.py:687
  48.3 5.7 %forward.3 = (bf16[2,2,256,128]{3,2,1,0:T(8,128)(2,1)S(1)}, bf16[2,2,256,128]{3,2,1,0:T(8,128)(2,1)S(1)}, bf16[2,512,128]{2,1,0:T(8,128)(2,1)S(1)}, bf16[304,128]{1,0:T(8,128)(2,1)S(1)}) custom-call(s32[1]{0:T(128)} %bitcast.core_ref, s32[8]{0:T(128)S(1)} %copy-done.4, bf16[4112,128]{1,0:T(8,128)(2,1)S(1)} %collective-permute-done.refs_0_.pair, ...), custom_call_target="tpu_custom_call" | custom-call | flops 6899999744 | bytes 6000000 | tf_op jit(solution)/shard_map/forward/pallas_call | solution.py:416
  53.9 3.7 %collective-permute-start.16 = (bf16[304,128]{1,0:T(8,128)(2,1)S(1)}, bf16[304,128]{1,0:T(8,128)(2,1)S(1)}, u32[]{:S(2)}, u32[]{:S(2)}) collective-permute-start(bf16[304,128]{1,0:T(8,128)(2,1)S(1)} %get-tuple-element.64.message), channel_id=1, source_target_pairs={{4,0},{5,1},{8,4},{9,5},{12,8},{13,9},{6,2},{7,3},{10,6},{11,7},{1... | collective-permute-start | bytes 233480 | tf_op jit(solution)/shard_map/ppermute | solution.py:687
  57.6 1.3 %collective-permute-start.17 = (bf16[304,128]{1,0:T(8,128)(2,1)S(1)}, bf16[304,128]{1,0:T(8,128)(2,1)S(1)}, u32[]{:S(2)}, u32[]{:S(2)}) collective-permute-start(bf16[304,128]{1,0:T(8,128)(2,1)S(1)} %get-tuple-element.64.message), channel_id=1, source_target_pairs={{8,0},{9,1},{12,4},{13,5},{10,2},{11,3},{14,6},{15,7},{24,16},{25,... | collective-permute-start | bytes 233480 | tf_op jit(solution)/shard_map/ppermute | solution.py:687
  59.0 5.8 %forward.2 = (bf16[2,2,256,128]{3,2,1,0:T(8,128)(2,1)S(1)}, bf16[2,2,256,128]{3,2,1,0:T(8,128)(2,1)S(1)}, bf16[2,512,128]{2,1,0:T(8,128)(2,1)S(1)}, bf16[304,128]{1,0:T(8,128)(2,1)S(1)}) custom-call(s32[1]{0:T(128)} %bitcast.core_ref, s32[8]{0:T(128)S(1)} %copy-done.4, bf16[4112,128]{1,0:T(8,128)(2,1)S(1)} %collective-permute-done.refs_0_.pair, ...), custom_call_target="tpu_custom_call" | custom-call | flops 6899999744 | bytes 6000000 | tf_op jit(solution)/shard_map/forward/pallas_call | solution.py:416
  64.8 1.9 %collective-permute-start.13 = (bf16[304,128]{1,0:T(8,128)(2,1)S(1)}, bf16[304,128]{1,0:T(8,128)(2,1)S(1)}, u32[]{:S(2)}, u32[]{:S(2)}) collective-permute-start(bf16[304,128]{1,0:T(8,128)(2,1)S(1)} %get-tuple-element.58.message), channel_id=1, source_target_pairs={{4,0},{5,1},{8,4},{9,5},{12,8},{13,9},{6,2},{7,3},{10,6},{11,7},{1... | collective-permute-start | bytes 233480 | tf_op jit(solution)/shard_map/ppermute | solution.py:687
  66.7 1.3 %collective-permute-start.14 = (bf16[304,128]{1,0:T(8,128)(2,1)S(1)}, bf16[304,128]{1,0:T(8,128)(2,1)S(1)}, u32[]{:S(2)}, u32[]{:S(2)}) collective-permute-start(bf16[304,128]{1,0:T(8,128)(2,1)S(1)} %get-tuple-element.58.message), channel_id=1, source_target_pairs={{8,0},{9,1},{12,4},{13,5},{10,2},{11,3},{14,6},{15,7},{24,16},{25,... | collective-permute-start | bytes 233480 | tf_op jit(solution)/shard_map/ppermute | solution.py:687
  68.0 2.9 %own_keys.3 = (f32[2,512,128]{2,1,0:T(8,128)S(1)}, f32[2,512,128]{2,1,0:T(8,128)S(1)}) custom-call(s32[1]{0:T(128)} %bitcast.core_ref, s32[8]{0:T(128)S(1)} %copy-done.4, bf16[4112,128]{1,0:T(8,128)(2,1)S(1)} %collective-permute-done.refs_0_.pair, bf16[1040,128]{1,0:T(8,128)(2,1)S(1)} %copy-done.2, bf16[1040,128]{1,0:T(8,128)(2,1)S(1)} %copy-done.3, ...), custom_call_target="tpu_custom_call" | custom-call | flops 3449999872 | bytes 3000000 | tf_op jit(solution)/shard_map/own_keys/pallas_call | solution.py:511
  71.0 2.9 %own_keys.2 = (f32[2,512,128]{2,1,0:T(8,128)S(1)}, f32[2,512,128]{2,1,0:T(8,128)S(1)}) custom-call(s32[1]{0:T(128)} %bitcast.core_ref, s32[8]{0:T(128)S(1)} %copy-done.4, bf16[4112,128]{1,0:T(8,128)(2,1)S(1)} %collective-permute-done.refs_0_.pair, bf16[1040,128]{1,0:T(8,128)(2,1)S(1)} %copy-done, bf16[1040,128]{1,0:T(8,128)(2,1)S(1)} %copy-done.1, ...), custom_call_target="tpu_custom_call" | custom-call | flops 3449999872 | bytes 3000000 | tf_op jit(solution)/shard_map/own_keys/pallas_call | solution.py:511
  74.5 3.0 %later_keys.3 = (bf16[2,2,256,128]{3,2,1,0:T(8,128)(2,1)S(1)}, bf16[2,2,256,128]{3,2,1,0:T(8,128)(2,1)S(1)}) custom-call(s32[1]{0:T(128)} %bitcast.core_ref, s32[8]{0:T(128)S(1)} %copy-done.4, bf16[4112,128]{1,0:T(8,128)(2,1)S(1)} %collective-permute-done.refs_0_.pair, bf16[1040,128]{1,0:T(8,128)(2,1)S(1)} %copy-done.2, bf16[1040,128]{1,0:T(8,128)(2,1)S(1)} %copy-done.3, ...), custom_call_target="tpu_custom_call" | custom-call | flops 3449999872 | bytes 3000000 | tf_op jit(solution)/shard_map/later_keys/pallas_call | solution.py:618
  77.6 2.8 %later_keys.2 = (bf16[2,2,256,128]{3,2,1,0:T(8,128)(2,1)S(1)}, bf16[2,2,256,128]{3,2,1,0:T(8,128)(2,1)S(1)}) custom-call(s32[1]{0:T(128)} %bitcast.core_ref, s32[8]{0:T(128)S(1)} %copy-done.4, bf16[4112,128]{1,0:T(8,128)(2,1)S(1)} %collective-permute-done.refs_0_.pair, bf16[1040,128]{1,0:T(8,128)(2,1)S(1)} %copy-done, bf16[1040,128]{1,0:T(8,128)(2,1)S(1)} %copy-done.1, ...), custom_call_target="tpu_custom_call" | custom-call | flops 3449999872 | bytes 3000000 | tf_op jit(solution)/shard_map/later_keys/pallas_call | solution.py:618
  81.0 1.3 %unpack.2 = (bf16[256,8,128]{2,1,0:T(8,128)(2,1)}, bf16[256,8,128]{2,1,0:T(8,128)(2,1)}) custom-call(s32[1]{0:T(128)} %bitcast.core_ref, bf16[2,2,256,128]{3,2,1,0:T(8,128)(2,1)S(1)} %get-tuple-element.48.refs_0_, bf16[2,2,256,128]{3,2,1,0:T(8,128)(2,1)S(1)} %collective-permute-done.7.refs_1_, bf16[2,2,256,128]{3,2,1,0:T(8,128)(2,1)S(1)} %get-tuple-element.54.refs_2_, ...), custom_call_target="tpu_custom_call" | custom-call | flops 1610000000 | bytes 1400000 | tf_op jit(solution)/shard_map/unpack/pallas_call | solution.py:643
  82.3 1.3 %unpack.3 = (bf16[256,8,128]{2,1,0:T(8,128)(2,1)}, bf16[256,8,128]{2,1,0:T(8,128)(2,1)}) custom-call(s32[1]{0:T(128)} %bitcast.core_ref, bf16[2,2,256,128]{3,2,1,0:T(8,128)(2,1)S(1)} %get-tuple-element.62.refs_0_, bf16[2,2,256,128]{3,2,1,0:T(8,128)(2,1)S(1)} %collective-permute-done.15.refs_1_, bf16[2,2,256,128]{3,2,1,0:T(8,128)(2,1)S(1)} %get-tuple-element.68.refs_2_, ...), custom_call_target="tpu_custom_call" | custom-call | flops 1610000000 | bytes 1400000 | tf_op jit(solution)/shard_map/unpack/pallas_call | solution.py:643
  (33 shorter events, 4.5 us)
Async XLA Ops:
  0.6 45.7 %copy-start.4 = (s32[8]{0:T(128)S(1)}, s32[8]{0:T(128)}, u32[]{:S(2)}) copy-start(s32[8]{0:T(128)} %win_ref.11) | copy-start | bytes 100
  5.7 3.2 %collective-permute-start = (bf16[4112,128]{1,0:T(8,128)(2,1)}, bf16[4112,128]{1,0:T(8,128)(2,1)S(1)}, u32[]{:S(2)}, u32[]{:S(2)}) collective-permute-start(bf16[4112,128]{1,0:T(8,128)(2,1)} %get-tuple-element.40), channel_id=1, source_target_pairs={{0,1},{1,0},{4,5},{5,4},{8,9},{9,8},{12,13},{13,12},{2,3},{3,2},{6... | collective-permute-start | bytes 3158024 | tf_op jit(solution)/shard_map/ppermute | solution.py:687
  6.4 13.8 %collective-permute-start.8 = (bf16[1040,128]{1,0:T(8,128)(2,1)}, bf16[1040,128]{1,0:T(8,128)(2,1)S(1)}, u32[]{:S(2)}, u32[]{:S(2)}) collective-permute-start(bf16[1040,128]{1,0:T(8,128)(2,1)} %get-tuple-element.50.refs_1_.x1), channel_id=1, source_target_pairs={{0,4},{4,8},{5,1},{8,12},{9,5},{13,9},{2,6},{6,10},{7,3},{10,14},{... | collective-permute-start | bytes 798728 | tf_op jit(solution)/shard_map/ppermute | solution.py:687
  8.9 34.7 %collective-permute-start.5 = (bf16[1424,128]{1,0:T(8,128)(2,1)}, bf16[1424,128]{1,0:T(8,128)(2,1)S(1)}, u32[]{:S(2)}, u32[]{:S(2)}) collective-permute-start(bf16[1424,128]{1,0:T(8,128)(2,1)} %get-tuple-element.46), channel_id=1, source_target_pairs={{1,9},{5,13},{8,0},{12,4},{3,11},{7,15},{10,2},{14,6},{17,25},{21,... | collective-permute-start | bytes 1093640 | tf_op jit(solution)/shard_map/ppermute | solution.py:687
  13.1 33.2 %collective-permute-start.6 = (bf16[1424,128]{1,0:T(8,128)(2,1)}, bf16[1424,128]{1,0:T(8,128)(2,1)S(1)}, u32[]{:S(2)}, u32[]{:S(2)}) collective-permute-start(bf16[1424,128]{1,0:T(8,128)(2,1)} %get-tuple-element.47), channel_id=1, source_target_pairs={{1,8},{5,12},{8,1},{12,5},{3,10},{7,14},{10,3},{14,7},{17,24},{21,... | collective-permute-start | bytes 1093640 | tf_op jit(solution)/shard_map/ppermute | solution.py:687
  16.3 18.9 %collective-permute-start.9 = (bf16[1040,128]{1,0:T(8,128)(2,1)}, bf16[1040,128]{1,0:T(8,128)(2,1)S(1)}, u32[]{:S(2)}, u32[]{:S(2)}) collective-permute-start(bf16[1040,128]{1,0:T(8,128)(2,1)} %get-tuple-element.51.refs_2_.x2), channel_id=1, source_target_pairs={{1,5},{4,0},{5,9},{8,4},{9,13},{12,8},{3,7},{6,2},{7,11},{10,6},{1... | collective-permute-start | bytes 798728 | tf_op jit(solution)/shard_map/ppermute | solution.py:687
  18.2 18.9 %collective-permute-start.10 = (bf16[1040,128]{1,0:T(8,128)(2,1)}, bf16[1040,128]{1,0:T(8,128)(2,1)S(1)}, u32[]{:S(2)}, u32[]{:S(2)}) collective-permute-start(bf16[1040,128]{1,0:T(8,128)(2,1)} %get-tuple-element.52), channel_id=1, source_target_pairs={{0,5},{4,9},{5,0},{8,13},{9,4},{13,8},{2,7},{6,11},{7,2},{10,15},{... | collective-permute-start | bytes 798728 | tf_op jit(solution)/shard_map/ppermute | solution.py:687
  20.2 20.7 %collective-permute-start.11 = (bf16[1040,128]{1,0:T(8,128)(2,1)}, bf16[1040,128]{1,0:T(8,128)(2,1)S(1)}, u32[]{:S(2)}, u32[]{:S(2)}) collective-permute-start(bf16[1040,128]{1,0:T(8,128)(2,1)} %get-tuple-element.53), channel_id=1, source_target_pairs={{1,4},{4,1},{5,8},{8,5},{9,12},{12,9},{3,6},{6,3},{7,10},{10,7},{1... | collective-permute-start | bytes 798728 | tf_op jit(solution)/shard_map/ppermute | solution.py:687
  35.2 22.4 %collective-permute-start.1 = (bf16[1040,128]{1,0:T(8,128)(2,1)}, bf16[1040,128]{1,0:T(8,128)(2,1)S(1)}, u32[]{:S(2)}, u32[]{:S(2)}) collective-permute-start(bf16[1040,128]{1,0:T(8,128)(2,1)} %get-tuple-element.42.refs_1_.x1), channel_id=1, source_target_pairs={{0,4},{4,8},{5,1},{8,12},{9,5},{13,9},{2,6},{6,10},{7,3},{10,14},{... | collective-permute-start | bytes 798728 | tf_op jit(solution)/shard_map/ppermute | solution.py:687
  37.1 21.8 %collective-permute-start.2 = (bf16[1040,128]{1,0:T(8,128)(2,1)}, bf16[1040,128]{1,0:T(8,128)(2,1)S(1)}, u32[]{:S(2)}, u32[]{:S(2)}) collective-permute-start(bf16[1040,128]{1,0:T(8,128)(2,1)} %get-tuple-element.43.refs_2_.x2), channel_id=1, source_target_pairs={{1,5},{4,0},{5,9},{8,4},{9,13},{12,8},{3,7},{6,2},{7,11},{10,6},{1... | collective-permute-start | bytes 798728 | tf_op jit(solution)/shard_map/ppermute | solution.py:687
  40.8 18.1 %collective-permute-start.3 = (bf16[1040,128]{1,0:T(8,128)(2,1)}, bf16[1040,128]{1,0:T(8,128)(2,1)S(1)}, u32[]{:S(2)}, u32[]{:S(2)}) collective-permute-start(bf16[1040,128]{1,0:T(8,128)(2,1)} %get-tuple-element.44), channel_id=1, source_target_pairs={{0,5},{4,9},{5,0},{8,13},{9,4},{13,8},{2,7},{6,11},{7,2},{10,15},{... | collective-permute-start | bytes 798728 | tf_op jit(solution)/shard_map/ppermute | solution.py:687
  43.7 15.3 %copy-start = (bf16[1040,128]{1,0:T(8,128)(2,1)S(1)}, bf16[1040,128]{1,0:T(8,128)(2,1)}, u32[]{:S(2)}) copy-start(bf16[1040,128]{1,0:T(8,128)(2,1)} %get-tuple-element.42.refs_1_.x1) | copy-start | bytes 798724
  43.7 15.3 %copy-start.1 = (bf16[1040,128]{1,0:T(8,128)(2,1)S(1)}, bf16[1040,128]{1,0:T(8,128)(2,1)}, u32[]{:S(2)}) copy-start(bf16[1040,128]{1,0:T(8,128)(2,1)} %get-tuple-element.43.refs_2_.x2) | copy-start | bytes 798724
  43.7 15.3 %collective-permute-start.4 = (bf16[1040,128]{1,0:T(8,128)(2,1)}, bf16[1040,128]{1,0:T(8,128)(2,1)S(1)}, u32[]{:S(2)}, u32[]{:S(2)}) collective-permute-start(bf16[1040,128]{1,0:T(8,128)(2,1)} %get-tuple-element.45), channel_id=1, source_target_pairs={{1,4},{4,1},{5,8},{8,5},{9,12},{12,9},{3,6},{6,3},{7,10},{10,7},{1... | collective-permute-start | bytes 798728 | tf_op jit(solution)/shard_map/ppermute | solution.py:687
  46.4 1.0 %copy-start.2 = (bf16[1040,128]{1,0:T(8,128)(2,1)S(1)}, bf16[1040,128]{1,0:T(8,128)(2,1)}, u32[]{:S(2)}) copy-start(bf16[1040,128]{1,0:T(8,128)(2,1)} %get-tuple-element.50.refs_1_.x1) | copy-start | bytes 798724
  47.3 1.0 %copy-start.3 = (bf16[1040,128]{1,0:T(8,128)(2,1)S(1)}, bf16[1040,128]{1,0:T(8,128)(2,1)}, u32[]{:S(2)}) copy-start(bf16[1040,128]{1,0:T(8,128)(2,1)} %get-tuple-element.51.refs_2_.x2) | copy-start | bytes 798724
  53.9 20.0 %collective-permute-start.16 = (bf16[304,128]{1,0:T(8,128)(2,1)S(1)}, bf16[304,128]{1,0:T(8,128)(2,1)S(1)}, u32[]{:S(2)}, u32[]{:S(2)}) collective-permute-start(bf16[304,128]{1,0:T(8,128)(2,1)S(1)} %get-tuple-element.64.message), channel_id=1, source_target_pairs={{4,0},{5,1},{8,4},{9,5},{12,8},{13,9},{6,2},{7,3},{10,6},{11,7},{1... | collective-permute-start | bytes 233480 | tf_op jit(solution)/shard_map/ppermute | solution.py:687
  57.6 16.8 %collective-permute-start.17 = (bf16[304,128]{1,0:T(8,128)(2,1)S(1)}, bf16[304,128]{1,0:T(8,128)(2,1)S(1)}, u32[]{:S(2)}, u32[]{:S(2)}) collective-permute-start(bf16[304,128]{1,0:T(8,128)(2,1)S(1)} %get-tuple-element.64.message), channel_id=1, source_target_pairs={{8,0},{9,1},{12,4},{13,5},{10,2},{11,3},{14,6},{15,7},{24,16},{25,... | collective-permute-start | bytes 233480 | tf_op jit(solution)/shard_map/ppermute | solution.py:687
  64.8 12.8 %collective-permute-start.13 = (bf16[304,128]{1,0:T(8,128)(2,1)S(1)}, bf16[304,128]{1,0:T(8,128)(2,1)S(1)}, u32[]{:S(2)}, u32[]{:S(2)}) collective-permute-start(bf16[304,128]{1,0:T(8,128)(2,1)S(1)} %get-tuple-element.58.message), channel_id=1, source_target_pairs={{4,0},{5,1},{8,4},{9,5},{12,8},{13,9},{6,2},{7,3},{10,6},{11,7},{1... | collective-permute-start | bytes 233480 | tf_op jit(solution)/shard_map/ppermute | solution.py:687
  66.7 10.9 %collective-permute-start.14 = (bf16[304,128]{1,0:T(8,128)(2,1)S(1)}, bf16[304,128]{1,0:T(8,128)(2,1)S(1)}, u32[]{:S(2)}, u32[]{:S(2)}) collective-permute-start(bf16[304,128]{1,0:T(8,128)(2,1)S(1)} %get-tuple-element.58.message), channel_id=1, source_target_pairs={{8,0},{9,1},{12,4},{13,5},{10,2},{11,3},{14,6},{15,7},{24,16},{25,... | collective-permute-start | bytes 233480 | tf_op jit(solution)/shard_map/ppermute | solution.py:687
  73.9 7.1 %collective-permute-start.12 = (bf16[2,2,256,128]{3,2,1,0:T(8,128)(2,1)S(1)}, bf16[2,2,256,128]{3,2,1,0:T(8,128)(2,1)S(1)}, u32[]{:S(2)}, u32[]{:S(2)}) collective-permute-start(bf16[2,2,256,128]{3,2,1,0:T(8,128)(2,1)S(1)} %get-tuple-element.55), channel_id=1, source_target_pairs={{0,1},{1,0},{4,5},{5,4},{8,9},{9,8},{12,13},{13,12},{2,3},{3,2},{6... | collective-permute-start | bytes 786440 | tf_op jit(solution)/shard_map/ppermute | solution.py:687
  74.0 7.0 %collective-permute-start.7 = (bf16[2,2,256,128]{3,2,1,0:T(8,128)(2,1)S(1)}, bf16[2,2,256,128]{3,2,1,0:T(8,128)(2,1)S(1)}, u32[]{:S(2)}, u32[]{:S(2)}) collective-permute-start(bf16[2,2,256,128]{3,2,1,0:T(8,128)(2,1)S(1)} %get-tuple-element.49), channel_id=1, source_target_pairs={{0,1},{1,0},{4,5},{5,4},{8,9},{9,8},{12,13},{13,12},{2,3},{3,2},{6... | collective-permute-start | bytes 786440 | tf_op jit(solution)/shard_map/ppermute | solution.py:687
  77.5 4.9 %collective-permute-start.18 = (bf16[2,2,256,128]{3,2,1,0:T(8,128)(2,1)S(1)}, bf16[2,2,256,128]{3,2,1,0:T(8,128)(2,1)S(1)}, u32[]{:S(2)}, u32[]{:S(2)}) collective-permute-start(bf16[2,2,256,128]{3,2,1,0:T(8,128)(2,1)S(1)} %get-tuple-element.69), channel_id=1, source_target_pairs={{0,1},{1,0},{4,5},{5,4},{8,9},{9,8},{12,13},{13,12},{2,3},{3,2},{6... | collective-permute-start | bytes 786440 | tf_op jit(solution)/shard_map/ppermute | solution.py:687
  80.5 1.9 %collective-permute-start.15 = (bf16[2,2,256,128]{3,2,1,0:T(8,128)(2,1)S(1)}, bf16[2,2,256,128]{3,2,1,0:T(8,128)(2,1)S(1)}, u32[]{:S(2)}, u32[]{:S(2)}) collective-permute-start(bf16[2,2,256,128]{3,2,1,0:T(8,128)(2,1)S(1)} %get-tuple-element.63), channel_id=1, source_target_pairs={{0,1},{1,0},{4,5},{5,4},{8,9},{9,8},{12,13},{13,12},{2,3},{3,2},{6... | collective-permute-start | bytes 786440 | tf_op jit(solution)/shard_map/ppermute | solution.py:687

commit v3 on v2

v3 whole, which is shorter than its diff:
```python
import functools
import math

import jax
import jax.numpy as jnp
from jax import lax
from jax.experimental import pallas as pl
from jax.experimental.pallas import tpu as pltpu
from jax.sharding import PartitionSpec as P

WIN = 1024
SESSIONS = 6
EPSILON = 1e-06
MASKED = -1e30
AXES = ("ctx", "pair")
EXTRA = 16
LANES = 128
VMEM_LIMIT = 20 << 20

f32 = jnp.float32
bf16 = jnp.bfloat16


def dot(a, b):
    return lax.dot_general(a, b, (((1,), (0,)), ((), ())), preferred_element_type=f32)


def dot_t(a, b):
    return lax.dot_general(a, b, (((1,), (1,)), ((), ())), preferred_element_type=f32)


def t_dot(a, b):
    return lax.dot_general(a, b, (((0,), (0,)), ((), ())), preferred_element_type=f32)


def feature(x):
    return jnp.where(x > 0, x + 1.0, jnp.exp(jnp.minimum(x, 0.0)))


def slope(x):
    return jnp.where(x > 0, 1.0, jnp.exp(jnp.minimum(x, 0.0)))


def params(micros):
    return dict(
        compiler_params=pltpu.CompilerParams(vmem_limit_bytes=VMEM_LIMIT),
        cost_estimate=pl.CostEstimate(
            flops=int(micros * 1.15e9), bytes_accessed=int(micros * 1e6), transcendentals=0
        ),
    )


def row_of(column):
    n = column.shape[0]
    return jnp.concatenate(
        [
            jnp.transpose(jnp.broadcast_to(column[i : i + LANES], (LANES, LANES)))[0:1]
            for i in range(0, n, LANES)
        ],
        axis=1,
    )


def column_of(rows):
    return jnp.concatenate(
        [
            jnp.transpose(jnp.broadcast_to(rows[i : i + 1], (LANES, LANES)))[:, 0:1]
            for i in range(rows.shape[0])
        ],
        axis=0,
    )


class Plan:
    def __init__(self, length, heads, width, total):
        self.length = length
        self.heads = heads
        self.all = heads // 2
        self.width = width
        self.chip = 2 * length
        longest = total // 3
        reach = min(WIN, longest) - 1
        tail = max(reach - self.chip, 0)
        self.far = longest - 1 > 2 * self.chip or longest - 1 > reach
        self.merged = tail <= length
        self.tail = -(-tail // 16) * 16 if self.merged else length
        self.tail_fill = length if self.merged else self.chip
        self.before = self.tail_fill + self.chip
        self.code_rows = length // LANES
        self.rows = self.all * 2 * length + EXTRA
        self.tail_rows = self.all * 2 * self.tail + EXTRA
        self.pair_rows = self.all * 4 * length + EXTRA
        self.stat_rows = -(-2 * self.all * self.code_rows // 16) * 16
        self.state_rows = self.all * width
        self.far_refs = 2 if self.merged else 4


def pack_body(p, core_ref, q_ref, k_ref, v_ref, t_ref, w_ref, s_ref, *rest):
    number = (len(rest) - 4) // 2
    outs, staged = list(rest[:number]), list(rest[number : 2 * number])
    scratch, landed, sems, out_sems = rest[2 * number :]
    core = core_ref[0]
    L = p.length
    copies = [
        pltpu.make_async_copy(ref, landed.at[n], sems.at[n])
        for n, ref in enumerate((k_ref, v_ref, q_ref, t_ref))
    ]
    for copy_in in copies:
        copy_in.start()
    weight = column_of(w_ref[...].astype(f32))
    codes = jnp.concatenate(
        [s_ref[...].astype(f32) + 1.0, jnp.zeros((EXTRA - p.code_rows, LANES), f32)], axis=0
    ).astype(bf16)
    for ref in staged:
        ref[ref.shape[0] - EXTRA :, :] = codes
    leaving = []

    def leave():
        copy_out = pltpu.make_async_copy(staged.pop(0), outs.pop(0), out_sems.at[len(leaving)])
        copy_out.start()
        leaving.append(copy_out)

    other = (1 - core) * p.all
    for n in range(4):
        copies[n].wait()
        x = jnp.swapaxes(landed[n].astype(f32), 0, 1)
        if n == 3:
            x = x * weight[None]
        scratch[n] = x.astype(bf16)
    for n in range(4):
        for h in range(p.all):
            at = (n * p.all + h) * L
            staged[0][at : at + L, :] = scratch[n, other + h]
    leave()
    for first, base in (
        (core * 2, core * p.all),
        ((1 - core) * 2, core * p.all),
        (core * 2, other),
        ((1 - core) * 2, other),
    ):
        for n in range(2):
            for h in range(p.all):
                at = (n * p.all + h) * L
                staged[0][at : at + L, :] = scratch[first + n, base + h]
        leave()
    if p.merged:
        first = (1 - core) * 2
        lead = core * (L - p.tail)
        for base in (core * p.all, other):
            for n in range(2):
                for h in range(p.all):
                    at = (n * p.all + h) * p.tail
                    staged[0][at : at + p.tail, :] = scratch[
                        first + n, base + h, pl.ds(pl.multiple_of(lead, 16), p.tail), :
                    ]
            leave()
    for copy_out in leaving:
        copy_out.wait()


def pack(p, core, q, k, v, targets, weights, sessions):
    rows = [p.pair_rows] + [p.rows] * 4 + [p.tail_rows] * (2 if p.merged else 0)
    shapes = [(n, p.width) for n in rows]
    vmem = pl.BlockSpec(memory_space=pltpu.VMEM)
    hbm = pl.BlockSpec(memory_space=pl.ANY)
    return pl.pallas_call(
        functools.partial(pack_body, p),
        out_shape=[jax.ShapeDtypeStruct(x, bf16) for x in shapes],
        in_specs=[pl.BlockSpec(memory_space=pltpu.SMEM)] + [hbm] * 4 + [vmem] * 2,
        out_specs=[hbm] * len(shapes),
        scratch_shapes=[pltpu.VMEM(x, bf16) for x in shapes]
        + [
            pltpu.VMEM((4, p.heads, p.length, p.width), bf16),
            pltpu.VMEM((4, p.length, p.heads, p.width), bf16),
            pltpu.SemaphoreType.DMA((4,)),
            pltpu.SemaphoreType.DMA((len(shapes),)),
        ],
        compiler_params=pltpu.CompilerParams(vmem_limit_bytes=56 << 20),
        name="pack",
    )(core, q, k, v, targets, weights, sessions)


def code_block(p, core, pick):
    one, two = (ref[ref.shape[0] - EXTRA :, :].astype(f32)[: p.code_rows] for ref in pick)
    return jnp.where(core == 0, one, two)


def count(condition):
    return jnp.sum(
        jnp.sum(jnp.where(condition, 1.0, 0.0), axis=1, keepdims=True), axis=0, keepdims=True
    )


def drive(streams):
    streams = list(streams)
    while streams:
        streams = [x for x in streams if next(x, streams) is not streams]


def flat(rows):
    return jnp.concatenate([rows[i : i + 1] for i in range(rows.shape[0])], axis=1)


def in_order(core, same, cross):
    first = jnp.where(core == 0, same, cross)
    second = jnp.where(core == 0, cross, same)
    return jnp.concatenate([first, second], axis=0)


class Chip:
    def __init__(self, p, core, same, cross, index=0):
        self.p, self.core, self.same, self.cross = p, core, same, cross
        self.index = index

    def codes(self):
        return in_order(
            self.core,
            code_block(self.p, self.core, self.same),
            code_block(self.p, self.core, self.cross),
        )

    def bring(self, targets, start, tile=None):
        p = self.p
        L = p.length
        for me in range(2):

            @pl.when(self.core == me)
            def _():
                for ref, which, first in (
                    (self.same[me], me, 0),
                    (self.cross[me], 1 - me, self.index),
                ):
                    if tile not in (None, which):
                        continue
                    to = start + (which * L if tile is None else 0)
                    for n, target in enumerate(targets):
                        for h in range(p.all):
                            at = ((first + n) * p.all + h) * L
                            target[h, to : to + L, :] = ref[at : at + L, :]


def own_chip(p, core, refs):
    pair, x1, x2 = refs[:3]
    keys = Chip(p, core, (x1, x2), (pair, pair), 0)
    return keys, Chip(p, core, (x2, x1), (pair, pair), 2)


def near_chips(p, core, refs):
    r1, r2, r3, r4 = refs[3:7]
    return Chip(p, core, (r1, r2), (r4, r3)), Chip(p, core, (r2, r1), (r3, r4))


def bring_tail(p, core, pick, targets, start):
    for me in range(2):

        @pl.when(core == me)
        def _():
            for n, target in enumerate(targets):
                for h in range(p.all):
                    at = (n * p.all + h) * p.tail
                    target[h, start : start + p.tail, :] = pick[me][at : at + p.tail, :]


def divide(core, tiles, keep, send):
    for me in range(2):

        @pl.when(core == me)
        def _():
            keep[...] = tiles[me][...]
            send[...] = tiles[1 - me][...]


def forward_body(p, r, core_ref, win_ref, *refs):
    near, refs = refs[:7], refs[7:]
    far_here = r == 0 or not p.merged
    if far_here:
        far, refs = refs[: p.far_refs], refs[p.far_refs :]
    if p.far:
        far_ref, refs = refs[0], refs[1:]
    if r == 0:
        (state_in, stats_in, second), refs = refs[:3], refs[3:]
        keep, send, gn_out, stats_out, message, ks, vs, qs, gs, stat, out = refs
    else:
        out, gn_out, stats_out, state_out, ks, vs, qs, gs, stat = refs
    core = core_ref[0]
    L, C, B, D = p.length, p.chip, p.before, p.width
    scale = 1.0 / math.sqrt(D)
    c2 = scale * math.log2(math.e)

    own_keys_at, own_queries_at = own_chip(p, core, near)
    near_at, _ = near_chips(p, core, near)
    own_keys_at.bring((ks, vs), B)
    own_queries_at.bring((qs, gs), 0, r)
    near_at.bring((ks, vs), p.tail_fill)
    own_codes = own_keys_at.codes()
    near_codes = near_at.codes()
    halo_codes = near_codes
    if far_here:
        if p.merged:
            pick = (far[1], far[0])
            bring_tail(p, core, pick, (ks, vs), p.tail_fill - p.tail)
            far_codes = code_block(p, core, pick)
            if p.tail < p.tail_fill:
                gap = p.tail_fill - p.tail
                ks[:, 0:gap, :] = jnp.zeros((p.all, gap, D), bf16)
                vs[:, 0:gap, :] = jnp.zeros((p.all, gap, D), bf16)
        else:
            far_at = Chip(p, core, (far[0], far[1]), (far[3], far[2]))
            far_at.bring((ks, vs), 0)
            far_codes = far_at.codes()
        halo_codes = jnp.concatenate([far_codes, near_codes], axis=0)
    begin = 0 if far_here else p.tail_fill
    if not far_here:
        begin = max(begin, r * L)
    n_halo = B - begin
    n_own = (r + 1) * L
    wide = n_halo + n_own
    mine = column_of(own_codes[r * p.code_rows : (r + 1) * p.code_rows])
    last = near_codes[2 * p.code_rows - 1 :, LANES - 1 :]
    first_own = own_codes[0:1, 0:1]
    lo = jnp.zeros((L, 1), f32)
    for n in range(1, SESSIONS + 1):
        start = count(own_codes < n) - count(halo_codes >= n)
        lo = jnp.where(mine == n, start, lo)
    lo = lo.astype(jnp.int32)
    cont = count(jnp.logical_and(halo_codes == last, halo_codes > 0)).astype(jnp.int32)
    halo_pos = lax.broadcasted_iota(jnp.int32, (n_halo, 1), 0) - n_halo
    in_start = jnp.broadcast_to(halo_pos >= -cont, (n_halo, D))
    t_pos = lax.broadcasted_iota(jnp.int32, (L, 1), 0) + r * L
    reads = mine == last
    opening = mine == first_own

    def stream(h):
        q = qs[h]
        g = gs[h]
        gf = g.astype(f32)
        qf = q.astype(f32)
        window = win_ref[core * p.all + h]
        low = jnp.maximum(lo, t_pos - window + 1)
        k_part = ks[h, begin : begin + wide, :]
        v_part = vs[h, begin : begin + wide, :]
        v_own = vs[h, B : B + n_own, :]
        score = dot_t(q, k_part)
        yield
        phi_k = feature(ks[h, B : B + n_own, :].astype(f32)).astype(bf16)
        if p.far:
            start_state = far_ref[h * D : (h + 1) * D, :]
        else:
            halo_phi = jnp.where(in_start, feature(ks[h, begin:B, :].astype(f32)), 0.0)
            start_state = t_dot(halo_phi.astype(bf16), vs[h, begin:B, :]).astype(bf16)
        phi_q = feature(qf).astype(bf16)
        a = dot_t(phi_q, phi_k)
        from_start = dot(phi_q, start_state)
        yield
        s_pos = lax.broadcasted_iota(jnp.int32, (L, n_halo), 1) - n_halo
        own_pos = lax.broadcasted_iota(jnp.int32, (L, n_own), 1)
        causal = own_pos <= t_pos
        score = jnp.concatenate(
            [
                jnp.where(s_pos >= low, score[:, :n_halo], MASKED),
                jnp.where(
                    jnp.logical_and(own_pos >= low, causal), score[:, n_halo:], MASKED
                ),
            ],
            axis=1,
        )
        peak = jnp.max(score, axis=1, keepdims=True) * c2
        e = jnp.exp2(score * c2 - peak)
        total = jnp.sum(e, axis=1, keepdims=True)
        yield
        inverse = 1.0 / total
        window_out = dot(e.astype(bf16), v_part) * inverse
        alike = jnp.logical_and(own_pos >= lo, causal)
        a = jnp.where(alike, a, 0.0).astype(bf16)
        numerator = dot(a, v_own) + jnp.where(reads, from_start, 0.0)
        grad_prob = dot_t(g, v_part)
        yield
        rowdot = jnp.sum(gf * window_out, axis=1, keepdims=True)
        inverse_rms = lax.rsqrt(jnp.mean(numerator * numerator, axis=1, keepdims=True) + EPSILON)
        linear_out = numerator * inverse_rms
        grad_num = (
            inverse_rms * (gf - linear_out * jnp.mean(gf * linear_out, axis=1, keepdims=True))
        ).astype(bf16)
        gn_out[h] = grad_num
        out[0, h] = (linear_out + window_out).astype(bf16)
        b = dot_t(grad_num, v_own)
        ds = (e * (grad_prob - rowdot)).astype(bf16)
        yield
        dq = dot(ds, k_part) * (inverse * scale)
        state = t_dot(jnp.where(opening, phi_q, jnp.zeros_like(phi_q)), grad_num)
        lse = peak + jnp.log2(total)
        for which, column in ((0, lse), (1, rowdot)):
            base = (which * p.all + h) * p.code_rows
            row = row_of(column)
            for j in range(p.code_rows):
                stat[base + j : base + j + 1, :] = row[:, j * LANES : (j + 1) * LANES]
        yield
        b = jnp.where(alike, b, 0.0).astype(bf16)
        grad_phi_q = dot(b, phi_k) + jnp.where(reads, dot_t(grad_num, start_state), 0.0)
        out[1, h] = (slope(qf) * grad_phi_q + dq).astype(bf16)
        here = slice(h * D, (h + 1) * D)
        if r == 0:
            message[here, :] = (state_in[here, :] + state).astype(bf16)
        else:
            state_out[here, :] = state

    drive(stream(h) for h in range(p.all))

    if r == 0:
        divide(core, (out, second), keep, send)
    values = stat[...]
    used = 2 * p.all * p.code_rows
    if used < p.stat_rows:
        inside = lax.broadcasted_iota(jnp.int32, values.shape, 0) < used
        values = jnp.where(inside, values, 0.0)
    stats_out[...] = values
    if r == 0:
        for tile, values in enumerate((values, stats_in[...])):
            for n in range(3):
                piece = values.astype(bf16)
                at = p.state_rows + (3 * tile + n) * p.stat_rows
                message[at : at + p.stat_rows, :] = piece
                values = values - piece.astype(f32)


def forward(p, r, core, windows, near, far, far_state, carried=()):
    vmem = pl.BlockSpec(memory_space=pltpu.VMEM)
    smem = pl.BlockSpec(memory_space=pltpu.SMEM)
    both = jax.ShapeDtypeStruct((2, p.all, p.length, p.width), bf16)
    outs = [both] * (2 - r)
    outs += [
        jax.ShapeDtypeStruct((p.all, p.length, p.width), bf16),
        jax.ShapeDtypeStruct((p.stat_rows, p.width), f32),
    ]
    if r == 0:
        outs.append(jax.ShapeDtypeStruct((p.state_rows + 6 * p.stat_rows, p.width), bf16))
    else:
        outs.append(jax.ShapeDtypeStruct((p.state_rows, p.width), f32))
    args = list(near)
    if r == 0 or not p.merged:
        args += far
    if p.far:
        args.append(far_state)
    args += carried
    span = pltpu.VMEM((p.all, p.before + p.chip, p.width), bf16)
    tile = pltpu.VMEM((p.all, p.length, p.width), bf16)
    return pl.pallas_call(
        functools.partial(forward_body, p, r),
        out_shape=outs,
        in_specs=[smem, smem] + [vmem] * len(args),
        out_specs=[vmem] * len(outs),
        scratch_shapes=[span, span, tile, tile, pltpu.VMEM((p.stat_rows, p.width), f32)]
        + ([pltpu.VMEM(both.shape, bf16)] if r == 0 else []),
        **params(5.7),
        name="forward",
    )(core, windows, *args)


def stats_of(p, values, head):
    result = []
    for which in range(2):
        base = (which * p.all + head) * p.code_rows
        result.append(flat(values[base : base + p.code_rows]))
    return result


def unpack_stats(p, message, tile):
    total = jnp.zeros((p.stat_rows, LANES), f32)
    for n in reversed(range(3)):
        at = p.state_rows + (3 * tile + n) * p.stat_rows
        total = total + message[at : at + p.stat_rows, :].astype(f32)
    return total


def own_body(p, r, core_ref, win_ref, *refs):
    near, (gn, stats_in), refs = refs[:3], refs[3:5], refs[5:]
    if r == 0:
        (dk_i, dv_i), refs = refs[:2], refs[2:]
    dk_o, dv_o, ks, vs, qs, gs = refs
    core = core_ref[0]
    L, C, D = p.length, p.chip, p.width
    scale = 1.0 / math.sqrt(D)
    c2 = scale * math.log2(math.e)
    own_keys_at, own_queries_at = own_chip(p, core, near)
    own_keys_at.bring((ks, vs), 0)
    own_queries_at.bring((qs, gs), 0, r)
    own_codes = own_keys_at.codes()
    code = column_of(own_codes)
    hi_all = jnp.zeros((C, 1), f32)
    for n in range(1, SESSIONS + 1):
        hi_all = jnp.where(code == n, count(own_codes <= n) - 1.0, hi_all)
    hi_all = hi_all.astype(jnp.int32)
    stats = stats_in[...]

    def stream(h, tile):
        window = win_ref[core * p.all + h]
        lse, rowdot = stats_of(p, stats, h)
        rows = slice(tile * L, (tile + 1) * L)
        k, v = ks[h, rows, :], vs[h, rows, :]
        q, g = qs[h], gs[h]
        score = dot_t(k, q)
        grad_prob = dot_t(v, g)
        yield
        phi_q = feature(q.astype(f32)).astype(bf16)
        kf = k.astype(f32)
        grad_num = gn[h]
        a = dot_t(feature(kf).astype(bf16), phi_q)
        b = dot_t(v, grad_num)
        yield
        hi = hi_all[rows]
        s_pos = lax.broadcasted_iota(jnp.int32, (L, 1), 0) + tile * L
        t_pos = lax.broadcasted_iota(jnp.int32, (L, L), 1) + r * L
        alike = t_pos <= hi
        if tile == r:
            alike = jnp.logical_and(alike, t_pos >= s_pos)
        allowed = jnp.logical_and(alike, t_pos < s_pos + window)
        prob = jnp.exp2(jnp.where(allowed, score * c2 - lse, MASKED))
        ds = (prob * (grad_prob - rowdot)).astype(bf16)
        yield
        dk = dot(ds, q) * scale
        dv = dot(prob.astype(bf16), g)
        a = jnp.where(alike, a, 0.0).astype(bf16)
        b = jnp.where(alike, b, 0.0).astype(bf16)
        yield
        dk = dk + slope(kf) * dot(b, phi_q)
        dv = dv + dot(a, grad_num)
        if r == 0:
            dk_o[h] = dk_i[h, rows, :] + dk
            dv_o[h] = dv_i[h, rows, :] + dv
        else:
            dk_o[h, rows, :] = dk
            dv_o[h, rows, :] = dv

    drive(stream(h, tile) for h in range(p.all) for tile in range(r + 1))


def own_keys(p, r, core, windows, near, gn, stats, carried=()):
    vmem = pl.BlockSpec(memory_space=pltpu.VMEM)
    smem = pl.BlockSpec(memory_space=pltpu.SMEM)
    full = jax.ShapeDtypeStruct((p.all, p.chip if r else p.length, p.width), f32)
    args = [*near[:3], gn, stats, *carried]
    keys = pltpu.VMEM((p.all, p.chip, p.width), bf16)
    tile = pltpu.VMEM((p.all, p.length, p.width), bf16)
    return pl.pallas_call(
        functools.partial(own_body, p, r),
        out_shape=[full, full],
        in_specs=[smem, smem] + [vmem] * len(args),
        out_specs=[vmem] * 2,
        scratch_shapes=[keys, keys, tile, tile],
        **params(4.0 if r else 2.0),
        name="own_keys",
    )(core, windows, *args)


def later_body(p, core_ref, win_ref, *refs):
    near, refs = refs[:7], refs[7:]
    far, refs = refs[: p.far_refs], refs[p.far_refs :]
    (message_1, message_2), sums, refs = refs[:2], (refs[2:4], refs[4:6]), refs[6:]
    if p.far:
        far_ref, refs = refs[0], refs[1:]
    keep, send, ks, vs, qs, gs, first, second = refs
    core = core_ref[0]
    L, C, D = p.length, p.chip, p.width
    N = p.tail_fill
    scale = 1.0 / math.sqrt(D)
    c2 = scale * math.log2(math.e)
    own_keys_at, _ = own_chip(p, core, near)
    _, near_at = near_chips(p, core, near)
    own_keys_at.bring((ks, vs), 0)
    near_at.bring((qs, gs), 0)
    own_codes = own_keys_at.codes()
    near_codes = near_at.codes()
    if p.merged:
        pick = (far[0], far[1])
        far_codes = code_block(p, core, pick)
        bring_tail(p, core, pick, (qs, gs), C)
        if p.tail < p.tail_fill:
            gap = p.tail_fill - p.tail
            qs[:, C + p.tail :, :] = jnp.zeros((p.all, gap, D), bf16)
            gs[:, C + p.tail :, :] = jnp.zeros((p.all, gap, D), bf16)
    else:
        far_at = Chip(p, core, (far[1], far[0]), (far[2], far[3]))
        far_at.bring((qs, gs), C)
        far_codes = far_at.codes()
    after_codes = jnp.concatenate([near_codes, far_codes], axis=0)
    code = column_of(own_codes)
    final = own_codes[2 * p.code_rows - 1 :, LANES - 1 :]
    hi_last = C - 1 + count(after_codes == final)
    hi = jnp.where(code == final, hi_last, -1.0).astype(jnp.int32)
    first_next = near_codes[0:1, 0:1]
    goes_on = jnp.logical_and(first_next > 0, first_next == far_codes[0:1, 0:1])
    tiles = [unpack_stats(p, message_1, 0), unpack_stats(p, message_1, 1)]
    tiles += [unpack_stats(p, message_2, n) for n in range(N // L)]

    def stream(h, r):
        far_here = r == 1 or not p.merged
        wide = C + N if far_here else C
        rows = slice(r * L, (r + 1) * L)
        uses = code[rows] == first_next
        dk_i, dv_i = sums[r]
        window = win_ref[core * p.all + h]
        lse, rowdot = (
            jnp.concatenate(x, axis=1) for x in zip(*(stats_of(p, tile, h) for tile in tiles[: wide // L]))
        )
        k, v = ks[h, rows, :], vs[h, rows, :]
        q, g = qs[h, 0:wide, :], gs[h, 0:wide, :]
        score = dot_t(k, q)
        grad_prob = dot_t(v, g)
        yield
        here = slice(h * D, (h + 1) * D)
        if p.far:
            later_state = far_ref[here, :]
        else:
            later_state = message_1[here, :]
            if far_here:
                later_state = (
                    later_state.astype(f32)
                    + jnp.where(goes_on, message_2[here, :].astype(f32), 0.0)
                ).astype(bf16)
        kf = k.astype(f32)
        phi_k = feature(kf).astype(bf16)
        dk_lin = dot_t(v, later_state)
        dv_lin = dot(phi_k, later_state)
        yield
        s_pos = lax.broadcasted_iota(jnp.int32, (L, 1), 0) + r * L
        t_pos = lax.broadcasted_iota(jnp.int32, (L, wide), 1) + C
        allowed = t_pos <= jnp.minimum(hi[rows], s_pos + window - 1)
        prob = jnp.exp2(jnp.where(allowed, score * c2 - lse, MASKED))
        ds = (prob * (grad_prob - rowdot)).astype(bf16)
        yield
        dk = dot(ds, q) * scale
        dv = dot(prob.astype(bf16), g)
        yield
        out = (first, second)[r]
        dk = dk_i[h, rows, :] + dk + slope(kf) * jnp.where(uses, dk_lin, 0.0)
        dv = dv_i[h, rows, :] + dv + jnp.where(uses, dv_lin, 0.0)
        out[0, h] = dk.astype(bf16)
        out[1, h] = dv.astype(bf16)

    drive(stream(h, r) for h in range(p.all) for r in range(2))
    divide(core, (first, second), keep, send)


def later_keys(p, core, windows, near, far, messages, sums, far_state):
    vmem = pl.BlockSpec(memory_space=pltpu.VMEM)
    smem = pl.BlockSpec(memory_space=pltpu.SMEM)
    args = [*near, *far, *messages, *sums] + ([far_state] if p.far else [])
    both = jax.ShapeDtypeStruct((2, p.all, p.length, p.width), bf16)
    keys = pltpu.VMEM((p.all, p.chip, p.width), bf16)
    tall = pltpu.VMEM((p.all, p.chip + p.tail_fill, p.width), bf16)
    return pl.pallas_call(
        functools.partial(later_body, p),
        out_shape=[both, both],
        in_specs=[smem, smem] + [vmem] * len(args),
        out_specs=[vmem, vmem],
        scratch_shapes=[keys, keys, tall, tall] + [pltpu.VMEM(both.shape, bf16)] * 2,
        **params(5.5),
        name="later_keys",
    )(core, windows, *args)


def unpack_body(p, core_ref, mine, theirs, out_a, out_b, scratch):
    core = core_ref[0]
    for n in range(2):
        for h in range(p.all):
            scratch[n, core * p.all + h] = mine[n, h].astype(f32)
            scratch[n, (1 - core) * p.all + h] = theirs[n, h].astype(f32)
    for n, out in ((0, out_a), (1, out_b)):
        out[...] = jnp.swapaxes(scratch[n], 0, 1).astype(bf16)


def unpack(p, core, mine, theirs):
    vmem = pl.BlockSpec(memory_space=pltpu.VMEM)
    out = jax.ShapeDtypeStruct((p.length, p.heads, p.width), bf16)
    return pl.pallas_call(
        functools.partial(unpack_body, p),
        out_shape=[out, out],
        in_specs=[pl.BlockSpec(memory_space=pltpu.SMEM)] + [vmem] * 2,
        out_specs=[vmem, vmem],
        scratch_shapes=[pltpu.VMEM((2, p.heads, p.length, p.width), f32)],
        **params(1.4),
        name="unpack",
    )(core, mine, theirs)


def folded(session, state, backward):
    sessions = lax.all_gather(session, "ctx")
    states = lax.all_gather(state, "ctx")
    count = lax.axis_size("ctx")
    here = lax.axis_index("ctx")

    def one(hop, carry):
        held, total = carry
        source = count - 1 - hop if backward else hop
        new = lax.dynamic_index_in_dim(sessions, source, 0, False)
        first, last = new[0], new[1]
        part = lax.dynamic_index_in_dim(states, source, 0, False).astype(f32)
        entering, leaving = (last, first) if backward else (first, last)
        whole = jnp.logical_and(entering == held, entering == leaving)
        return leaving, part + jnp.where(whole, total, 0.0)

    steps = count - 1 - here if backward else here
    start = (jnp.zeros((), jnp.int32) - 1, jnp.zeros(state.shape, f32))
    return lax.fori_loop(0, steps, one, start)[1].astype(bf16)


def shards(p, queries, key_vectors, value_vectors, targets, token_weights, sessions, window_size):
    L = p.length
    chips = lax.axis_size("ctx")
    core_id = lax.axis_index("pair").astype(jnp.int32)
    core = core_id.reshape(1)
    def move(x, target):
        pairs = []
        for c in range(chips):
            for i in range(2):
                to, j = target(c, i)
                if 0 <= to < chips:
                    pairs.append((2 * c + i, 2 * to + j))
        return lax.ppermute(x, AXES, pairs)

    packed = pack(
        p,
        core,
        queries,
        key_vectors,
        value_vectors,
        targets,
        token_weights.reshape(-1, LANES),
        sessions.reshape(-1, LANES),
    )
    for_pair, payloads, tails = packed[0], packed[1:5], packed[5:]

    def exchange(payloads, by):
        x1, x2, x3, x4 = payloads
        return (
            move(x1, lambda c, i: (c + by, 0) if i == 0 else (c - by, 1)),
            move(x2, lambda c, i: (c + by, 1) if i == 1 else (c - by, 0)),
            move(x3, lambda c, i: (c + by, 1) if i == 0 else (c - by, 0)),
            move(x4, lambda c, i: (c + by, 0) if i == 1 else (c - by, 1)),
        )

    pair = move(for_pair, lambda c, i: (c, 1 - i))
    got = exchange(payloads, 1)
    if p.merged:
        tail_1, r1 = lax.optimization_barrier((tails[0], got[0]))
        tail_2, r2 = lax.optimization_barrier((tails[1], got[1]))
        got = (r1, r2, *got[2:])
        far = (
            move(tail_1, lambda c, i: (c + 2, 1) if i == 1 else (c - 2, 0)),
            move(tail_2, lambda c, i: (c + 2, 0) if i == 1 else (c - 2, 1)),
        )
    else:
        far = exchange(payloads, 2)
    near = (pair, *payloads[:2], *got)

    far_before = far_after = None
    if p.far:
        both = lax.all_gather(sessions, "pair")
        chip_ends = jnp.stack([both[0, 0], both[1, -1]])

        total = jnp.zeros((p.all, p.width, p.width), f32)
        keys_here = jnp.where(core_id == 0, payloads[0], payloads[1])[: p.rows - EXTRA]
        keys_here = keys_here.reshape(2, p.all, L, p.width)
        keys_pair = pair[: p.pair_rows - EXTRA].reshape(4, p.all, L, p.width)[:2]
        for part, owner in ((keys_here, core_id), (keys_pair, 1 - core_id)):
            rows = lax.dynamic_index_in_dim(both, owner, 0, False)
            phi = feature(part[0].astype(f32))
            phi = jnp.where((rows == chip_ends[1])[None, :, None], phi, 0.0).astype(bf16)
            total = total + jnp.einsum(
                "hsk,hsd->hkd", phi, part[1], preferred_element_type=f32
            )
        far_before = folded(chip_ends, total.astype(bf16), False).reshape(-1, p.width)

    queries_1, grad_1, stats_1, state_1 = forward(p, 1, core, window_size, near, far, far_before)
    keep_q, send_q, grad_0, stats_0, message = forward(
        p, 0, core, window_size, near, far, far_before, (state_1, stats_1, queries_1)
    )
    messages = (
        move(message, lambda c, i: (c - 1, i)),
        move(message, lambda c, i: (c - 2, i)),
    )
    if p.far:
        state = message[: p.state_rows].reshape(p.all, p.width, p.width)
        far_after = folded(chip_ends, state, True).reshape(-1, p.width)
    sums_1 = own_keys(p, 1, core, window_size, near, grad_1, stats_1)
    sums_0 = own_keys(p, 0, core, window_size, near, grad_0, stats_0, sums_1)
    keep_k, send_k = later_keys(
        p, core, window_size, near, far, messages, (*sums_0, *sums_1), far_after
    )
    attended, grad_queries = unpack(p, core, keep_q, move(send_q, lambda c, i: (c, 1 - i)))
    grad_keys, grad_values = unpack(p, core, keep_k, move(send_k, lambda c, i: (c, 1 - i)))
    return (attended, grad_queries, grad_keys, grad_values)


def solution(mesh):
    rows = P(("groups", "ctx", "pair"), "head", None)
    events = P(("groups", "ctx", "pair"))

    def run(queries, key_vectors, value_vectors, targets, token_weights, sessions, window_size):
        total = queries.shape[0] // mesh.shape["groups"]
        length = total // (mesh.shape["ctx"] * mesh.shape["pair"])
        heads = queries.shape[1] // mesh.shape["head"]
        p = Plan(length, heads, queries.shape[2], total)
        return jax.shard_map(
            functools.partial(shards, p),
            mesh=mesh,
            in_specs=(rows, rows, rows, rows, events, events, P("head")),
            out_specs=(rows, rows, rows, rows),
            check_vma=False,
        )(queries, key_vectors, value_vectors, targets, token_weights, sessions, window_size)

    return run
```

time: 84.9 us -> 79 us (0.931)
  starting transfers between devices: 36.6 us -> 23.4 us
  waiting for transfers between devices: 13.3 us -> 22.2 us
    ppermute x19 -> x11, starting transfers between devices: 36.6 us -> 23.4 us  [move(): return lax.ppermute(x, AXES, pairs)]
    ppermute x19 -> x11, waiting for transfers between devices: 13.3 us -> 22.2 us  [move(): return lax.ppermute(x, AXES, pairs)]
    pallas_call x6 -> x5, Pallas kernels: 23.2 us -> 22.5 us  [the longest x2 11.7 us: forward(): pl.pallas_call(functools.partial(forward_body, p, r), out_shape=outs, in_...]
    unnamed x10 -> x6, local copies, waits for them, and re-layouts: 1.91 us -> 2.09 us
  transfers between devices with their start and end apart: 19 -> 11, of which waited for: 2 -> 8; matrix products, arithmetic and copies ran while one was open for 0% -> 0% of each run, Pallas kernels for 29% -> 23%
where the time goes in v3:
time: 79 us; the launch traced here: 78.6 us
  Pallas kernels  30.1 us (38%)
  starting transfers between devices  23.4 us (30%)
  waiting for transfers between devices  22.2 us (28%)
  local copies, waits for them, and re-layouts  2.09 us (3%)
    ppermute x11, starting transfers between devices, move(): return lax.ppermute(x, AXES, pairs)  23.4 us
    ppermute x11, waiting for transfers between devices, move(): return lax.ppermute(x, AXES, pairs)  22.2 us
    pallas_call x2, Pallas kernels, forward(): pl.pallas_call(functools.partial(forward_body, p, r), out_shape=outs, in_...  11.7 us
    pallas_call x2, Pallas kernels, own_keys(): pl.pallas_call(functools.partial(own_body, p, r), out_shape=[full, full],...  5.67 us
    pallas_call x1, Pallas kernels, later_keys(): pl.pallas_call(functools.partial(later_body, p), out_shape=[both, both],...  5.09 us
    pallas_call x1, Pallas kernels, pack(): pl.pallas_call(functools.partial(pack_body, p), out_shape=[jax.ShapeDtype...  4.95 us
    pallas_call x2, Pallas kernels, unpack(): pl.pallas_call(functools.partial(unpack_body, p), out_shape=[out, out], i...  2.68 us
    unnamed x6, local copies, waits for them, and re-layouts  2.09 us
  transfers between devices with their start and end apart: 11, of which 8 were waited for; matrix products, arithmetic and copies ran while one was open for 0% of the time, Pallas kernels for 23%

profile of v3, /device:TPU:9, one launch (start us, length us, event | category | flops | bytes accessed | tf_op | source)
XLA Modules:
  0.0 78.6 jit_solution(424420607162037523)
XLA Ops:
  0.6 4.9 %pack.1 = (bf16[4112,128]{1,0:T(8,128)(2,1)}, bf16[2064,128]{1,0:T(8,128)(2,1)}, bf16[2064,128]{1,0:T(8,128)(2,1)}, bf16[2064,128]{1,0:T(8,128)(2,1)}, bf16[2064...) custom-call(s32[1]{0:T(128)} %bitcast.core_ref, bf16[256,8,128]{2,1,0:T(8,128)(2,1)} %q_ref.1, ...), custom_call_target="tpu_custom_call" | custom-call | tf_op jit(solution)/shard_map/pack/pallas_call | solution.py:166
  6.3 1.9 %collective-permute-start.1 = (bf16[2064,128]{1,0:T(8,128)(2,1)}, bf16[2064,128]{1,0:T(8,128)(2,1)S(1)}, u32[]{:S(2)}, u32[]{:S(2)}) collective-permute-start(bf16[2064,128]{1,0:T(8,128)(2,1)} %get-tuple-element.35.refs_1_), channel_id=1, source_target_pairs={{0,4},{4,8},{5,1},{8,12},{9,5},{13,9},{2,6},{6,10},{7,3},{10,14},{... | collective-permute-start | bytes 1585160 | tf_op jit(solution)/shard_map/ppermute | solution.py:719
  8.3 3.4 %collective-permute-start.2 = (bf16[2064,128]{1,0:T(8,128)(2,1)}, bf16[2064,128]{1,0:T(8,128)(2,1)S(1)}, u32[]{:S(2)}, u32[]{:S(2)}) collective-permute-start(bf16[2064,128]{1,0:T(8,128)(2,1)} %get-tuple-element.36.refs_2_), channel_id=1, source_target_pairs={{1,5},{4,0},{5,9},{8,4},{9,13},{12,8},{3,7},{6,2},{7,11},{10,6},{1... | collective-permute-start | bytes 1585160 | tf_op jit(solution)/shard_map/ppermute | solution.py:719
  11.6 1.9 %collective-permute-start.3 = (bf16[2064,128]{1,0:T(8,128)(2,1)}, bf16[2064,128]{1,0:T(8,128)(2,1)S(1)}, u32[]{:S(2)}, u32[]{:S(2)}) collective-permute-start(bf16[2064,128]{1,0:T(8,128)(2,1)} %get-tuple-element.41), channel_id=1, source_target_pairs={{0,5},{4,9},{5,0},{8,13},{9,4},{13,8},{2,7},{6,11},{7,2},{10,15},{... | collective-permute-start | bytes 1585160 | tf_op jit(solution)/shard_map/ppermute | solution.py:719
  13.6 3.7 %collective-permute-start.4 = (bf16[2064,128]{1,0:T(8,128)(2,1)}, bf16[2064,128]{1,0:T(8,128)(2,1)S(1)}, u32[]{:S(2)}, u32[]{:S(2)}) collective-permute-start(bf16[2064,128]{1,0:T(8,128)(2,1)} %get-tuple-element.42), channel_id=1, source_target_pairs={{1,4},{4,1},{5,8},{8,5},{9,12},{12,9},{3,6},{6,3},{7,10},{10,7},{1... | collective-permute-start | bytes 1585160 | tf_op jit(solution)/shard_map/ppermute | solution.py:719
  17.2 1.2 %collective-permute-done.1.refs_3_ = bf16[2064,128]{1,0:T(8,128)(2,1)S(1)} collective-permute-done((bf16[2064,128]{1,0:T(8,128)(2,1)}, bf16[2064,128]{1,0:T(8,128)(2,1)S(1)}, u32[]{:S(2)}, u32[]{:S(2)}) %collective-permute-start.1) | collective-permute-done | bytes 528416 | tf_op jit(solution)/shard_map/ppermute | solution.py:719
  18.4 2.3 %collective-permute-start.5 = (bf16[1424,128]{1,0:T(8,128)(2,1)}, bf16[1424,128]{1,0:T(8,128)(2,1)S(1)}, u32[]{:S(2)}, u32[]{:S(2)}) collective-permute-start(bf16[1424,128]{1,0:T(8,128)(2,1)} %get-tuple-element.43), channel_id=1, source_target_pairs={{1,9},{5,13},{8,0},{12,4},{3,11},{7,15},{10,2},{14,6},{17,25},{21,... | collective-permute-start | bytes 1093640 | tf_op jit(solution)/shard_map/ppermute | solution.py:719
  20.7 3.7 %collective-permute-done.2.refs_4_ = bf16[2064,128]{1,0:T(8,128)(2,1)S(1)} collective-permute-done((bf16[2064,128]{1,0:T(8,128)(2,1)}, bf16[2064,128]{1,0:T(8,128)(2,1)S(1)}, u32[]{:S(2)}, u32[]{:S(2)}) %collective-permute-start.2) | collective-permute-done | bytes 528416 | tf_op jit(solution)/shard_map/ppermute | solution.py:719
  24.5 4.6 %collective-permute-start.6 = (bf16[1424,128]{1,0:T(8,128)(2,1)}, bf16[1424,128]{1,0:T(8,128)(2,1)S(1)}, u32[]{:S(2)}, u32[]{:S(2)}) collective-permute-start(bf16[1424,128]{1,0:T(8,128)(2,1)} %get-tuple-element.44), channel_id=1, source_target_pairs={{1,8},{5,12},{8,1},{12,5},{3,10},{7,14},{10,3},{14,7},{17,24},{21,... | collective-permute-start | bytes 1093640 | tf_op jit(solution)/shard_map/ppermute | solution.py:719
  29.1 3.7 %collective-permute-done.3.refs_5_ = bf16[2064,128]{1,0:T(8,128)(2,1)S(1)} collective-permute-done((bf16[2064,128]{1,0:T(8,128)(2,1)}, bf16[2064,128]{1,0:T(8,128)(2,1)S(1)}, u32[]{:S(2)}, u32[]{:S(2)}) %collective-permute-start.3) | collective-permute-done | bytes 528416 | tf_op jit(solution)/shard_map/ppermute | solution.py:719
  33.8 1.0 %copy-done = bf16[2064,128]{1,0:T(8,128)(2,1)S(1)} copy-done((bf16[2064,128]{1,0:T(8,128)(2,1)S(1)}, bf16[2064,128]{1,0:T(8,128)(2,1)}, u32[]{:S(2)}) %copy-start) | copy-done | bytes 528408
  34.8 1.0 %copy-done.1 = bf16[2064,128]{1,0:T(8,128)(2,1)S(1)} copy-done((bf16[2064,128]{1,0:T(8,128)(2,1)S(1)}, bf16[2064,128]{1,0:T(8,128)(2,1)}, u32[]{:S(2)}) %copy-start.1) | copy-done | bytes 528408
  35.9 5.9 %forward.2 = (bf16[2,4,256,128]{3,2,1,0:T(8,128)(2,1)S(1)}, bf16[4,256,128]{2,1,0:T(8,128)(2,1)S(1)}, f32[16,128]{1,0:T(8,128)S(1)}, f32[512,128]{1,0:T(8,128)S(1)}) custom-call(s32[1]{0:T(128)} %bitcast.core_ref, s32[8]{0:T(128)S(1)} %copy-done.2, bf16[4112,128]{1,0:T(8,128)(2,1)S(1)} %collective-permute-done.refs_0_, bf16[2064,128]{1,0:T(8,128)(2,1)S(1)} %copy-done, ...), custom_call_target="tpu_custom_call" | custom-call | flops 6554999808 | bytes 5700000 | tf_op jit(solution)/shard_map/forward/pallas_call | solution.py:447
  41.8 3.4 %collective-permute-done.5.refs_7_ = bf16[1424,128]{1,0:T(8,128)(2,1)S(1)} collective-permute-done((bf16[1424,128]{1,0:T(8,128)(2,1)}, bf16[1424,128]{1,0:T(8,128)(2,1)S(1)}, u32[]{:S(2)}, u32[]{:S(2)}) %collective-permute-start.5) | collective-permute-done | bytes 364576 | tf_op jit(solution)/shard_map/ppermute | solution.py:719
  45.2 3.9 %collective-permute-done.6.refs_8_ = bf16[1424,128]{1,0:T(8,128)(2,1)S(1)} collective-permute-done((bf16[1424,128]{1,0:T(8,128)(2,1)}, bf16[1424,128]{1,0:T(8,128)(2,1)S(1)}, u32[]{:S(2)}, u32[]{:S(2)}) %collective-permute-start.6) | collective-permute-done | bytes 364576 | tf_op jit(solution)/shard_map/ppermute | solution.py:719
  49.1 5.8 %forward.3 = (bf16[2,4,256,128]{3,2,1,0:T(8,128)(2,1)S(1)}, bf16[2,4,256,128]{3,2,1,0:T(8,128)(2,1)S(1)}, bf16[4,256,128]{2,1,0:T(8,128)(2,1)S(1)}, f32[16,128]{1,0:T(8,128)S(1)}, bf16[608,128]{1,0:T(8,128)(2,1)S(1)}) custom-call(s32[1]{0:T(128)} %bitcast.core_ref, s32[8]{0:T(128)S(1)} %copy-done.2, bf16[4112,128]{1,0:T(8,128)(2,1)S(1)} %collective-permute-done.refs_0_, ...), custom_call_target="tpu_custom_call" | custom-call | flops 6554999808 | bytes 5700000 | tf_op jit(solution)/shard_map/forward/pallas_call | solution.py:447
  55.0 1.3 %collective-permute-start.9 = (bf16[608,128]{1,0:T(8,128)(2,1)S(1)}, bf16[608,128]{1,0:T(8,128)(2,1)S(1)}, u32[]{:S(2)}, u32[]{:S(2)}) collective-permute-start(bf16[608,128]{1,0:T(8,128)(2,1)S(1)} %get-tuple-element.52), channel_id=1, source_target_pairs={{8,0},{9,1},{12,4},{13,5},{10,2},{11,3},{14,6},{15,7},{24,16},{25,... | collective-permute-start | bytes 466952 | tf_op jit(solution)/shard_map/ppermute | solution.py:719
  56.2 3.1 %collective-permute-start.8 = (bf16[608,128]{1,0:T(8,128)(2,1)S(1)}, bf16[608,128]{1,0:T(8,128)(2,1)S(1)}, u32[]{:S(2)}, u32[]{:S(2)}) collective-permute-start(bf16[608,128]{1,0:T(8,128)(2,1)S(1)} %get-tuple-element.52), channel_id=1, source_target_pairs={{4,0},{5,1},{8,4},{9,5},{12,8},{13,9},{6,2},{7,3},{10,6},{11,7},{1... | collective-permute-start | bytes 466952 | tf_op jit(solution)/shard_map/ppermute | solution.py:719
  59.4 3.5 %own_keys.2 = (f32[4,512,128]{2,1,0:T(8,128)S(1)}, f32[4,512,128]{2,1,0:T(8,128)S(1)}) custom-call(s32[1]{0:T(128)} %bitcast.core_ref, s32[8]{0:T(128)S(1)} %copy-done.2, bf16[4112,128]{1,0:T(8,128)(2,1)S(1)} %collective-permute-done.refs_0_, bf16[2064,128]{1,0:T(8,128)(2,1)S(1)} %copy-done, bf16[2064,128]{1,0:T(8,128)(2,1)S(1)} %copy-done.1, ...), custom_call_target="tpu_custom_call" | custom-call | flops 4600000000 | bytes 4000000 | tf_op jit(solution)/shard_map/own_keys/pallas_call | solution.py:544
  62.9 2.2 %own_keys.3 = (f32[4,256,128]{2,1,0:T(8,128)S(1)}, f32[4,256,128]{2,1,0:T(8,128)S(1)}) custom-call(s32[1]{0:T(128)} %bitcast.core_ref, s32[8]{0:T(128)S(1)} %copy-done.2, bf16[4112,128]{1,0:T(8,128)(2,1)S(1)} %collective-permute-done.refs_0_, bf16[2064,128]{1,0:T(8,128)(2,1)S(1)} %copy-done, bf16[2064,128]{1,0:T(8,128)(2,1)S(1)} %copy-done.1, ...), custom_call_target="tpu_custom_call" | custom-call | flops 2300000000 | bytes 2000000 | tf_op jit(solution)/shard_map/own_keys/pallas_call | solution.py:544
  65.1 5.0 %collective-permute-done.8.refs_9_ = bf16[608,128]{1,0:T(8,128)(2,1)S(1)} collective-permute-done((bf16[608,128]{1,0:T(8,128)(2,1)S(1)}, bf16[608,128]{1,0:T(8,128)(2,1)S(1)}, u32[]{:S(2)}, u32[]{:S(2)}) %collective-permute-start.8) | collective-permute-done | bytes 155680 | tf_op jit(solution)/shard_map/ppermute | solution.py:719
  70.2 5.1 %later_keys.1 = (bf16[2,4,256,128]{3,2,1,0:T(8,128)(2,1)S(1)}, bf16[2,4,256,128]{3,2,1,0:T(8,128)(2,1)S(1)}) custom-call(s32[1]{0:T(128)} %bitcast.core_ref, s32[8]{0:T(128)S(1)} %copy-done.2, bf16[4112,128]{1,0:T(8,128)(2,1)S(1)} %collective-permute-done.refs_0_, bf16[2064,128]{1,0:T(8,128)(2,1)S(1)} %copy-done, bf16[2064,128]{1,0:T(8,128)(2,1)S(1)} %copy-done.1, ...), custom_call_target="tpu_custom_call" | custom-call | flops 6325000192 | bytes 5500000 | tf_op jit(solution)/shard_map/later_keys/pallas_call | solution.py:651
  75.7 1.3 %unpack.2 = (bf16[256,8,128]{2,1,0:T(8,128)(2,1)}, bf16[256,8,128]{2,1,0:T(8,128)(2,1)}) custom-call(s32[1]{0:T(128)} %bitcast.core_ref, bf16[2,4,256,128]{3,2,1,0:T(8,128)(2,1)S(1)} %get-tuple-element.48.mine, bf16[2,4,256,128]{3,2,1,0:T(8,128)(2,1)S(1)} %collective-permute-done.7.theirs), custom_call_target="tpu_custom_call" | custom-call | flops 1610000000 | bytes 1400000 | tf_op jit(solution)/shard_map/unpack/pallas_call | solution.py:675
  77.2 1.3 %unpack.3 = (bf16[256,8,128]{2,1,0:T(8,128)(2,1)}, bf16[256,8,128]{2,1,0:T(8,128)(2,1)}) custom-call(s32[1]{0:T(128)} %bitcast.core_ref, bf16[2,4,256,128]{3,2,1,0:T(8,128)(2,1)S(1)} %get-tuple-element.60.mine, bf16[2,4,256,128]{3,2,1,0:T(8,128)(2,1)S(1)} %collective-permute-done.10.theirs), custom_call_target="tpu_custom_call" | custom-call | flops 1610000000 | bytes 1400000 | tf_op jit(solution)/shard_map/unpack/pallas_call | solution.py:675
  (12 shorter events, 2.5 us)
Async XLA Ops:
  0.6 33.2 %copy-start.2 = (s32[8]{0:T(128)S(1)}, s32[8]{0:T(128)}, u32[]{:S(2)}) copy-start(s32[8]{0:T(128)} %win_ref.9) | copy-start | bytes 100
  5.6 28.2 %collective-permute-start = (bf16[4112,128]{1,0:T(8,128)(2,1)}, bf16[4112,128]{1,0:T(8,128)(2,1)S(1)}, u32[]{:S(2)}, u32[]{:S(2)}) collective-permute-start(bf16[4112,128]{1,0:T(8,128)(2,1)} %get-tuple-element.34), channel_id=1, source_target_pairs={{0,1},{1,0},{4,5},{5,4},{8,9},{9,8},{12,13},{13,12},{2,3},{3,2},{6... | collective-permute-start | bytes 3158024 | tf_op jit(solution)/shard_map/ppermute | solution.py:719
  6.3 12.1 %collective-permute-start.1 = (bf16[2064,128]{1,0:T(8,128)(2,1)}, bf16[2064,128]{1,0:T(8,128)(2,1)S(1)}, u32[]{:S(2)}, u32[]{:S(2)}) collective-permute-start(bf16[2064,128]{1,0:T(8,128)(2,1)} %get-tuple-element.35.refs_1_), channel_id=1, source_target_pairs={{0,4},{4,8},{5,1},{8,12},{9,5},{13,9},{2,6},{6,10},{7,3},{10,14},{... | collective-permute-start | bytes 1585160 | tf_op jit(solution)/shard_map/ppermute | solution.py:719
  8.3 16.2 %collective-permute-start.2 = (bf16[2064,128]{1,0:T(8,128)(2,1)}, bf16[2064,128]{1,0:T(8,128)(2,1)S(1)}, u32[]{:S(2)}, u32[]{:S(2)}) collective-permute-start(bf16[2064,128]{1,0:T(8,128)(2,1)} %get-tuple-element.36.refs_2_), channel_id=1, source_target_pairs={{1,5},{4,0},{5,9},{8,4},{9,13},{12,8},{3,7},{6,2},{7,11},{10,6},{1... | collective-permute-start | bytes 1585160 | tf_op jit(solution)/shard_map/ppermute | solution.py:719
  11.6 21.1 %collective-permute-start.3 = (bf16[2064,128]{1,0:T(8,128)(2,1)}, bf16[2064,128]{1,0:T(8,128)(2,1)S(1)}, u32[]{:S(2)}, u32[]{:S(2)}) collective-permute-start(bf16[2064,128]{1,0:T(8,128)(2,1)} %get-tuple-element.41), channel_id=1, source_target_pairs={{0,5},{4,9},{5,0},{8,13},{9,4},{13,8},{2,7},{6,11},{7,2},{10,15},{... | collective-permute-start | bytes 1585160 | tf_op jit(solution)/shard_map/ppermute | solution.py:719
  13.6 20.2 %collective-permute-start.4 = (bf16[2064,128]{1,0:T(8,128)(2,1)}, bf16[2064,128]{1,0:T(8,128)(2,1)S(1)}, u32[]{:S(2)}, u32[]{:S(2)}) collective-permute-start(bf16[2064,128]{1,0:T(8,128)(2,1)} %get-tuple-element.42), channel_id=1, source_target_pairs={{1,4},{4,1},{5,8},{8,5},{9,12},{12,9},{3,6},{6,3},{7,10},{10,7},{1... | collective-permute-start | bytes 1585160 | tf_op jit(solution)/shard_map/ppermute | solution.py:719
  18.4 26.8 %collective-permute-start.5 = (bf16[1424,128]{1,0:T(8,128)(2,1)}, bf16[1424,128]{1,0:T(8,128)(2,1)S(1)}, u32[]{:S(2)}, u32[]{:S(2)}) collective-permute-start(bf16[1424,128]{1,0:T(8,128)(2,1)} %get-tuple-element.43), channel_id=1, source_target_pairs={{1,9},{5,13},{8,0},{12,4},{3,11},{7,15},{10,2},{14,6},{17,25},{21,... | collective-permute-start | bytes 1093640 | tf_op jit(solution)/shard_map/ppermute | solution.py:719
  24.5 24.6 %collective-permute-start.6 = (bf16[1424,128]{1,0:T(8,128)(2,1)}, bf16[1424,128]{1,0:T(8,128)(2,1)S(1)}, u32[]{:S(2)}, u32[]{:S(2)}) collective-permute-start(bf16[1424,128]{1,0:T(8,128)(2,1)} %get-tuple-element.44), channel_id=1, source_target_pairs={{1,8},{5,12},{8,1},{12,5},{3,10},{7,14},{10,3},{14,7},{17,24},{21,... | collective-permute-start | bytes 1093640 | tf_op jit(solution)/shard_map/ppermute | solution.py:719
  33.8 1.0 %copy-start = (bf16[2064,128]{1,0:T(8,128)(2,1)S(1)}, bf16[2064,128]{1,0:T(8,128)(2,1)}, u32[]{:S(2)}) copy-start(bf16[2064,128]{1,0:T(8,128)(2,1)} %get-tuple-element.35.refs_1_) | copy-start | bytes 1585156
  34.8 1.0 %copy-start.1 = (bf16[2064,128]{1,0:T(8,128)(2,1)S(1)}, bf16[2064,128]{1,0:T(8,128)(2,1)}, u32[]{:S(2)}) copy-start(bf16[2064,128]{1,0:T(8,128)(2,1)} %get-tuple-element.36.refs_2_) | copy-start | bytes 1585156
  55.0 10.2 %collective-permute-start.9 = (bf16[608,128]{1,0:T(8,128)(2,1)S(1)}, bf16[608,128]{1,0:T(8,128)(2,1)S(1)}, u32[]{:S(2)}, u32[]{:S(2)}) collective-permute-start(bf16[608,128]{1,0:T(8,128)(2,1)S(1)} %get-tuple-element.52), channel_id=1, source_target_pairs={{8,0},{9,1},{12,4},{13,5},{10,2},{11,3},{14,6},{15,7},{24,16},{25,... | collective-permute-start | bytes 466952 | tf_op jit(solution)/shard_map/ppermute | solution.py:719
  56.2 13.9 %collective-permute-start.8 = (bf16[608,128]{1,0:T(8,128)(2,1)S(1)}, bf16[608,128]{1,0:T(8,128)(2,1)S(1)}, u32[]{:S(2)}, u32[]{:S(2)}) collective-permute-start(bf16[608,128]{1,0:T(8,128)(2,1)S(1)} %get-tuple-element.52), channel_id=1, source_target_pairs={{4,0},{5,1},{8,4},{9,5},{12,8},{13,9},{6,2},{7,3},{10,6},{11,7},{1... | collective-permute-start | bytes 466952 | tf_op jit(solution)/shard_map/ppermute | solution.py:719
  59.4 16.3 %collective-permute-start.7 = (bf16[2,4,256,128]{3,2,1,0:T(8,128)(2,1)S(1)}, bf16[2,4,256,128]{3,2,1,0:T(8,128)(2,1)S(1)}, u32[]{:S(2)}, u32[]{:S(2)}) collective-permute-start(bf16[2,4,256,128]{3,2,1,0:T(8,128)(2,1)S(1)} %get-tuple-element.49), channel_id=1, source_target_pairs={{0,1},{1,0},{4,5},{5,4},{8,9},{9,8},{12,13},{13,12},{2,3},{3,2},{6... | collective-permute-start | bytes 1572872 | tf_op jit(solution)/shard_map/ppermute | solution.py:719
  75.3 2.0 %collective-permute-start.10 = (bf16[2,4,256,128]{3,2,1,0:T(8,128)(2,1)S(1)}, bf16[2,4,256,128]{3,2,1,0:T(8,128)(2,1)S(1)}, u32[]{:S(2)}, u32[]{:S(2)}) collective-permute-start(bf16[2,4,256,128]{3,2,1,0:T(8,128)(2,1)S(1)} %get-tuple-element.61), channel_id=1, source_target_pairs={{0,1},{1,0},{4,5},{5,4},{8,9},{9,8},{12,13},{13,12},{2,3},{3,2},{6... | collective-permute-start | bytes 1572872 | tf_op jit(solution)/shard_map/ppermute | solution.py:719

commit v4 on v3

--- a/solution.py
+++ b/solution.py
@@ -92,14 +92,13 @@
         self.pair_rows = self.all * 4 * length + EXTRA
         self.stat_rows = -(-2 * self.all * self.code_rows // 16) * 16
         self.state_rows = self.all * width
-        self.far_refs = 2 if self.merged else 4
+        self.far_refs = 1 if self.merged else 2
 
 
 def pack_body(p, core_ref, q_ref, k_ref, v_ref, t_ref, w_ref, s_ref, *rest):
-    number = (len(rest) - 4) // 2
-    outs, staged = list(rest[:number]), list(rest[number : 2 * number])
-    scratch, landed, sems, out_sems = rest[2 * number :]
-    core = core_ref[0]
+    number = (len(rest) - 3) // 2
+    outs, staged = rest[:number], rest[number : 2 * number]
+    landed, sems, out_sems = rest[2 * number :]
     L = p.length
     copies = [
         pltpu.make_async_copy(ref, landed.at[n], sems.at[n])
@@ -113,53 +112,46 @@
     ).astype(bf16)
     for ref in staged:
         ref[ref.shape[0] - EXTRA :, :] = codes
-    leaving = []
-
-    def leave():
-        copy_out = pltpu.make_async_copy(staged.pop(0), outs.pop(0), out_sems.at[len(leaving)])
-        copy_out.start()
-        leaving.append(copy_out)
-
-    other = (1 - core) * p.all
-    for n in range(4):
-        copies[n].wait()
-        x = jnp.swapaxes(landed[n].astype(f32), 0, 1)
-        if n == 3:
-            x = x * weight[None]
-        scratch[n] = x.astype(bf16)
-    for n in range(4):
-        for h in range(p.all):
-            at = (n * p.all + h) * L
-            staged[0][at : at + L, :] = scratch[n, other + h]
-    leave()
-    for first, base in (
-        (core * 2, core * p.all),
-        ((1 - core) * 2, core * p.all),
-        (core * 2, other),
-        ((1 - core) * 2, other),
-    ):
-        for n in range(2):
+
+    def pack_for(me):
+        leaving = []
+
+        def leave(x, part, parts, rows):
+            here = slice(part * rows, (part + 1) * rows + EXTRA * (part == parts - 1))
+            copy_out = pltpu.make_async_copy(
+                staged[x].at[here, :], outs[x].at[here, :], out_sems.at[len(leaving)]
+            )
+            copy_out.start()
+            leaving.append(copy_out)
+
+        for n in range(4):
+            copies[n].wait()
+            x = jnp.swapaxes(landed[n].astype(f32), 0, 1)
+            if n == 3:
+                x = x * weight[None]
+            x = x.astype(bf16)
+            mine = x[me * p.all : (me + 1) * p.all]
+            other = x[(1 - me) * p.all : (2 - me) * p.all]
+            to = n % 2 * p.all
+            for at, heads in ((1 + n // 2 * 2, mine), (2 + n // 2 * 2, other)):
+                for h in range(p.all):
+                    staged[at][(to + h) * L : (to + h + 1) * L, :] = heads[h]
+                leave(at, n % 2, 2, p.all * L)
             for h in range(p.all):
-                at = (n * p.all + h) * L
-                staged[0][at : at + L, :] = scratch[first + n, base + h]
-        leave()
-    if p.merged:
-        first = (1 - core) * 2
-        lead = core * (L - p.tail)
-        for base in (core * p.all, other):
-            for n in range(2):
-                for h in range(p.all):
-                    at = (n * p.all + h) * p.tail
-                    staged[0][at : at + p.tail, :] = scratch[
-                        first + n, base + h, pl.ds(pl.multiple_of(lead, 16), p.tail), :
-                    ]
-            leave()
-    for copy_out in leaving:
-        copy_out.wait()
+                staged[0][(n * p.all + h) * L : (n * p.all + h + 1) * L, :] = other[h]
+            leave(0, n, 4, p.all * L)
+        for copy_out in leaving:
+            copy_out.wait()
+
+    for me in range(2):
+
+        @pl.when(core_ref[0] == me)
+        def _():
+            pack_for(me)
 
 
 def pack(p, core, q, k, v, targets, weights, sessions):
-    rows = [p.pair_rows] + [p.rows] * 4 + [p.tail_rows] * (2 if p.merged else 0)
+    rows = [p.pair_rows] + [p.rows] * 4
     shapes = [(n, p.width) for n in rows]
     vmem = pl.BlockSpec(memory_space=pltpu.VMEM)
     hbm = pl.BlockSpec(memory_space=pl.ANY)
@@ -170,19 +162,48 @@
         out_specs=[hbm] * len(shapes),
         scratch_shapes=[pltpu.VMEM(x, bf16) for x in shapes]
         + [
-            pltpu.VMEM((4, p.heads, p.length, p.width), bf16),
             pltpu.VMEM((4, p.length, p.heads, p.width), bf16),
             pltpu.SemaphoreType.DMA((4,)),
-            pltpu.SemaphoreType.DMA((len(shapes),)),
+            pltpu.SemaphoreType.DMA((12,)),
         ],
         compiler_params=pltpu.CompilerParams(vmem_limit_bytes=56 << 20),
         name="pack",
     )(core, q, k, v, targets, weights, sessions)
 
 
-def code_block(p, core, pick):
-    one, two = (ref[ref.shape[0] - EXTRA :, :].astype(f32)[: p.code_rows] for ref in pick)
-    return jnp.where(core == 0, one, two)
+def tails_body(p, core_ref, pair, own_keys, own_queries, keys, queries):
+    L = p.length
+
+    def tails_for(me):
+        sources = [(pair, 0), (own_queries, 0)] if me == 0 else [(own_keys, 0), (pair, 2)]
+        for out, (ref, first), lead in zip((keys, queries), sources, (L - p.tail, 0)):
+            for n in range(2 * p.all):
+                at = (first * p.all + n) * L + lead
+                out[n * p.tail : (n + 1) * p.tail, :] = ref[at : at + p.tail, :]
+            out[p.tail_rows - EXTRA :, :] = ref[ref.shape[0] - EXTRA :, :]
+
+    for me in range(2):
+
+        @pl.when(core_ref[0] == me)
+        def _():
+            tails_for(me)
+
+
+def make_tails(p, core, pair, own_keys, own_queries):
+    vmem = pl.BlockSpec(memory_space=pltpu.VMEM)
+    out = jax.ShapeDtypeStruct((p.tail_rows, p.width), bf16)
+    return pl.pallas_call(
+        functools.partial(tails_body, p),
+        out_shape=[out, out],
+        in_specs=[pl.BlockSpec(memory_space=pltpu.SMEM), vmem, vmem, vmem],
+        out_specs=[vmem, vmem],
+        **params(1.0),
+        name="tails",
+    )(core, pair, own_keys, own_queries)
+
+
+def code_block(p, ref):
+    return ref[ref.shape[0] - EXTRA :, :].astype(f32)[: p.code_rows]
 
 
 def count(condition):
@@ -215,8 +236,8 @@
     def codes(self):
         return in_order(
             self.core,
-            code_block(self.p, self.core, self.same),
-            code_block(self.p, self.core, self.cross),
+            code_block(self.p, self.same),
+            code_block(self.p, self.cross),
         )
 
     def bring(self, targets, start, tile=None):
@@ -227,8 +248,8 @@
             @pl.when(self.core == me)
             def _():
                 for ref, which, first in (
-                    (self.same[me], me, 0),
-                    (self.cross[me], 1 - me, self.index),
+                    (self.same, me, 0),
+                    (self.cross, 1 - me, self.index),
                 ):
                     if tile not in (None, which):
                         continue
@@ -240,25 +261,19 @@
 
 
 def own_chip(p, core, refs):
-    pair, x1, x2 = refs[:3]
-    keys = Chip(p, core, (x1, x2), (pair, pair), 0)
-    return keys, Chip(p, core, (x2, x1), (pair, pair), 2)
-
-
-def near_chips(p, core, refs):
-    r1, r2, r3, r4 = refs[3:7]
-    return Chip(p, core, (r1, r2), (r4, r3)), Chip(p, core, (r2, r1), (r3, r4))
-
-
-def bring_tail(p, core, pick, targets, start):
-    for me in range(2):
-
-        @pl.when(core == me)
-        def _():
-            for n, target in enumerate(targets):
-                for h in range(p.all):
-                    at = (n * p.all + h) * p.tail
-                    target[h, start : start + p.tail, :] = pick[me][at : at + p.tail, :]
+    pair, kv, qg = refs[:3]
+    return Chip(p, core, kv, pair, 0), Chip(p, core, qg, pair, 2)
+
+
+def near_chip(p, core, refs):
+    return Chip(p, core, *refs[3:5])
+
+
+def bring_tail(p, ref, targets, start):
+    for n, target in enumerate(targets):
+        for h in range(p.all):
+            at = (n * p.all + h) * p.tail
+            target[h, start : start + p.tail, :] = ref[at : at + p.tail, :]
 
 
 def divide(core, tiles, keep, send):
@@ -270,190 +285,385 @@
             send[...] = tiles[1 - me][...]
 
 
-def forward_body(p, r, core_ref, win_ref, *refs):
-    near, refs = refs[:7], refs[7:]
-    far_here = r == 0 or not p.merged
-    if far_here:
+class Events:
+    def __init__(self, p, r, own_codes, halo_codes):
+        L = p.length
+        self.mine = column_of(own_codes[r * p.code_rows : (r + 1) * p.code_rows])
+        self.last = halo_codes[-1:, LANES - 1 :]
+        self.first_own = own_codes[0:1, 0:1]
+        lo = jnp.zeros((L, 1), f32)
+        for n in range(1, SESSIONS + 1):
+            start = count(own_codes < n) - count(halo_codes >= n)
+            lo = jnp.where(self.mine == n, start, lo)
+        self.lo = lo.astype(jnp.int32)
+        self.continued = count(
+            jnp.logical_and(halo_codes == self.last, halo_codes > 0)
+        ).astype(jnp.int32)
+        self.t_pos = lax.broadcasted_iota(jnp.int32, (L, 1), 0) + r * L
+        self.reads = self.mine == self.last
+        self.opening = self.mine == self.first_own
+
+    def low(self, window):
+        return jnp.maximum(self.lo, self.t_pos - window + 1)
+
+
+def halo_state(events, k, v, start):
+    pos = lax.broadcasted_iota(jnp.int32, (k.shape[0], 1), 0) + start
+    inside = jnp.broadcast_to(pos >= -events.continued, k.shape)
+    phi = jnp.where(inside, feature(k.astype(f32)), 0.0).astype(bf16)
+    return t_dot(phi, v)
+
+
+def masked(events, score, low, start):
+    L, wide = score.shape
+    n_halo = -start
+    s_pos = lax.broadcasted_iota(jnp.int32, (L, n_halo), 1) - n_halo
+    own_pos = lax.broadcasted_iota(jnp.int32, (L, wide - n_halo), 1)
+    inside = jnp.logical_and(own_pos >= low, own_pos <= events.t_pos)
+    return jnp.concatenate(
+        [
+            jnp.where(s_pos >= low, score[:, :n_halo], MASKED),
+            jnp.where(inside, score[:, n_halo:], MASKED),
+        ],
+        axis=1,
+    )
+
+
+def similar(events, score):
+    own_pos = lax.broadcasted_iota(jnp.int32, score.shape, 1)
+    inside = jnp.logical_and(own_pos >= events.lo, own_pos <= events.t_pos)
+    return jnp.where(inside, score, 0.0).astype(bf16)
+
+
+def normalized(numerator, gf):
+    inverse_rms = lax.rsqrt(jnp.mean(numerator * numerator, axis=1, keepdims=True) + EPSILON)
+    linear_out = numerator * inverse_rms
+    grad_num = inverse_rms * (gf - linear_out * jnp.mean(gf * linear_out, axis=1, keepdims=True))
+    return linear_out, grad_num.astype(bf16)
+
+
+def put_stats(p, stat, h, lse, rowdot):
+    for which, column in ((0, lse), (1, rowdot)):
+        base = (which * p.all + h) * p.code_rows
+        row = row_of(column)
+        for j in range(p.code_rows):
+            stat[base + j : base + j + 1, :] = row[:, j * LANES : (j + 1) * LANES]
+
+
+def stat_values(p, stat):
+    values = stat[...]
+    used = 2 * p.all * p.code_rows
+    if used < p.stat_rows:
+        inside = lax.broadcasted_iota(jnp.int32, values.shape, 0) < used
+        values = jnp.where(inside, values, 0.0)
+    return values
+
+
+def wide_column(column):
+    return jnp.broadcast_to(column, (column.shape[0], LANES))
+
+
+def bring_far_keys(p, core, far, targets):
+    if not p.merged:
+        far_at = Chip(p, core, *far)
+        far_at.bring(targets, 0)
+        return far_at.codes()
+    bring_tail(p, far[0], targets, p.tail_fill - p.tail)
+    if p.tail < p.tail_fill:
+        gap = p.tail_fill - p.tail
+        for target in targets:
+            target[:, 0:gap, :] = jnp.zeros((p.all, gap, p.width), bf16)
+    return code_block(p, far[0])
+
+
+def scales(p):
+    scale = 1.0 / math.sqrt(p.width)
+    return scale, scale * math.log2(math.e)
+
+
+def second_body(p, core_ref, win_ref, *refs):
+    near, refs = refs[:5], refs[5:]
+    if not p.merged:
         far, refs = refs[: p.far_refs], refs[p.far_refs :]
     if p.far:
         far_ref, refs = refs[0], refs[1:]
-    if r == 0:
-        (state_in, stats_in, second), refs = refs[:3], refs[3:]
-        keep, send, gn_out, stats_out, message, ks, vs, qs, gs, stat, out = refs
-    else:
-        out, gn_out, stats_out, state_out, ks, vs, qs, gs, stat = refs
+    out, gn_out, stats_out, state_out, ks, vs, qs, gs, stat = refs
     core = core_ref[0]
     L, C, B, D = p.length, p.chip, p.before, p.width
-    scale = 1.0 / math.sqrt(D)
-    c2 = scale * math.log2(math.e)
-
+    scale, c2 = scales(p)
     own_keys_at, own_queries_at = own_chip(p, core, near)
-    near_at, _ = near_chips(p, core, near)
+    near_at = near_chip(p, core, near)
     own_keys_at.bring((ks, vs), B)
-    own_queries_at.bring((qs, gs), 0, r)
+    own_queries_at.bring((qs, gs), 0, 1)
     near_at.bring((ks, vs), p.tail_fill)
-    own_codes = own_keys_at.codes()
-    near_codes = near_at.codes()
-    halo_codes = near_codes
-    if far_here:
-        if p.merged:
-            pick = (far[1], far[0])
-            bring_tail(p, core, pick, (ks, vs), p.tail_fill - p.tail)
-            far_codes = code_block(p, core, pick)
-            if p.tail < p.tail_fill:
-                gap = p.tail_fill - p.tail
-                ks[:, 0:gap, :] = jnp.zeros((p.all, gap, D), bf16)
-                vs[:, 0:gap, :] = jnp.zeros((p.all, gap, D), bf16)
-        else:
-            far_at = Chip(p, core, (far[0], far[1]), (far[3], far[2]))
-            far_at.bring((ks, vs), 0)
-            far_codes = far_at.codes()
-        halo_codes = jnp.concatenate([far_codes, near_codes], axis=0)
-    begin = 0 if far_here else p.tail_fill
-    if not far_here:
-        begin = max(begin, r * L)
-    n_halo = B - begin
-    n_own = (r + 1) * L
-    wide = n_halo + n_own
-    mine = column_of(own_codes[r * p.code_rows : (r + 1) * p.code_rows])
-    last = near_codes[2 * p.code_rows - 1 :, LANES - 1 :]
-    first_own = own_codes[0:1, 0:1]
-    lo = jnp.zeros((L, 1), f32)
-    for n in range(1, SESSIONS + 1):
-        start = count(own_codes < n) - count(halo_codes >= n)
-        lo = jnp.where(mine == n, start, lo)
-    lo = lo.astype(jnp.int32)
-    cont = count(jnp.logical_and(halo_codes == last, halo_codes > 0)).astype(jnp.int32)
-    halo_pos = lax.broadcasted_iota(jnp.int32, (n_halo, 1), 0) - n_halo
-    in_start = jnp.broadcast_to(halo_pos >= -cont, (n_halo, D))
-    t_pos = lax.broadcasted_iota(jnp.int32, (L, 1), 0) + r * L
-    reads = mine == last
-    opening = mine == first_own
+    halo_codes = near_at.codes()
+    begin = p.tail_fill
+    if not p.merged:
+        far_codes = bring_far_keys(p, core, far, (ks, vs))
+        halo_codes = jnp.concatenate([far_codes, halo_codes], axis=0)
+        begin = 0
+    events = Events(p, 1, own_keys_at.codes(), halo_codes)
 
     def stream(h):
         q = qs[h]
         g = gs[h]
         gf = g.astype(f32)
         qf = q.astype(f32)
-        window = win_ref[core * p.all + h]
-        low = jnp.maximum(lo, t_pos - window + 1)
-        k_part = ks[h, begin : begin + wide, :]
-        v_part = vs[h, begin : begin + wide, :]
-        v_own = vs[h, B : B + n_own, :]
+        k_part = ks[h, begin:, :]
+        v_part = vs[h, begin:, :]
+        v_own = vs[h, B:, :]
         score = dot_t(q, k_part)
         yield
-        phi_k = feature(ks[h, B : B + n_own, :].astype(f32)).astype(bf16)
+        phi_k = feature(ks[h, B:, :].astype(f32)).astype(bf16)
+        here = slice(h * D, (h + 1) * D)
         if p.far:
-            start_state = far_ref[h * D : (h + 1) * D, :]
+            start_state = far_ref[here, :]
         else:
-            halo_phi = jnp.where(in_start, feature(ks[h, begin:B, :].astype(f32)), 0.0)
-            start_state = t_dot(halo_phi.astype(bf16), vs[h, begin:B, :]).astype(bf16)
+            start_state = halo_state(events, ks[h, begin:B, :], vs[h, begin:B, :], begin - B)
+            start_state = start_state.astype(bf16)
         phi_q = feature(qf).astype(bf16)
         a = dot_t(phi_q, phi_k)
         from_start = dot(phi_q, start_state)
         yield
-        s_pos = lax.broadcasted_iota(jnp.int32, (L, n_halo), 1) - n_halo
-        own_pos = lax.broadcasted_iota(jnp.int32, (L, n_own), 1)
-        causal = own_pos <= t_pos
-        score = jnp.concatenate(
-            [
-                jnp.where(s_pos >= low, score[:, :n_halo], MASKED),
-                jnp.where(
-                    jnp.logical_and(own_pos >= low, causal), score[:, n_halo:], MASKED
-                ),
-            ],
-            axis=1,
-        )
+        low = events.low(win_ref[core * p.all + h])
+        score = masked(events, score, low, begin - B)
         peak = jnp.max(score, axis=1, keepdims=True) * c2
         e = jnp.exp2(score * c2 - peak)
         total = jnp.sum(e, axis=1, keepdims=True)
         yield
         inverse = 1.0 / total
         window_out = dot(e.astype(bf16), v_part) * inverse
-        alike = jnp.logical_and(own_pos >= lo, causal)
-        a = jnp.where(alike, a, 0.0).astype(bf16)
-        numerator = dot(a, v_own) + jnp.where(reads, from_start, 0.0)
+        a = similar(events, a)
+        numerator = dot(a, v_own) + jnp.where(events.reads, from_start, 0.0)
         grad_prob = dot_t(g, v_part)
         yield
         rowdot = jnp.sum(gf * window_out, axis=1, keepdims=True)
-        inverse_rms = lax.rsqrt(jnp.mean(numerator * numerator, axis=1, keepdims=True) + EPSILON)
-        linear_out = numerator * inverse_rms
-        grad_num = (
-            inverse_rms * (gf - linear_out * jnp.mean(gf * linear_out, axis=1, keepdims=True))
-        ).astype(bf16)
+        linear_out, grad_num = normalized(numerator, gf)
         gn_out[h] = grad_num
         out[0, h] = (linear_out + window_out).astype(bf16)
         b = dot_t(grad_num, v_own)
         ds = (e * (grad_prob - rowdot)).astype(bf16)
         yield
         dq = dot(ds, k_part) * (inverse * scale)
-        state = t_dot(jnp.where(opening, phi_q, jnp.zeros_like(phi_q)), grad_num)
-        lse = peak + jnp.log2(total)
-        for which, column in ((0, lse), (1, rowdot)):
-            base = (which * p.all + h) * p.code_rows
-            row = row_of(column)
-            for j in range(p.code_rows):
-                stat[base + j : base + j + 1, :] = row[:, j * LANES : (j + 1) * LANES]
-        yield
-        b = jnp.where(alike, b, 0.0).astype(bf16)
-        grad_phi_q = dot(b, phi_k) + jnp.where(reads, dot_t(grad_num, start_state), 0.0)
+        opening = jnp.where(events.opening, phi_q, jnp.zeros_like(phi_q))
+        state_out[here, :] = t_dot(opening, grad_num)
+        put_stats(p, stat, h, peak + jnp.log2(total), rowdot)
+        yield
+        grad_phi_q = dot(similar(events, b), phi_k) + jnp.where(
+            events.reads, dot_t(grad_num, start_state), 0.0
+        )
         out[1, h] = (slope(qf) * grad_phi_q + dq).astype(bf16)
+
+    drive(stream(h) for h in range(p.all))
+    stats_out[...] = stat_values(p, stat)
+
+
+def start_body(p, core_ref, win_ref, *refs):
+    near, refs = refs[:5], refs[5:]
+    acc_out, num_out, peak_out, total_out, state_out, ks, vs, qs, gs = refs
+    core = core_ref[0]
+    L, C, D = p.length, p.chip, p.width
+    scale, c2 = scales(p)
+    own_keys_at, own_queries_at = own_chip(p, core, near)
+    near_at = near_chip(p, core, near)
+    own_keys_at.bring((ks, vs), C, 0)
+    own_queries_at.bring((qs, gs), 0, 0)
+    near_at.bring((ks, vs), 0)
+    events = Events(p, 0, own_keys_at.codes(), near_at.codes())
+
+    def stream(h):
+        q = qs[h]
+        score = dot_t(q, ks[h])
+        yield
+        phi_q = feature(q.astype(f32)).astype(bf16)
+        a = dot_t(phi_q, feature(ks[h, C:, :].astype(f32)).astype(bf16))
+        if not p.far:
+            state_out[h * D : (h + 1) * D, :] = halo_state(
+                events, ks[h, :C, :], vs[h, :C, :], -C
+            )
+        yield
+        low = events.low(win_ref[core * p.all + h])
+        score = masked(events, score, low, -C)
+        peak = jnp.max(score, axis=1, keepdims=True) * c2
+        e = jnp.exp2(score * c2 - peak)
+        peak_out[h] = wide_column(peak)
+        total_out[h] = wide_column(jnp.sum(e, axis=1, keepdims=True))
+        yield
+        acc_out[h] = dot(e.astype(bf16), vs[h])
+        num_out[h] = dot(similar(events, a), vs[h, C:, :])
+
+    drive(stream(h) for h in range(p.all))
+
+
+def first_body(p, core_ref, win_ref, *refs):
+    near, far, refs = refs[:5], refs[5 : 5 + p.far_refs], refs[5 + p.far_refs :]
+    begun, refs = refs[:5], refs[5:]
+    acc_in, num_in, peak_in, total_in, near_state = begun
+    (second_state, second_stats), refs = refs[:2], refs[2:]
+    if p.far:
+        far_ref, refs = refs[0], refs[1:]
+    out, gn_out, stats_out, lse_out, rowdot_out, state_out, message, ks, vs, qs, gs, stat = refs
+    core = core_ref[0]
+    L, B, D = p.length, p.before, p.width
+    scale, c2 = scales(p)
+    own_keys_at, own_queries_at = own_chip(p, core, near)
+    near_at = near_chip(p, core, near)
+    own_queries_at.bring((qs, gs), 0, 0)
+    far_codes = bring_far_keys(p, core, far, (ks, vs))
+    halo_codes = jnp.concatenate([far_codes, near_at.codes()], axis=0)
+    events = Events(p, 0, own_keys_at.codes(), halo_codes)
+
+    def stream(h):
+        q = qs[h]
+        gf = gs[h].astype(f32)
         here = slice(h * D, (h + 1) * D)
-        if r == 0:
-            message[here, :] = (state_in[here, :] + state).astype(bf16)
+        score = dot_t(q, ks[h])
+        if p.far:
+            start_state = far_ref[here, :]
         else:
-            state_out[here, :] = state
+            start_state = near_state[here, :] + halo_state(events, ks[h], vs[h], -B)
+            start_state = start_state.astype(bf16)
+        state_out[here, :] = start_state
+        yield
+        phi_q = feature(q.astype(f32)).astype(bf16)
+        from_start = dot(phi_q, start_state)
+        low = events.low(win_ref[core * p.all + h])
+        s_pos = lax.broadcasted_iota(jnp.int32, score.shape, 1) - B
+        score = jnp.where(s_pos >= low, score, MASKED) * c2
+        old = peak_in[h]
+        peak = jnp.maximum(old[:, 0:1], jnp.max(score, axis=1, keepdims=True))
+        e = jnp.exp2(score - peak)
+        yield
+        kept = jnp.exp2(old - peak)
+        total = total_in[h] * kept + jnp.sum(e, axis=1, keepdims=True)
+        window_out = (acc_in[h] * kept + dot(e.astype(bf16), vs[h])) / total
+        numerator = num_in[h] + jnp.where(events.reads, from_start, 0.0)
+        linear_out, grad_num = normalized(numerator, gf)
+        gn_out[h] = grad_num
+        yield
+        rowdot = jnp.sum(gf * window_out, axis=1, keepdims=True)
+        out[h] = (linear_out + window_out).astype(bf16)
+        opening = jnp.where(events.opening, phi_q, jnp.zeros_like(phi_q))
+        message[here, :] = (second_state[here, :] + t_dot(opening, grad_num)).astype(bf16)
+        lse = (peak + jnp.log2(total))[:, 0:1]
+        lse_out[h] = wide_column(lse)
+        rowdot_out[h] = wide_column(rowdot)
+        yield
+        put_stats(p, stat, h, lse, rowdot)
 
     drive(stream(h) for h in range(p.all))
-
-    if r == 0:
-        divide(core, (out, second), keep, send)
-    values = stat[...]
-    used = 2 * p.all * p.code_rows
-    if used < p.stat_rows:
-        inside = lax.broadcasted_iota(jnp.int32, values.shape, 0) < used
-        values = jnp.where(inside, values, 0.0)
+    values = stat_values(p, stat)
     stats_out[...] = values
-    if r == 0:
-        for tile, values in enumerate((values, stats_in[...])):
-            for n in range(3):
-                piece = values.astype(bf16)
-                at = p.state_rows + (3 * tile + n) * p.stat_rows
-                message[at : at + p.stat_rows, :] = piece
-                values = values - piece.astype(f32)
-
-
-def forward(p, r, core, windows, near, far, far_state, carried=()):
+    for tile, values in enumerate((values, second_stats[...])):
+        for n in range(3):
+            piece = values.astype(bf16)
+            at = p.state_rows + (3 * tile + n) * p.stat_rows
+            message[at : at + p.stat_rows, :] = piece
+            values = values - piece.astype(f32)
+
+
+def grad_body(p, core_ref, win_ref, *refs):
+    near, far, refs = refs[:5], refs[5 : 5 + p.far_refs], refs[5 + p.far_refs :]
+    (first_out, gn, lse_in, rowdot_in, state_in, second), refs = refs[:6], refs[6:]
+    keep, send, ks, vs, qs, gs, out = refs
+    core = core_ref[0]
+    L, B, D = p.length, p.before, p.width
+    scale, c2 = scales(p)
+    own_keys_at, own_queries_at = own_chip(p, core, near)
+    near_at = near_chip(p, core, near)
+    own_keys_at.bring((ks, vs), B, 0)
+    own_queries_at.bring((qs, gs), 0, 0)
+    near_at.bring((ks, vs), p.tail_fill)
+    far_codes = bring_far_keys(p, core, far, (ks, vs))
+    halo_codes = jnp.concatenate([far_codes, near_at.codes()], axis=0)
+    events = Events(p, 0, own_keys_at.codes(), halo_codes)
+
+    def stream(h):
+        q = qs[h]
+        score = dot_t(q, ks[h])
+        grad_prob = dot_t(gs[h], vs[h])
+        yield
+        grad_num = gn[h]
+        b = dot_t(grad_num, vs[h, B:, :])
+        from_start = dot_t(grad_num, state_in[h * D : (h + 1) * D, :])
+        yield
+        low = events.low(win_ref[core * p.all + h])
+        score = masked(events, score, low, -B)
+        prob = jnp.exp2(score * c2 - lse_in[h][:, 0:1])
+        ds = (prob * (grad_prob - rowdot_in[h][:, 0:1])).astype(bf16)
+        yield
+        dq = dot(ds, ks[h]) * scale
+        phi_k = feature(ks[h, B:, :].astype(f32)).astype(bf16)
+        grad_phi_q = dot(similar(events, b), phi_k) + jnp.where(events.reads, from_start, 0.0)
+        yield
+        out[0, h] = first_out[h]
+        out[1, h] = (slope(q.astype(f32)) * grad_phi_q + dq).astype(bf16)
+
+    drive(stream(h) for h in range(p.all))
+    divide(core, (out, second), keep, send)
+
+
+def query_side(p, core, windows, near, far, far_state, near_queries, far_queries):
     vmem = pl.BlockSpec(memory_space=pltpu.VMEM)
     smem = pl.BlockSpec(memory_space=pltpu.SMEM)
-    both = jax.ShapeDtypeStruct((2, p.all, p.length, p.width), bf16)
-    outs = [both] * (2 - r)
-    outs += [
-        jax.ShapeDtypeStruct((p.all, p.length, p.width), bf16),
-        jax.ShapeDtypeStruct((p.stat_rows, p.width), f32),
-    ]
-    if r == 0:
-        outs.append(jax.ShapeDtypeStruct((p.state_rows + 6 * p.stat_rows, p.width), bf16))
-    else:
-        outs.append(jax.ShapeDtypeStruct((p.state_rows, p.width), f32))
-    args = list(near)
-    if r == 0 or not p.merged:
-        args += far
-    if p.far:
-        args.append(far_state)
-    args += carried
-    span = pltpu.VMEM((p.all, p.before + p.chip, p.width), bf16)
-    tile = pltpu.VMEM((p.all, p.length, p.width), bf16)
-    return pl.pallas_call(
-        functools.partial(forward_body, p, r),
-        out_shape=outs,
-        in_specs=[smem, smem] + [vmem] * len(args),
-        out_specs=[vmem] * len(outs),
-        scratch_shapes=[span, span, tile, tile, pltpu.VMEM((p.stat_rows, p.width), f32)]
-        + ([pltpu.VMEM(both.shape, bf16)] if r == 0 else []),
-        **params(5.7),
-        name="forward",
-    )(core, windows, *args)
+
+    def kernel(body, micros, args, outs, scratch):
+        return pl.pallas_call(
+            functools.partial(body, p),
+            out_shape=[jax.ShapeDtypeStruct(shape, kind) for shape, kind in outs],
+            in_specs=[smem, smem] + [vmem] * len(args),
+            out_specs=[vmem] * len(outs),
+            scratch_shapes=[pltpu.VMEM(shape, kind) for shape, kind in scratch],
+            **params(micros),
+            name=body.__name__,
+        )(core, windows, *args)
+
+    tile = (p.all, p.length, p.width)
+    both = (2, *tile)
+    stats = ((p.stat_rows, p.width), f32)
+    state = (p.state_rows, p.width)
+    rows = [(tile, bf16)] * 2
+    far_state = [far_state] if p.far else []
+
+    def keys(n):
+        return [((p.all, n, p.width), bf16)] * 2
+
+    second, grad_1, stats_1, state_1 = kernel(
+        second_body,
+        5.7,
+        [*near, *(() if p.merged else far), *far_state],
+        [(both, bf16), (tile, bf16), stats, (state, f32)],
+        keys(p.before + p.chip) + rows + [stats],
+    )
+    begun = kernel(
+        start_body,
+        3.0,
+        near,
+        [(tile, f32)] * 2 + [((p.all, p.length, LANES), f32)] * 2 + [(state, f32)],
+        keys(p.chip + p.length) + rows,
+    )
+    state_1, *_ = lax.optimization_barrier((state_1, *near_queries))
+    first, grad_0, stats_0, lse, rowdot, start_state, message = kernel(
+        first_body,
+        2.0,
+        [*near, *far, *begun, state_1, stats_1, *far_state],
+        [(tile, bf16)] * 2
+        + [stats]
+        + [((p.all, p.length, LANES), f32)] * 2
+        + [(state, bf16), ((p.state_rows + 6 * p.stat_rows, p.width), bf16)],
+        keys(p.tail_fill) + rows + [stats],
+    )
+
+    def finish():
+        return kernel(
+            grad_body,
+            3.5,
+            [*near, *far, first, grad_0, lse, rowdot, start_state, second],
+            [(both, bf16)] * 2,
+            keys(p.before + p.length) + rows + [(both, bf16)],
+        )
+
+    return grad_1, stats_1, grad_0, stats_0, message, finish
 
 
 def stats_of(p, values, head):
@@ -553,7 +763,7 @@
 
 
 def later_body(p, core_ref, win_ref, *refs):
-    near, refs = refs[:7], refs[7:]
+    near, refs = refs[:5], refs[5:]
     far, refs = refs[: p.far_refs], refs[p.far_refs :]
     (message_1, message_2), sums, refs = refs[:2], (refs[2:4], refs[4:6]), refs[6:]
     if p.far:
@@ -565,21 +775,20 @@
     scale = 1.0 / math.sqrt(D)
     c2 = scale * math.log2(math.e)
     own_keys_at, _ = own_chip(p, core, near)
-    _, near_at = near_chips(p, core, near)
+    near_at = near_chip(p, core, near)
     own_keys_at.bring((ks, vs), 0)
     near_at.bring((qs, gs), 0)
     own_codes = own_keys_at.codes()
     near_codes = near_at.codes()
     if p.merged:
-        pick = (far[0], far[1])
-        far_codes = code_block(p, core, pick)
-        bring_tail(p, core, pick, (qs, gs), C)
+        far_codes = code_block(p, far[0])
+        bring_tail(p, far[0], (qs, gs), C)
         if p.tail < p.tail_fill:
             gap = p.tail_fill - p.tail
             qs[:, C + p.tail :, :] = jnp.zeros((p.all, gap, D), bf16)
             gs[:, C + p.tail :, :] = jnp.zeros((p.all, gap, D), bf16)
     else:
-        far_at = Chip(p, core, (far[1], far[0]), (far[2], far[3]))
+        far_at = Chip(p, core, *far)
         far_at.bring((qs, gs), C)
         far_codes = far_at.codes()
     after_codes = jnp.concatenate([near_codes, far_codes], axis=0)
@@ -728,30 +937,31 @@
         token_weights.reshape(-1, LANES),
         sessions.reshape(-1, LANES),
     )
-    for_pair, payloads, tails = packed[0], packed[1:5], packed[5:]
-
-    def exchange(payloads, by):
-        x1, x2, x3, x4 = payloads
+    for_pair, payloads = packed[0], packed[1:]
+
+    def exchange(same, cross, by):
         return (
-            move(x1, lambda c, i: (c + by, 0) if i == 0 else (c - by, 1)),
-            move(x2, lambda c, i: (c + by, 1) if i == 1 else (c - by, 0)),
-            move(x3, lambda c, i: (c + by, 1) if i == 0 else (c - by, 0)),
-            move(x4, lambda c, i: (c + by, 0) if i == 1 else (c - by, 1)),
+            move(same, lambda c, i: (c + by, i)),
+            move(cross, lambda c, i: (c + by, 1 - i)),
         )
 
     pair = move(for_pair, lambda c, i: (c, 1 - i))
-    got = exchange(payloads, 1)
+    kv_same, kv_cross, qg_same, qg_cross = payloads
+    near_keys = exchange(kv_same, kv_cross, 1)
+    near_queries = exchange(qg_same, qg_cross, -1)
     if p.merged:
-        tail_1, r1 = lax.optimization_barrier((tails[0], got[0]))
-        tail_2, r2 = lax.optimization_barrier((tails[1], got[1]))
-        got = (r1, r2, *got[2:])
-        far = (
-            move(tail_1, lambda c, i: (c + 2, 1) if i == 1 else (c - 2, 0)),
-            move(tail_2, lambda c, i: (c + 2, 0) if i == 1 else (c - 2, 1)),
-        )
+        last_keys, first_queries = make_tails(p, core, pair, kv_same, qg_same)
+        last_keys, key_part = lax.optimization_barrier((last_keys, near_keys[0]))
+        near_keys = (key_part, near_keys[1])
+        first_queries, query_part = lax.optimization_barrier((first_queries, near_queries[0]))
+        near_queries = (query_part, near_queries[1])
+        far_keys = (move(last_keys, lambda c, i: (c + 2, i)),)
+        far_queries = (move(first_queries, lambda c, i: (c - 2, i)),)
     else:
-        far = exchange(payloads, 2)
-    near = (pair, *payloads[:2], *got)
+        far_keys = exchange(kv_same, kv_cross, 2)
+        far_queries = exchange(qg_same, qg_cross, -2)
+    own = (pair, kv_same, qg_same)
+    near = (*own, *near_keys)
 
     far_before = far_after = None
     if p.far:
@@ -759,7 +969,7 @@
         chip_ends = jnp.stack([both[0, 0], both[1, -1]])
 
         total = jnp.zeros((p.all, p.width, p.width), f32)
-        keys_here = jnp.where(core_id == 0, payloads[0], payloads[1])[: p.rows - EXTRA]
+        keys_here = kv_same[: p.rows - EXTRA]
         keys_here = keys_here.reshape(2, p.all, L, p.width)
         keys_pair = pair[: p.pair_rows - EXTRA].reshape(4, p.all, L, p.width)[:2]
         for part, owner in ((keys_here, core_id), (keys_pair, 1 - core_id)):
@@ -771,10 +981,11 @@
             )
         far_before = folded(chip_ends, total.astype(bf16), False).reshape(-1, p.width)
 
-    queries_1, grad_1, stats_1, state_1 = forward(p, 1, core, window_size, near, far, far_before)
-    keep_q, send_q, grad_0, stats_0, message = forward(
-        p, 0, core, window_size, near, far, far_before, (state_1, stats_1, queries_1)
-    )
+    grad_1, stats_1, grad_0, stats_0, message, finish = query_side(
+        p, core, window_size, near, far_keys, far_before, near_queries, far_queries
+    )
+    message, grad_1 = lax.optimization_barrier((message, grad_1))
+    sums_1 = own_keys(p, 1, core, window_size, near, grad_1, stats_1)
     messages = (
         move(message, lambda c, i: (c - 1, i)),
         move(message, lambda c, i: (c - 2, i)),
@@ -782,10 +993,10 @@
     if p.far:
         state = message[: p.state_rows].reshape(p.all, p.width, p.width)
         far_after = folded(chip_ends, state, True).reshape(-1, p.width)
-    sums_1 = own_keys(p, 1, core, window_size, near, grad_1, stats_1)
+    keep_q, send_q = finish()
     sums_0 = own_keys(p, 0, core, window_size, near, grad_0, stats_0, sums_1)
     keep_k, send_k = later_keys(
-        p, core, window_size, near, far, messages, (*sums_0, *sums_1), far_after
+        p, core, window_size, (*own, *near_queries), far_queries, messages, (*sums_0, *sums_1), far_after
     )
     attended, grad_queries = unpack(p, core, keep_q, move(send_q, lambda c, i: (c, 1 - i)))
     grad_keys, grad_values = unpack(p, core, keep_k, move(send_k, lambda c, i: (c, 1 - i)))

time: 79 us -> 75.3 us (0.953)
  waiting for transfers between devices: 22.2 us -> 14 us
  Pallas kernels: 30.1 us -> 33.9 us
    ppermute x11, waiting for transfers between devices: 22.2 us -> 14 us  [move(): return lax.ppermute(x, AXES, pairs)]
    pallas_call x2 -> x5, Pallas kernels: 11.7 us -> 16.7 us  [the longest x4 16.7 us: kernel(): pl.pallas_call(functools.partial(body, p), out_shape=[jax.ShapeDtypeStruc...]
    pallas_call x1, Pallas kernels: 4.95 us -> 3.83 us  [pack(): pl.pallas_call(functools.partial(pack_body, p), out_shape=[jax.ShapeDtype...]
  transfers between devices with their start and end apart: 11 -> 11, of which waited for: 8 -> 5; matrix products, arithmetic and copies ran while one was open for 0% -> 0% of each run, Pallas kernels for 23% -> 39%
where the time goes in v4:
time: 75.3 us; the launch traced here: 74.4 us
  Pallas kernels  33.9 us (45%)
  starting transfers between devices  23.5 us (31%)
  waiting for transfers between devices  14 us (19%)
  local copies, waits for them, and re-layouts  2.09 us (3%)
  between operations  0.83 us (1%)
    ppermute x11, starting transfers between devices, move(): return lax.ppermute(x, AXES, pairs)  23.5 us
    pallas_call x4, Pallas kernels, kernel(): pl.pallas_call(functools.partial(body, p), out_shape=[jax.ShapeDtypeStruc...  16.7 us
    ppermute x11, waiting for transfers between devices, move(): return lax.ppermute(x, AXES, pairs)  14 us
    pallas_call x2, Pallas kernels, own_keys(): pl.pallas_call(functools.partial(own_body, p, r), out_shape=[full, full],...  5.64 us
    pallas_call x1, Pallas kernels, later_keys(): pl.pallas_call(functools.partial(later_body, p), out_shape=[both, both],...  5.02 us
    pallas_call x1, Pallas kernels, pack(): pl.pallas_call(functools.partial(pack_body, p), out_shape=[jax.ShapeDtype...  3.83 us
    pallas_call x2, Pallas kernels, unpack(): pl.pallas_call(functools.partial(unpack_body, p), out_shape=[out, out], i...  2.68 us
    unnamed x6, local copies, waits for them, and re-layouts  2.09 us
  transfers between devices with their start and end apart: 11, of which 5 were waited for; matrix products, arithmetic and copies ran while one was open for 0% of the time, Pallas kernels for 39%

profile of v4, /device:TPU:9, one launch (start us, length us, event | category | flops | bytes accessed | tf_op | source)
XLA Modules:
  0.0 74.4 jit_solution(13958435605409277406)
XLA Ops:
  0.6 3.8 %pack.1 = (bf16[4112,128]{1,0:T(8,128)(2,1)}, bf16[2064,128]{1,0:T(8,128)(2,1)}, bf16[2064,128]{1,0:T(8,128)(2,1)}, bf16[2064,128]{1,0:T(8,128)(2,1)}, bf16[2064,128]{1,0:T(8,128)(2,1)}) custom-call(s32[1]{0:T(128)} %bitcast.core_ref, bf16[256,8,128]{2,1,0:T(8,128)(2,1)} %q_ref.1, bf16[256,8,128]{2,1,0:T(8,128)(2,1)} %k_ref.1, bf16[256,8,128]{2,1,0:T(8,128)(2,1)} %v_ref.1, ...), custom_call_target="tpu_custom_call" | custom-call | tf_op jit(solution)/shard_map/pack/pallas_call | solution.py:158
  5.2 3.2 %collective-permute-start.1 = (bf16[2064,128]{1,0:T(8,128)(2,1)}, bf16[2064,128]{1,0:T(8,128)(2,1)S(1)}, u32[]{:S(2)}, u32[]{:S(2)}) collective-permute-start(bf16[2064,128]{1,0:T(8,128)(2,1)} %get-tuple-element.47.own_keys.refs_1_), channel_id=1, source_target_pairs={{0,4},{1,5},{4,8},{5,9},{8,12},{9,13},{2,6},{3,7},{6,10},{7,11},{1... | collective-permute-start | bytes 1585160 | tf_op jit(solution)/shard_map/ppermute | solution.py:928
  8.4 2.1 %collective-permute-start.4 = (bf16[2064,128]{1,0:T(8,128)(2,1)}, bf16[2064,128]{1,0:T(8,128)(2,1)S(1)}, u32[]{:S(2)}, u32[]{:S(2)}) collective-permute-start(bf16[2064,128]{1,0:T(8,128)(2,1)} %get-tuple-element.48.own_queries.refs_2_), channel_id=1, source_target_pairs={{4,0},{5,1},{8,4},{9,5},{12,8},{13,9},{6,2},{7,3},{10,6},{11,7},{1... | collective-permute-start | bytes 1585160 | tf_op jit(solution)/shard_map/ppermute | solution.py:928
  10.5 3.6 %collective-permute-start.2 = (bf16[2064,128]{1,0:T(8,128)(2,1)}, bf16[2064,128]{1,0:T(8,128)(2,1)S(1)}, u32[]{:S(2)}, u32[]{:S(2)}) collective-permute-start(bf16[2064,128]{1,0:T(8,128)(2,1)} %get-tuple-element.51), channel_id=1, source_target_pairs={{0,5},{1,4},{4,9},{5,8},{8,13},{9,12},{2,7},{3,6},{6,11},{7,10},{1... | collective-permute-start | bytes 1585160 | tf_op jit(solution)/shard_map/ppermute | solution.py:928
  14.2 1.9 %collective-permute-start.5 = (bf16[2064,128]{1,0:T(8,128)(2,1)}, bf16[2064,128]{1,0:T(8,128)(2,1)S(1)}, u32[]{:S(2)}, u32[]{:S(2)}) collective-permute-start(bf16[2064,128]{1,0:T(8,128)(2,1)} %get-tuple-element.61), channel_id=1, source_target_pairs={{4,1},{5,0},{8,5},{9,4},{12,9},{13,8},{6,3},{7,2},{10,7},{11,6},{1... | collective-permute-start | bytes 1585160 | tf_op jit(solution)/shard_map/ppermute | solution.py:928
  17.2 1.0 %copy-done.1 = bf16[2064,128]{1,0:T(8,128)(2,1)S(1)} copy-done((bf16[2064,128]{1,0:T(8,128)(2,1)S(1)}, bf16[2064,128]{1,0:T(8,128)(2,1)}, u32[]{:S(2)}) %copy-start.1) | copy-done | bytes 528408
  18.3 2.6 %collective-permute-done.1.refs_3_ = bf16[2064,128]{1,0:T(8,128)(2,1)S(1)} collective-permute-done((bf16[2064,128]{1,0:T(8,128)(2,1)}, bf16[2064,128]{1,0:T(8,128)(2,1)S(1)}, u32[]{:S(2)}, u32[]{:S(2)}) %collective-permute-start.1) | collective-permute-done | bytes 528416 | tf_op jit(solution)/shard_map/ppermute | solution.py:928
  20.9 2.9 %collective-permute-done.4.refs_3_ = bf16[2064,128]{1,0:T(8,128)(2,1)S(1)} collective-permute-done((bf16[2064,128]{1,0:T(8,128)(2,1)}, bf16[2064,128]{1,0:T(8,128)(2,1)S(1)}, u32[]{:S(2)}, u32[]{:S(2)}) %collective-permute-start.4) | collective-permute-done | bytes 528416 | tf_op jit(solution)/shard_map/ppermute | solution.py:928
  23.8 1.3 %collective-permute-start.7 = (bf16[1424,128]{1,0:T(8,128)(2,1)S(1)}, bf16[1424,128]{1,0:T(8,128)(2,1)S(1)}, u32[]{:S(2)}, u32[]{:S(2)}) collective-permute-start(bf16[1424,128]{1,0:T(8,128)(2,1)S(1)} %get-tuple-element.74), channel_id=1, source_target_pairs={{8,0},{9,1},{12,4},{13,5},{10,2},{11,3},{14,6},{15,7},{24,16},{25,... | collective-permute-start | bytes 1093640 | tf_op jit(solution)/shard_map/ppermute | solution.py:928
  25.1 4.9 %collective-permute-start.3 = (bf16[1424,128]{1,0:T(8,128)(2,1)S(1)}, bf16[1424,128]{1,0:T(8,128)(2,1)S(1)}, u32[]{:S(2)}, u32[]{:S(2)}) collective-permute-start(bf16[1424,128]{1,0:T(8,128)(2,1)S(1)} %get-tuple-element.52), channel_id=1, source_target_pairs={{0,8},{1,9},{4,12},{5,13},{2,10},{3,11},{6,14},{7,15},{16,24},{17,... | collective-permute-start | bytes 1093640 | tf_op jit(solution)/shard_map/ppermute | solution.py:928
  30.0 3.0 %collective-permute-done.2.refs_4_ = bf16[2064,128]{1,0:T(8,128)(2,1)S(1)} collective-permute-done((bf16[2064,128]{1,0:T(8,128)(2,1)}, bf16[2064,128]{1,0:T(8,128)(2,1)S(1)}, u32[]{:S(2)}, u32[]{:S(2)}) %collective-permute-start.2) | collective-permute-done | bytes 528416 | tf_op jit(solution)/shard_map/ppermute | solution.py:928
  33.1 5.9 %second_body.1 = (bf16[2,4,256,128]{3,2,1,0:T(8,128)(2,1)S(1)}, bf16[4,256,128]{2,1,0:T(8,128)(2,1)S(1)}, f32[16,128]{1,0:T(8,128)S(1)}, f32[512,128]{1,0:T(8,128)S(1)}) custom-call(s32[1]{0:T(128)} %bitcast.core_ref, s32[8]{0:T(128)S(1)} %copy-done.2, bf16[4112,128]{1,0:T(8,128)(2,1)S(1)} %collective-permute-done.pair.refs_0_, ...), custom_call_target="tpu_custom_call" | custom-call | flops 6554999808 | bytes 5700000 | tf_op jit(solution)/shard_map/second_body/pallas_call | solution.py:611
  38.9 3.1 %start_body.1 = (f32[4,256,128]{2,1,0:T(8,128)S(1)}, f32[4,256,128]{2,1,0:T(8,128)S(1)}, f32[4,256,128]{2,1,0:T(8,128)S(1)}, f32[4,256,128]{2,1,0:T(8,128)S(1)}, f32[512,128]{1,0:T(8,128)S(1)}) custom-call(s32[1]{0:T(128)} %bitcast.core_ref, s32[8]{0:T(128)S(1)} %copy-done.2, bf16[4112,128]{1,0:T(8,128)(2,1)S(1)} %collective-permute-done.pair.refs_0_, ...), custom_call_target="tpu_custom_call" | custom-call | flops 3449999872 | bytes 3000000 | tf_op jit(solution)/shard_map/start_body/pallas_call | solution.py:611
  42.0 4.9 %collective-permute-done.3.refs_5_ = bf16[1424,128]{1,0:T(8,128)(2,1)S(1)} collective-permute-done((bf16[1424,128]{1,0:T(8,128)(2,1)S(1)}, bf16[1424,128]{1,0:T(8,128)(2,1)S(1)}, u32[]{:S(2)}, u32[]{:S(2)}) %collective-permute-start.3) | collective-permute-done | bytes 364576 | tf_op jit(solution)/shard_map/ppermute | solution.py:928
  47.0 4.3 %first_body.1 = (bf16[4,256,128]{2,1,0:T(8,128)(2,1)S(1)}, bf16[4,256,128]{2,1,0:T(8,128)(2,1)S(1)}, f32[16,128]{1,0:T(8,128)S(1)}, f32[4,256,128]{2,1,0:T(8,128...) custom-call(s32[1]{0:T(128)} %bitcast.core_ref, s32[8]{0:T(128)S(1)} %copy-done.2, ...), custom_call_target="tpu_custom_call" | custom-call | flops 2300000000 | bytes 2000000 | tf_op jit(solution)/shard_map/first_body/pallas_call | solution.py:611
  51.3 1.3 %collective-permute-start.9 = (bf16[608,128]{1,0:T(8,128)(2,1)S(1)}, bf16[608,128]{1,0:T(8,128)(2,1)S(1)}, u32[]{:S(2)}, u32[]{:S(2)}) collective-permute-start(bf16[608,128]{1,0:T(8,128)(2,1)S(1)} %get-tuple-element.77), channel_id=1, source_target_pairs={{8,0},{9,1},{12,4},{13,5},{10,2},{11,3},{14,6},{15,7},{24,16},{25,... | collective-permute-start | bytes 466952 | tf_op jit(solution)/shard_map/ppermute | solution.py:928
  52.6 1.9 %collective-permute-start.8 = (bf16[608,128]{1,0:T(8,128)(2,1)S(1)}, bf16[608,128]{1,0:T(8,128)(2,1)S(1)}, u32[]{:S(2)}, u32[]{:S(2)}) collective-permute-start(bf16[608,128]{1,0:T(8,128)(2,1)S(1)} %get-tuple-element.77), channel_id=1, source_target_pairs={{4,0},{5,1},{8,4},{9,5},{12,8},{13,9},{6,2},{7,3},{10,6},{11,7},{1... | collective-permute-start | bytes 466952 | tf_op jit(solution)/shard_map/ppermute | solution.py:928
  54.5 3.4 %grad_body.1 = (bf16[2,4,256,128]{3,2,1,0:T(8,128)(2,1)S(1)}, bf16[2,4,256,128]{3,2,1,0:T(8,128)(2,1)S(1)}) custom-call(s32[1]{0:T(128)} %bitcast.core_ref, s32[8]{0:T(128)S(1)} %copy-done.2, bf16[4112,128]{1,0:T(8,128)(2,1)S(1)} %collective-permute-done.pair.refs_0_, bf16[2064,128]{1,0:T(8,128)(2,1)S(1)} %copy-done, bf16[2064,128]{1,0:T(8,128)(2,1)S(1)} %copy-done.1, ...), custom_call_target="tpu_custom_call" | custom-call | flops 4024999936 | bytes 3500000 | tf_op jit(solution)/shard_map/grad_body/pallas_call | solution.py:611
  57.9 2.4 %collective-permute-start.6 = (bf16[2,4,256,128]{3,2,1,0:T(8,128)(2,1)S(1)}, bf16[2,4,256,128]{3,2,1,0:T(8,128)(2,1)S(1)}, u32[]{:S(2)}, u32[]{:S(2)}) collective-permute-start(bf16[2,4,256,128]{3,2,1,0:T(8,128)(2,1)S(1)} %get-tuple-element.71), channel_id=1, source_target_pairs={{0,1},{1,0},{4,5},{5,4},{8,9},{9,8},{12,13},{13,12},{2,3},{3,2},{6... | collective-permute-start | bytes 1572872 | tf_op jit(solution)/shard_map/ppermute | solution.py:928
  60.4 3.5 %own_keys.2 = (f32[4,512,128]{2,1,0:T(8,128)S(1)}, f32[4,512,128]{2,1,0:T(8,128)S(1)}) custom-call(s32[1]{0:T(128)} %bitcast.core_ref, s32[8]{0:T(128)S(1)} %copy-done.2, bf16[4112,128]{1,0:T(8,128)(2,1)S(1)} %collective-permute-done.pair.refs_0_, bf16[2064,128]{1,0:T(8,128)(2,1)S(1)} %copy-done, bf16[2064,128]{1,0:T(8,128)(2,1)S(1)} %copy-done.1, ...), custom_call_target="tpu_custom_call" | custom-call | flops 4600000000 | bytes 4000000 | tf_op jit(solution)/shard_map/own_keys/pallas_call | solution.py:754
  63.8 2.2 %own_keys.3 = (f32[4,256,128]{2,1,0:T(8,128)S(1)}, f32[4,256,128]{2,1,0:T(8,128)S(1)}) custom-call(s32[1]{0:T(128)} %bitcast.core_ref, s32[8]{0:T(128)S(1)} %copy-done.2, bf16[4112,128]{1,0:T(8,128)(2,1)S(1)} %collective-permute-done.pair.refs_0_, bf16[2064,128]{1,0:T(8,128)(2,1)S(1)} %copy-done, bf16[2064,128]{1,0:T(8,128)(2,1)S(1)} %copy-done.1, ...), custom_call_target="tpu_custom_call" | custom-call | flops 2300000000 | bytes 2000000 | tf_op jit(solution)/shard_map/own_keys/pallas_call | solution.py:754
  66.0 5.0 %later_keys.1 = (bf16[2,4,256,128]{3,2,1,0:T(8,128)(2,1)S(1)}, bf16[2,4,256,128]{3,2,1,0:T(8,128)(2,1)S(1)}) custom-call(s32[1]{0:T(128)} %bitcast.core_ref, s32[8]{0:T(128)S(1)} %copy-done.2, bf16[4112,128]{1,0:T(8,128)(2,1)S(1)} %collective-permute-done.pair.refs_0_, bf16[2064,128]{1,0:T(8,128)(2,1)S(1)} %copy-done, bf16[2064,128]{1,0:T(8,128)(2,1)S(1)} %copy-done.1, ...), custom_call_target="tpu_custom_call" | custom-call | flops 6325000192 | bytes 5500000 | tf_op jit(solution)/shard_map/later_keys/pallas_call | solution.py:860
  71.1 1.3 %unpack.2 = (bf16[256,8,128]{2,1,0:T(8,128)(2,1)}, bf16[256,8,128]{2,1,0:T(8,128)(2,1)}) custom-call(s32[1]{0:T(128)} %bitcast.core_ref, bf16[2,4,256,128]{3,2,1,0:T(8,128)(2,1)S(1)} %get-tuple-element.70.mine, bf16[2,4,256,128]{3,2,1,0:T(8,128)(2,1)S(1)} %collective-permute-done.6.theirs), custom_call_target="tpu_custom_call" | custom-call | flops 1610000000 | bytes 1400000 | tf_op jit(solution)/shard_map/unpack/pallas_call | solution.py:884
  73.0 1.3 %unpack.3 = (bf16[256,8,128]{2,1,0:T(8,128)(2,1)}, bf16[256,8,128]{2,1,0:T(8,128)(2,1)}) custom-call(s32[1]{0:T(128)} %bitcast.core_ref, bf16[2,4,256,128]{3,2,1,0:T(8,128)(2,1)S(1)} %get-tuple-element.84.mine, bf16[2,4,256,128]{3,2,1,0:T(8,128)(2,1)S(1)} %collective-permute-done.10.theirs), custom_call_target="tpu_custom_call" | custom-call | flops 1610000000 | bytes 1400000 | tf_op jit(solution)/shard_map/unpack/pallas_call | solution.py:884
  (15 shorter events, 2.5 us)
Async XLA Ops:
  4.5 11.7 %collective-permute-start = (bf16[4112,128]{1,0:T(8,128)(2,1)}, bf16[4112,128]{1,0:T(8,128)(2,1)S(1)}, u32[]{:S(2)}, u32[]{:S(2)}) collective-permute-start(bf16[4112,128]{1,0:T(8,128)(2,1)} %get-tuple-element.46), channel_id=1, source_target_pairs={{0,1},{1,0},{4,5},{5,4},{8,9},{9,8},{12,13},{13,12},{2,3},{3,2},{6... | collective-permute-start | bytes 3158024 | tf_op jit(solution)/shard_map/ppermute | solution.py:928
  5.2 15.7 %collective-permute-start.1 = (bf16[2064,128]{1,0:T(8,128)(2,1)}, bf16[2064,128]{1,0:T(8,128)(2,1)S(1)}, u32[]{:S(2)}, u32[]{:S(2)}) collective-permute-start(bf16[2064,128]{1,0:T(8,128)(2,1)} %get-tuple-element.47.own_keys.refs_1_), channel_id=1, source_target_pairs={{0,4},{1,5},{4,8},{5,9},{8,12},{9,13},{2,6},{3,7},{6,10},{7,11},{1... | collective-permute-start | bytes 1585160 | tf_op jit(solution)/shard_map/ppermute | solution.py:928
  8.4 15.4 %collective-permute-start.4 = (bf16[2064,128]{1,0:T(8,128)(2,1)}, bf16[2064,128]{1,0:T(8,128)(2,1)S(1)}, u32[]{:S(2)}, u32[]{:S(2)}) collective-permute-start(bf16[2064,128]{1,0:T(8,128)(2,1)} %get-tuple-element.48.own_queries.refs_2_), channel_id=1, source_target_pairs={{4,0},{5,1},{8,4},{9,5},{12,8},{13,9},{6,2},{7,3},{10,6},{11,7},{1... | collective-permute-start | bytes 1585160 | tf_op jit(solution)/shard_map/ppermute | solution.py:928
  10.5 22.5 %collective-permute-start.2 = (bf16[2064,128]{1,0:T(8,128)(2,1)}, bf16[2064,128]{1,0:T(8,128)(2,1)S(1)}, u32[]{:S(2)}, u32[]{:S(2)}) collective-permute-start(bf16[2064,128]{1,0:T(8,128)(2,1)} %get-tuple-element.51), channel_id=1, source_target_pairs={{0,5},{1,4},{4,9},{5,8},{8,13},{9,12},{2,7},{3,6},{6,11},{7,10},{1... | collective-permute-start | bytes 1585160 | tf_op jit(solution)/shard_map/ppermute | solution.py:928
  14.2 18.9 %copy-start.2 = (s32[8]{0:T(128)S(1)}, s32[8]{0:T(128)}, u32[]{:S(2)}) copy-start(s32[8]{0:T(128)} %win_ref.13) | copy-start | bytes 100
  14.2 24.7 %collective-permute-start.5 = (bf16[2064,128]{1,0:T(8,128)(2,1)}, bf16[2064,128]{1,0:T(8,128)(2,1)S(1)}, u32[]{:S(2)}, u32[]{:S(2)}) collective-permute-start(bf16[2064,128]{1,0:T(8,128)(2,1)} %get-tuple-element.61), channel_id=1, source_target_pairs={{4,1},{5,0},{8,5},{9,4},{12,9},{13,8},{6,3},{7,2},{10,7},{11,6},{1... | collective-permute-start | bytes 1585160 | tf_op jit(solution)/shard_map/ppermute | solution.py:928
  16.2 1.0 %copy-start = (bf16[2064,128]{1,0:T(8,128)(2,1)S(1)}, bf16[2064,128]{1,0:T(8,128)(2,1)}, u32[]{:S(2)}) copy-start(bf16[2064,128]{1,0:T(8,128)(2,1)} %get-tuple-element.47.own_keys.refs_1_) | copy-start | bytes 1585156
  17.2 1.0 %copy-start.1 = (bf16[2064,128]{1,0:T(8,128)(2,1)S(1)}, bf16[2064,128]{1,0:T(8,128)(2,1)}, u32[]{:S(2)}) copy-start(bf16[2064,128]{1,0:T(8,128)(2,1)} %get-tuple-element.48.own_queries.refs_2_) | copy-start | bytes 1585156
  23.8 42.2 %collective-permute-start.7 = (bf16[1424,128]{1,0:T(8,128)(2,1)S(1)}, bf16[1424,128]{1,0:T(8,128)(2,1)S(1)}, u32[]{:S(2)}, u32[]{:S(2)}) collective-permute-start(bf16[1424,128]{1,0:T(8,128)(2,1)S(1)} %get-tuple-element.74), channel_id=1, source_target_pairs={{8,0},{9,1},{12,4},{13,5},{10,2},{11,3},{14,6},{15,7},{24,16},{25,... | collective-permute-start | bytes 1093640 | tf_op jit(solution)/shard_map/ppermute | solution.py:928
  25.1 21.9 %collective-permute-start.3 = (bf16[1424,128]{1,0:T(8,128)(2,1)S(1)}, bf16[1424,128]{1,0:T(8,128)(2,1)S(1)}, u32[]{:S(2)}, u32[]{:S(2)}) collective-permute-start(bf16[1424,128]{1,0:T(8,128)(2,1)S(1)} %get-tuple-element.52), channel_id=1, source_target_pairs={{0,8},{1,9},{4,12},{5,13},{2,10},{3,11},{6,14},{7,15},{16,24},{17,... | collective-permute-start | bytes 1093640 | tf_op jit(solution)/shard_map/ppermute | solution.py:928
  51.3 14.7 %collective-permute-start.9 = (bf16[608,128]{1,0:T(8,128)(2,1)S(1)}, bf16[608,128]{1,0:T(8,128)(2,1)S(1)}, u32[]{:S(2)}, u32[]{:S(2)}) collective-permute-start(bf16[608,128]{1,0:T(8,128)(2,1)S(1)} %get-tuple-element.77), channel_id=1, source_target_pairs={{8,0},{9,1},{12,4},{13,5},{10,2},{11,3},{14,6},{15,7},{24,16},{25,... | collective-permute-start | bytes 466952 | tf_op jit(solution)/shard_map/ppermute | solution.py:928
  52.6 13.4 %collective-permute-start.8 = (bf16[608,128]{1,0:T(8,128)(2,1)S(1)}, bf16[608,128]{1,0:T(8,128)(2,1)S(1)}, u32[]{:S(2)}, u32[]{:S(2)}) collective-permute-start(bf16[608,128]{1,0:T(8,128)(2,1)S(1)} %get-tuple-element.77), channel_id=1, source_target_pairs={{4,0},{5,1},{8,4},{9,5},{12,8},{13,9},{6,2},{7,3},{10,6},{11,7},{1... | collective-permute-start | bytes 466952 | tf_op jit(solution)/shard_map/ppermute | solution.py:928
  57.9 13.2 %collective-permute-start.6 = (bf16[2,4,256,128]{3,2,1,0:T(8,128)(2,1)S(1)}, bf16[2,4,256,128]{3,2,1,0:T(8,128)(2,1)S(1)}, u32[]{:S(2)}, u32[]{:S(2)}) collective-permute-start(bf16[2,4,256,128]{3,2,1,0:T(8,128)(2,1)S(1)} %get-tuple-element.71), channel_id=1, source_target_pairs={{0,1},{1,0},{4,5},{5,4},{8,9},{9,8},{12,13},{13,12},{2,3},{3,2},{6... | collective-permute-start | bytes 1572872 | tf_op jit(solution)/shard_map/ppermute | solution.py:928
  71.1 2.0 %collective-permute-start.10 = (bf16[2,4,256,128]{3,2,1,0:T(8,128)(2,1)S(1)}, bf16[2,4,256,128]{3,2,1,0:T(8,128)(2,1)S(1)}, u32[]{:S(2)}, u32[]{:S(2)}) collective-permute-start(bf16[2,4,256,128]{3,2,1,0:T(8,128)(2,1)S(1)} %get-tuple-element.85), channel_id=1, source_target_pairs={{0,1},{1,0},{4,5},{5,4},{8,9},{9,8},{12,13},{13,12},{2,3},{3,2},{6... | collective-permute-start | bytes 1572872 | tf_op jit(solution)/shard_map/ppermute | solution.py:928

commit v5 on v4

--- a/solution.py
+++ b/solution.py
@@ -15,7 +15,7 @@
 AXES = ("ctx", "pair")
 EXTRA = 16
 LANES = 128
-VMEM_LIMIT = 20 << 20
+VMEM_LIMIT = 28 << 20
 
 f32 = jnp.float32
 bf16 = jnp.bfloat16
@@ -387,26 +387,29 @@
         far, refs = refs[: p.far_refs], refs[p.far_refs :]
     if p.far:
         far_ref, refs = refs[0], refs[1:]
-    out, gn_out, stats_out, state_out, ks, vs, qs, gs, stat = refs
+    (out, gn_out, stats_out, state_out), refs = refs[:4], refs[4:]
+    acc_out, num_out, peak_out, total_out, near_out, ks, vs, qs, gs, stat = refs
     core = core_ref[0]
     L, C, B, D = p.length, p.chip, p.before, p.width
     scale, c2 = scales(p)
     own_keys_at, own_queries_at = own_chip(p, core, near)
     near_at = near_chip(p, core, near)
     own_keys_at.bring((ks, vs), B)
-    own_queries_at.bring((qs, gs), 0, 1)
+    own_queries_at.bring((qs, gs), 0)
     near_at.bring((ks, vs), p.tail_fill)
+    own_codes = own_keys_at.codes()
     halo_codes = near_at.codes()
+    events_0 = Events(p, 0, own_codes, halo_codes)
     begin = p.tail_fill
     if not p.merged:
         far_codes = bring_far_keys(p, core, far, (ks, vs))
         halo_codes = jnp.concatenate([far_codes, halo_codes], axis=0)
         begin = 0
-    events = Events(p, 1, own_keys_at.codes(), halo_codes)
+    events = Events(p, 1, own_codes, halo_codes)
 
     def stream(h):
-        q = qs[h]
-        g = gs[h]
+        q = qs[h, L:, :]
+        g = gs[h, L:, :]
         gf = g.astype(f32)
         qf = q.astype(f32)
         k_part = ks[h, begin:, :]
@@ -454,45 +457,29 @@
         )
         out[1, h] = (slope(qf) * grad_phi_q + dq).astype(bf16)
 
-    drive(stream(h) for h in range(p.all))
-    stats_out[...] = stat_values(p, stat)
-
-
-def start_body(p, core_ref, win_ref, *refs):
-    near, refs = refs[:5], refs[5:]
-    acc_out, num_out, peak_out, total_out, state_out, ks, vs, qs, gs = refs
-    core = core_ref[0]
-    L, C, D = p.length, p.chip, p.width
-    scale, c2 = scales(p)
-    own_keys_at, own_queries_at = own_chip(p, core, near)
-    near_at = near_chip(p, core, near)
-    own_keys_at.bring((ks, vs), C, 0)
-    own_queries_at.bring((qs, gs), 0, 0)
-    near_at.bring((ks, vs), 0)
-    events = Events(p, 0, own_keys_at.codes(), near_at.codes())
-
-    def stream(h):
-        q = qs[h]
-        score = dot_t(q, ks[h])
+    def start_stream(h):
+        q = qs[h, :L, :]
+        k = ks[h, p.tail_fill : B + L, :]
+        v = vs[h, p.tail_fill : B + L, :]
+        score = dot_t(q, k)
         yield
         phi_q = feature(q.astype(f32)).astype(bf16)
-        a = dot_t(phi_q, feature(ks[h, C:, :].astype(f32)).astype(bf16))
+        a = dot_t(phi_q, feature(k[C:].astype(f32)).astype(bf16))
         if not p.far:
-            state_out[h * D : (h + 1) * D, :] = halo_state(
-                events, ks[h, :C, :], vs[h, :C, :], -C
-            )
-        yield
-        low = events.low(win_ref[core * p.all + h])
-        score = masked(events, score, low, -C)
+            near_out[h * D : (h + 1) * D, :] = halo_state(events_0, k[:C], v[:C], -C)
+        yield
+        low = events_0.low(win_ref[core * p.all + h])
+        score = masked(events_0, score, low, -C)
         peak = jnp.max(score, axis=1, keepdims=True) * c2
         e = jnp.exp2(score * c2 - peak)
         peak_out[h] = wide_column(peak)
         total_out[h] = wide_column(jnp.sum(e, axis=1, keepdims=True))
         yield
-        acc_out[h] = dot(e.astype(bf16), vs[h])
-        num_out[h] = dot(similar(events, a), vs[h, C:, :])
-
-    drive(stream(h) for h in range(p.all))
+        acc_out[h] = dot(e.astype(bf16), v)
+        num_out[h] = dot(similar(events_0, a), v[C:])
+
+    drive([stream(h) for h in range(p.all)] + [start_stream(h) for h in range(p.all)])
+    stats_out[...] = stat_values(p, stat)
 
 
 def first_body(p, core_ref, win_ref, *refs):
@@ -628,19 +615,15 @@
     def keys(n):
         return [((p.all, n, p.width), bf16)] * 2
 
-    second, grad_1, stats_1, state_1 = kernel(
+    second, grad_1, stats_1, state_1, *begun = kernel(
         second_body,
-        5.7,
+        8.0,
         [*near, *(() if p.merged else far), *far_state],
-        [(both, bf16), (tile, bf16), stats, (state, f32)],
-        keys(p.before + p.chip) + rows + [stats],
-    )
-    begun = kernel(
-        start_body,
-        3.0,
-        near,
-        [(tile, f32)] * 2 + [((p.all, p.length, LANES), f32)] * 2 + [(state, f32)],
-        keys(p.chip + p.length) + rows,
+        [(both, bf16), (tile, bf16), stats, (state, f32)]
+        + [(tile, f32)] * 2
+        + [((p.all, p.length, LANES), f32)] * 2
+        + [(state, f32)],
+        keys(p.before + p.chip) + keys(p.chip) + [stats],
     )
     state_1, *_ = lax.optimization_barrier((state_1, *near_queries))
     first, grad_0, stats_0, lse, rowdot, start_state, message = kernel(
@@ -682,10 +665,8 @@
     return total
 
 
-def own_body(p, r, core_ref, win_ref, *refs):
-    near, (gn, stats_in), refs = refs[:3], refs[3:5], refs[5:]
-    if r == 0:
-        (dk_i, dv_i), refs = refs[:2], refs[2:]
+def own_body(p, core_ref, win_ref, *refs):
+    near, grads, stats_in, refs = refs[:3], refs[3:5], refs[5:7], refs[7:]
     dk_o, dv_o, ks, vs, qs, gs = refs
     core = core_ref[0]
     L, C, D = p.length, p.chip, p.width
@@ -693,27 +674,28 @@
     c2 = scale * math.log2(math.e)
     own_keys_at, own_queries_at = own_chip(p, core, near)
     own_keys_at.bring((ks, vs), 0)
-    own_queries_at.bring((qs, gs), 0, r)
+    own_queries_at.bring((qs, gs), 0)
     own_codes = own_keys_at.codes()
     code = column_of(own_codes)
     hi_all = jnp.zeros((C, 1), f32)
     for n in range(1, SESSIONS + 1):
         hi_all = jnp.where(code == n, count(own_codes <= n) - 1.0, hi_all)
     hi_all = hi_all.astype(jnp.int32)
-    stats = stats_in[...]
-
-    def stream(h, tile):
+    stats = [ref[...] for ref in stats_in]
+
+    def stream(h, tile, r):
         window = win_ref[core * p.all + h]
-        lse, rowdot = stats_of(p, stats, h)
+        lse, rowdot = stats_of(p, stats[r], h)
         rows = slice(tile * L, (tile + 1) * L)
         k, v = ks[h, rows, :], vs[h, rows, :]
-        q, g = qs[h], gs[h]
+        after = slice(r * L, (r + 1) * L)
+        q, g = qs[h, after, :], gs[h, after, :]
         score = dot_t(k, q)
         grad_prob = dot_t(v, g)
         yield
         phi_q = feature(q.astype(f32)).astype(bf16)
         kf = k.astype(f32)
-        grad_num = gn[h]
+        grad_num = grads[r][h]
         a = dot_t(feature(kf).astype(bf16), phi_q)
         b = dot_t(v, grad_num)
         yield
@@ -735,29 +717,28 @@
         dk = dk + slope(kf) * dot(b, phi_q)
         dv = dv + dot(a, grad_num)
         if r == 0:
-            dk_o[h] = dk_i[h, rows, :] + dk
-            dv_o[h] = dv_i[h, rows, :] + dv
-        else:
-            dk_o[h, rows, :] = dk
-            dv_o[h, rows, :] = dv
-
-    drive(stream(h, tile) for h in range(p.all) for tile in range(r + 1))
-
-
-def own_keys(p, r, core, windows, near, gn, stats, carried=()):
+            dk += dk_o[h, rows, :]
+            dv += dv_o[h, rows, :]
+        dk_o[h, rows, :] = dk
+        dv_o[h, rows, :] = dv
+
+    pairs = ((0, 1), (1, 1), (0, 0))
+    drive(stream(h, tile, r) for tile, r in pairs for h in range(p.all))
+
+
+def own_keys(p, core, windows, near, grads, stats):
     vmem = pl.BlockSpec(memory_space=pltpu.VMEM)
     smem = pl.BlockSpec(memory_space=pltpu.SMEM)
-    full = jax.ShapeDtypeStruct((p.all, p.chip if r else p.length, p.width), f32)
-    args = [*near[:3], gn, stats, *carried]
+    full = jax.ShapeDtypeStruct((p.all, p.chip, p.width), f32)
+    args = [*near[:3], *grads, *stats]
     keys = pltpu.VMEM((p.all, p.chip, p.width), bf16)
-    tile = pltpu.VMEM((p.all, p.length, p.width), bf16)
     return pl.pallas_call(
-        functools.partial(own_body, p, r),
+        functools.partial(own_body, p),
         out_shape=[full, full],
         in_specs=[smem, smem] + [vmem] * len(args),
         out_specs=[vmem] * 2,
-        scratch_shapes=[keys, keys, tile, tile],
-        **params(4.0 if r else 2.0),
+        scratch_shapes=[keys] * 4,
+        **params(5.0),
         name="own_keys",
     )(core, windows, *args)
 
@@ -765,7 +746,7 @@
 def later_body(p, core_ref, win_ref, *refs):
     near, refs = refs[:5], refs[5:]
     far, refs = refs[: p.far_refs], refs[p.far_refs :]
-    (message_1, message_2), sums, refs = refs[:2], (refs[2:4], refs[4:6]), refs[6:]
+    (message_1, message_2, dk_i, dv_i), refs = refs[:4], refs[4:]
     if p.far:
         far_ref, refs = refs[0], refs[1:]
     keep, send, ks, vs, qs, gs, first, second = refs
@@ -806,7 +787,6 @@
         wide = C + N if far_here else C
         rows = slice(r * L, (r + 1) * L)
         uses = code[rows] == first_next
-        dk_i, dv_i = sums[r]
         window = win_ref[core * p.all + h]
         lse, rowdot = (
             jnp.concatenate(x, axis=1) for x in zip(*(stats_of(p, tile, h) for tile in tiles[: wide // L]))
@@ -985,7 +965,6 @@
         p, core, window_size, near, far_keys, far_before, near_queries, far_queries
     )
     message, grad_1 = lax.optimization_barrier((message, grad_1))
-    sums_1 = own_keys(p, 1, core, window_size, near, grad_1, stats_1)
     messages = (
         move(message, lambda c, i: (c - 1, i)),
         move(message, lambda c, i: (c - 2, i)),
@@ -994,9 +973,9 @@
         state = message[: p.state_rows].reshape(p.all, p.width, p.width)
         far_after = folded(chip_ends, state, True).reshape(-1, p.width)
     keep_q, send_q = finish()
-    sums_0 = own_keys(p, 0, core, window_size, near, grad_0, stats_0, sums_1)
+    sums = own_keys(p, core, window_size, near, (grad_0, grad_1), (stats_0, stats_1))
     keep_k, send_k = later_keys(
-        p, core, window_size, (*own, *near_queries), far_queries, messages, (*sums_0, *sums_1), far_after
+        p, core, window_size, (*own, *near_queries), far_queries, messages, sums, far_after
     )
     attended, grad_queries = unpack(p, core, keep_q, move(send_q, lambda c, i: (c, 1 - i)))
     grad_keys, grad_values = unpack(p, core, keep_k, move(send_k, lambda c, i: (c, 1 - i)))

time: 75.3 us -> 73.6 us (0.977)
  Pallas kernels: 33.9 us -> 32.1 us
  waiting for transfers between devices: 14 us -> 15.5 us
  starting transfers between devices: 23.5 us -> 22.7 us
    ppermute x11, waiting for transfers between devices: 14 us -> 15.5 us  [move(): return lax.ppermute(x, AXES, pairs)]
    pallas_call x2 -> x1, Pallas kernels: 5.64 us -> 4.75 us  [own_keys(): pl.pallas_call(functools.partial(own_body, p), out_shape=[full, full], in...]
    ppermute x11, starting transfers between devices: 23.5 us -> 22.7 us  [move(): return lax.ppermute(x, AXES, pairs)]
    pallas_call x4 -> x3, Pallas kernels: 16.7 us -> 15.8 us  [kernel(): pl.pallas_call(functools.partial(body, p), out_shape=[jax.ShapeDtypeStruc...]
  transfers between devices with their start and end apart: 11 -> 11, of which waited for: 5 -> 6; matrix products, arithmetic and copies ran while one was open for 0% -> 0% of each run, Pallas kernels for 39% -> 37%
where the time goes in v5:
time: 73.6 us; the launch traced here: 73.2 us
  Pallas kernels  32.1 us (44%)
  starting transfers between devices  22.7 us (31%)
  waiting for transfers between devices  15.5 us (21%)
  local copies, waits for them, and re-layouts  2.09 us (3%)
  between operations  0.81 us (1%)
    ppermute x11, starting transfers between devices, move(): return lax.ppermute(x, AXES, pairs)  22.7 us
    pallas_call x3, Pallas kernels, kernel(): pl.pallas_call(functools.partial(body, p), out_shape=[jax.ShapeDtypeStruc...  15.8 us
    ppermute x11, waiting for transfers between devices, move(): return lax.ppermute(x, AXES, pairs)  15.5 us
    pallas_call x1, Pallas kernels, later_keys(): pl.pallas_call(functools.partial(later_body, p), out_shape=[both, both],...  4.95 us
    pallas_call x1, Pallas kernels, own_keys(): pl.pallas_call(functools.partial(own_body, p), out_shape=[full, full], in...  4.75 us
    pallas_call x1, Pallas kernels, pack(): pl.pallas_call(functools.partial(pack_body, p), out_shape=[jax.ShapeDtype...  3.84 us
    pallas_call x2, Pallas kernels, unpack(): pl.pallas_call(functools.partial(unpack_body, p), out_shape=[out, out], i...  2.68 us
    unnamed x6, local copies, waits for them, and re-layouts  2.09 us
  transfers between devices with their start and end apart: 11, of which 6 were waited for; matrix products, arithmetic and copies ran while one was open for 0% of the time, Pallas kernels for 37%

profile of v5, /device:TPU:9, one launch (start us, length us, event | category | flops | bytes accessed | tf_op | source)
XLA Modules:
  0.0 73.2 jit_solution(6797562809401114077)
XLA Ops:
  0.6 3.8 %pack.1 = (bf16[4112,128]{1,0:T(8,128)(2,1)}, bf16[2064,128]{1,0:T(8,128)(2,1)}, bf16[2064,128]{1,0:T(8,128)(2,1)}, bf16[2064,128]{1,0:T(8,128)(2,1)}, bf16[2064,128]{1,0:T(8,128)(2,1)}) custom-call(s32[1]{0:T(128)} %bitcast.core_ref, bf16[256,8,128]{2,1,0:T(8,128)(2,1)} %q_ref.1, bf16[256,8,128]{2,1,0:T(8,128)(2,1)} %k_ref.1, bf16[256,8,128]{2,1,0:T(8,128)(2,1)} %v_ref.1, ...), custom_call_target="tpu_custom_call" | custom-call | tf_op jit(solution)/shard_map/pack/pallas_call | solution.py:158
  4.5 0.7 %collective-permute-start = (bf16[4112,128]{1,0:T(8,128)(2,1)}, bf16[4112,128]{1,0:T(8,128)(2,1)S(1)}, u32[]{:S(2)}, u32[]{:S(2)}) collective-permute-start(bf16[4112,128]{1,0:T(8,128)(2,1)} %get-tuple-element.44), channel_id=1, source_target_pairs={{0,1},{1,0},{4,5},{5,4},{8,9},{9,8},{12,13},{13,12},{2,3},{3,2},{6... | collective-permute-start | bytes 3158024 | tf_op jit(solution)/shard_map/ppermute | solution.py:908
  5.2 3.2 %collective-permute-start.1 = (bf16[2064,128]{1,0:T(8,128)(2,1)}, bf16[2064,128]{1,0:T(8,128)(2,1)S(1)}, u32[]{:S(2)}, u32[]{:S(2)}) collective-permute-start(bf16[2064,128]{1,0:T(8,128)(2,1)} %get-tuple-element.45.own_keys.refs_1_), channel_id=1, source_target_pairs={{0,4},{1,5},{4,8},{5,9},{8,12},{9,13},{2,6},{3,7},{6,10},{7,11},{1... | collective-permute-start | bytes 1585160 | tf_op jit(solution)/shard_map/ppermute | solution.py:908
  8.4 2.1 %collective-permute-start.4 = (bf16[2064,128]{1,0:T(8,128)(2,1)}, bf16[2064,128]{1,0:T(8,128)(2,1)S(1)}, u32[]{:S(2)}, u32[]{:S(2)}) collective-permute-start(bf16[2064,128]{1,0:T(8,128)(2,1)} %get-tuple-element.46.own_queries.refs_2_), channel_id=1, source_target_pairs={{4,0},{5,1},{8,4},{9,5},{12,8},{13,9},{6,2},{7,3},{10,6},{11,7},{1... | collective-permute-start | bytes 1585160 | tf_op jit(solution)/shard_map/ppermute | solution.py:908
  10.5 3.6 %collective-permute-start.2 = (bf16[2064,128]{1,0:T(8,128)(2,1)}, bf16[2064,128]{1,0:T(8,128)(2,1)S(1)}, u32[]{:S(2)}, u32[]{:S(2)}) collective-permute-start(bf16[2064,128]{1,0:T(8,128)(2,1)} %get-tuple-element.49), channel_id=1, source_target_pairs={{0,5},{1,4},{4,9},{5,8},{8,13},{9,12},{2,7},{3,6},{6,11},{7,10},{1... | collective-permute-start | bytes 1585160 | tf_op jit(solution)/shard_map/ppermute | solution.py:908
  14.2 1.9 %collective-permute-start.5 = (bf16[2064,128]{1,0:T(8,128)(2,1)}, bf16[2064,128]{1,0:T(8,128)(2,1)S(1)}, u32[]{:S(2)}, u32[]{:S(2)}) collective-permute-start(bf16[2064,128]{1,0:T(8,128)(2,1)} %get-tuple-element.59), channel_id=1, source_target_pairs={{4,1},{5,0},{8,5},{9,4},{12,9},{13,8},{6,3},{7,2},{10,7},{11,6},{1... | collective-permute-start | bytes 1585160 | tf_op jit(solution)/shard_map/ppermute | solution.py:908
  16.2 1.0 %copy-done = bf16[2064,128]{1,0:T(8,128)(2,1)S(1)} copy-done((bf16[2064,128]{1,0:T(8,128)(2,1)S(1)}, bf16[2064,128]{1,0:T(8,128)(2,1)}, u32[]{:S(2)}) %copy-start) | copy-done | bytes 528408
  17.2 1.0 %copy-done.1 = bf16[2064,128]{1,0:T(8,128)(2,1)S(1)} copy-done((bf16[2064,128]{1,0:T(8,128)(2,1)S(1)}, bf16[2064,128]{1,0:T(8,128)(2,1)}, u32[]{:S(2)}) %copy-start.1) | copy-done | bytes 528408
  18.3 2.6 %collective-permute-done.1.refs_3_ = bf16[2064,128]{1,0:T(8,128)(2,1)S(1)} collective-permute-done((bf16[2064,128]{1,0:T(8,128)(2,1)}, bf16[2064,128]{1,0:T(8,128)(2,1)S(1)}, u32[]{:S(2)}, u32[]{:S(2)}) %collective-permute-start.1) | collective-permute-done | bytes 528416 | tf_op jit(solution)/shard_map/ppermute | solution.py:908
  20.9 2.9 %collective-permute-done.4.refs_3_ = bf16[2064,128]{1,0:T(8,128)(2,1)S(1)} collective-permute-done((bf16[2064,128]{1,0:T(8,128)(2,1)}, bf16[2064,128]{1,0:T(8,128)(2,1)S(1)}, u32[]{:S(2)}, u32[]{:S(2)}) %collective-permute-start.4) | collective-permute-done | bytes 528416 | tf_op jit(solution)/shard_map/ppermute | solution.py:908
  23.8 1.3 %collective-permute-start.7 = (bf16[1424,128]{1,0:T(8,128)(2,1)S(1)}, bf16[1424,128]{1,0:T(8,128)(2,1)S(1)}, u32[]{:S(2)}, u32[]{:S(2)}) collective-permute-start(bf16[1424,128]{1,0:T(8,128)(2,1)S(1)} %get-tuple-element.72), channel_id=1, source_target_pairs={{8,0},{9,1},{12,4},{13,5},{10,2},{11,3},{14,6},{15,7},{24,16},{25,... | collective-permute-start | bytes 1093640 | tf_op jit(solution)/shard_map/ppermute | solution.py:908
  25.1 4.9 %collective-permute-start.3 = (bf16[1424,128]{1,0:T(8,128)(2,1)S(1)}, bf16[1424,128]{1,0:T(8,128)(2,1)S(1)}, u32[]{:S(2)}, u32[]{:S(2)}) collective-permute-start(bf16[1424,128]{1,0:T(8,128)(2,1)S(1)} %get-tuple-element.50), channel_id=1, source_target_pairs={{0,8},{1,9},{4,12},{5,13},{2,10},{3,11},{6,14},{7,15},{16,24},{17,... | collective-permute-start | bytes 1093640 | tf_op jit(solution)/shard_map/ppermute | solution.py:908
  30.0 3.0 %collective-permute-done.2.refs_4_ = bf16[2064,128]{1,0:T(8,128)(2,1)S(1)} collective-permute-done((bf16[2064,128]{1,0:T(8,128)(2,1)}, bf16[2064,128]{1,0:T(8,128)(2,1)S(1)}, u32[]{:S(2)}, u32[]{:S(2)}) %collective-permute-start.2) | collective-permute-done | bytes 528416 | tf_op jit(solution)/shard_map/ppermute | solution.py:908
  33.1 8.1 %second_body.1 = (bf16[2,4,256,128]{3,2,1,0:T(8,128)(2,1)S(1)}, bf16[4,256,128]{2,1,0:T(8,128)(2,1)S(1)}, f32[16,128]{1,0:T(8,128)S(1)}, f32[512,128]{1,0:T(8,12...) custom-call(s32[1]{0:T(128)} %bitcast.core_ref, ...), custom_call_target="tpu_custom_call" | custom-call | flops 9200000000 | bytes 8000000 | tf_op jit(solution)/shard_map/second_body/pallas_call | solution.py:598
  41.2 5.7 %collective-permute-done.3.refs_5_ = bf16[1424,128]{1,0:T(8,128)(2,1)S(1)} collective-permute-done((bf16[1424,128]{1,0:T(8,128)(2,1)S(1)}, bf16[1424,128]{1,0:T(8,128)(2,1)S(1)}, u32[]{:S(2)}, u32[]{:S(2)}) %collective-permute-start.3) | collective-permute-done | bytes 364576 | tf_op jit(solution)/shard_map/ppermute | solution.py:908
  47.0 4.3 %first_body.1 = (bf16[4,256,128]{2,1,0:T(8,128)(2,1)S(1)}, bf16[4,256,128]{2,1,0:T(8,128)(2,1)S(1)}, f32[16,128]{1,0:T(8,128)S(1)}, f32[4,256,128]{2,1,0:T(8,128...) custom-call(s32[1]{0:T(128)} %bitcast.core_ref, s32[8]{0:T(128)S(1)} %copy-done.2, ...), custom_call_target="tpu_custom_call" | custom-call | flops 2300000000 | bytes 2000000 | tf_op jit(solution)/shard_map/first_body/pallas_call | solution.py:598
  51.3 1.3 %collective-permute-start.9 = (bf16[608,128]{1,0:T(8,128)(2,1)S(1)}, bf16[608,128]{1,0:T(8,128)(2,1)S(1)}, u32[]{:S(2)}, u32[]{:S(2)}) collective-permute-start(bf16[608,128]{1,0:T(8,128)(2,1)S(1)} %get-tuple-element.75), channel_id=1, source_target_pairs={{8,0},{9,1},{12,4},{13,5},{10,2},{11,3},{14,6},{15,7},{24,16},{25,... | collective-permute-start | bytes 466952 | tf_op jit(solution)/shard_map/ppermute | solution.py:908
  52.6 1.9 %collective-permute-start.8 = (bf16[608,128]{1,0:T(8,128)(2,1)S(1)}, bf16[608,128]{1,0:T(8,128)(2,1)S(1)}, u32[]{:S(2)}, u32[]{:S(2)}) collective-permute-start(bf16[608,128]{1,0:T(8,128)(2,1)S(1)} %get-tuple-element.75), channel_id=1, source_target_pairs={{4,0},{5,1},{8,4},{9,5},{12,8},{13,9},{6,2},{7,3},{10,6},{11,7},{1... | collective-permute-start | bytes 466952 | tf_op jit(solution)/shard_map/ppermute | solution.py:908
  54.5 3.4 %grad_body.1 = (bf16[2,4,256,128]{3,2,1,0:T(8,128)(2,1)S(1)}, bf16[2,4,256,128]{3,2,1,0:T(8,128)(2,1)S(1)}) custom-call(s32[1]{0:T(128)} %bitcast.core_ref, s32[8]{0:T(128)S(1)} %copy-done.2, bf16[4112,128]{1,0:T(8,128)(2,1)S(1)} %collective-permute-done.pair.refs_0_, bf16[2064,128]{1,0:T(8,128)(2,1)S(1)} %copy-done, bf16[2064,128]{1,0:T(8,128)(2,1)S(1)} %copy-done.1, ...), custom_call_target="tpu_custom_call" | custom-call | flops 4024999936 | bytes 3500000 | tf_op jit(solution)/shard_map/grad_body/pallas_call | solution.py:598
  57.9 1.6 %collective-permute-start.6 = (bf16[2,4,256,128]{3,2,1,0:T(8,128)(2,1)S(1)}, bf16[2,4,256,128]{3,2,1,0:T(8,128)(2,1)S(1)}, u32[]{:S(2)}, u32[]{:S(2)}) collective-permute-start(bf16[2,4,256,128]{3,2,1,0:T(8,128)(2,1)S(1)} %get-tuple-element.69), channel_id=1, source_target_pairs={{0,1},{1,0},{4,5},{5,4},{8,9},{9,8},{12,13},{13,12},{2,3},{3,2},{6... | collective-permute-start | bytes 1572872 | tf_op jit(solution)/shard_map/ppermute | solution.py:908
  59.5 4.8 %own_keys.1 = (f32[4,512,128]{2,1,0:T(8,128)S(1)}, f32[4,512,128]{2,1,0:T(8,128)S(1)}) custom-call(s32[1]{0:T(128)} %bitcast.core_ref, s32[8]{0:T(128)S(1)} %copy-done.2, bf16[4112,128]{1,0:T(8,128)(2,1)S(1)} %collective-permute-done.pair.refs_0_, bf16[2064,128]{1,0:T(8,128)(2,1)S(1)} %copy-done, bf16[2064,128]{1,0:T(8,128)(2,1)S(1)} %copy-done.1, ...), custom_call_target="tpu_custom_call" | custom-call | flops 5750000128 | bytes 5000000 | tf_op jit(solution)/shard_map/own_keys/pallas_call | solution.py:735
  64.9 5.0 %later_keys.1 = (bf16[2,4,256,128]{3,2,1,0:T(8,128)(2,1)S(1)}, bf16[2,4,256,128]{3,2,1,0:T(8,128)(2,1)S(1)}) custom-call(s32[1]{0:T(128)} %bitcast.core_ref, s32[8]{0:T(128)S(1)} %copy-done.2, bf16[4112,128]{1,0:T(8,128)(2,1)S(1)} %collective-permute-done.pair.refs_0_, bf16[2064,128]{1,0:T(8,128)(2,1)S(1)} %copy-done, bf16[2064,128]{1,0:T(8,128)(2,1)S(1)} %copy-done.1, ...), custom_call_target="tpu_custom_call" | custom-call | flops 6325000192 | bytes 5500000 | tf_op jit(solution)/shard_map/later_keys/pallas_call | solution.py:840
  70.0 1.3 %unpack.2 = (bf16[256,8,128]{2,1,0:T(8,128)(2,1)}, bf16[256,8,128]{2,1,0:T(8,128)(2,1)}) custom-call(s32[1]{0:T(128)} %bitcast.core_ref, bf16[2,4,256,128]{3,2,1,0:T(8,128)(2,1)S(1)} %get-tuple-element.68.mine, bf16[2,4,256,128]{3,2,1,0:T(8,128)(2,1)S(1)} %collective-permute-done.6.theirs), custom_call_target="tpu_custom_call" | custom-call | flops 1610000000 | bytes 1400000 | tf_op jit(solution)/shard_map/unpack/pallas_call | solution.py:864
  71.9 1.3 %unpack.3 = (bf16[256,8,128]{2,1,0:T(8,128)(2,1)}, bf16[256,8,128]{2,1,0:T(8,128)(2,1)}) custom-call(s32[1]{0:T(128)} %bitcast.core_ref, bf16[2,4,256,128]{3,2,1,0:T(8,128)(2,1)S(1)} %get-tuple-element.80.mine, bf16[2,4,256,128]{3,2,1,0:T(8,128)(2,1)S(1)} %collective-permute-done.10.theirs), custom_call_target="tpu_custom_call" | custom-call | flops 1610000000 | bytes 1400000 | tf_op jit(solution)/shard_map/unpack/pallas_call | solution.py:864
  (13 shorter events, 1.3 us)
Async XLA Ops:
  4.5 11.7 %collective-permute-start = (bf16[4112,128]{1,0:T(8,128)(2,1)}, bf16[4112,128]{1,0:T(8,128)(2,1)S(1)}, u32[]{:S(2)}, u32[]{:S(2)}) collective-permute-start(bf16[4112,128]{1,0:T(8,128)(2,1)} %get-tuple-element.44), channel_id=1, source_target_pairs={{0,1},{1,0},{4,5},{5,4},{8,9},{9,8},{12,13},{13,12},{2,3},{3,2},{6... | collective-permute-start | bytes 3158024 | tf_op jit(solution)/shard_map/ppermute | solution.py:908
  5.2 15.7 %collective-permute-start.1 = (bf16[2064,128]{1,0:T(8,128)(2,1)}, bf16[2064,128]{1,0:T(8,128)(2,1)S(1)}, u32[]{:S(2)}, u32[]{:S(2)}) collective-permute-start(bf16[2064,128]{1,0:T(8,128)(2,1)} %get-tuple-element.45.own_keys.refs_1_), channel_id=1, source_target_pairs={{0,4},{1,5},{4,8},{5,9},{8,12},{9,13},{2,6},{3,7},{6,10},{7,11},{1... | collective-permute-start | bytes 1585160 | tf_op jit(solution)/shard_map/ppermute | solution.py:908
  8.4 15.4 %collective-permute-start.4 = (bf16[2064,128]{1,0:T(8,128)(2,1)}, bf16[2064,128]{1,0:T(8,128)(2,1)S(1)}, u32[]{:S(2)}, u32[]{:S(2)}) collective-permute-start(bf16[2064,128]{1,0:T(8,128)(2,1)} %get-tuple-element.46.own_queries.refs_2_), channel_id=1, source_target_pairs={{4,0},{5,1},{8,4},{9,5},{12,8},{13,9},{6,2},{7,3},{10,6},{11,7},{1... | collective-permute-start | bytes 1585160 | tf_op jit(solution)/shard_map/ppermute | solution.py:908
  10.5 22.5 %collective-permute-start.2 = (bf16[2064,128]{1,0:T(8,128)(2,1)}, bf16[2064,128]{1,0:T(8,128)(2,1)S(1)}, u32[]{:S(2)}, u32[]{:S(2)}) collective-permute-start(bf16[2064,128]{1,0:T(8,128)(2,1)} %get-tuple-element.49), channel_id=1, source_target_pairs={{0,5},{1,4},{4,9},{5,8},{8,13},{9,12},{2,7},{3,6},{6,11},{7,10},{1... | collective-permute-start | bytes 1585160 | tf_op jit(solution)/shard_map/ppermute | solution.py:908
  14.2 18.9 %copy-start.2 = (s32[8]{0:T(128)S(1)}, s32[8]{0:T(128)}, u32[]{:S(2)}) copy-start(s32[8]{0:T(128)} %win_ref.9) | copy-start | bytes 100
  14.2 27.0 %collective-permute-start.5 = (bf16[2064,128]{1,0:T(8,128)(2,1)}, bf16[2064,128]{1,0:T(8,128)(2,1)S(1)}, u32[]{:S(2)}, u32[]{:S(2)}) collective-permute-start(bf16[2064,128]{1,0:T(8,128)(2,1)} %get-tuple-element.59), channel_id=1, source_target_pairs={{4,1},{5,0},{8,5},{9,4},{12,9},{13,8},{6,3},{7,2},{10,7},{11,6},{1... | collective-permute-start | bytes 1585160 | tf_op jit(solution)/shard_map/ppermute | solution.py:908
  16.2 1.0 %copy-start = (bf16[2064,128]{1,0:T(8,128)(2,1)S(1)}, bf16[2064,128]{1,0:T(8,128)(2,1)}, u32[]{:S(2)}) copy-start(bf16[2064,128]{1,0:T(8,128)(2,1)} %get-tuple-element.45.own_keys.refs_1_) | copy-start | bytes 1585156
  17.2 1.0 %copy-start.1 = (bf16[2064,128]{1,0:T(8,128)(2,1)S(1)}, bf16[2064,128]{1,0:T(8,128)(2,1)}, u32[]{:S(2)}) copy-start(bf16[2064,128]{1,0:T(8,128)(2,1)} %get-tuple-element.46.own_queries.refs_2_) | copy-start | bytes 1585156
  23.8 40.5 %collective-permute-start.7 = (bf16[1424,128]{1,0:T(8,128)(2,1)S(1)}, bf16[1424,128]{1,0:T(8,128)(2,1)S(1)}, u32[]{:S(2)}, u32[]{:S(2)}) collective-permute-start(bf16[1424,128]{1,0:T(8,128)(2,1)S(1)} %get-tuple-element.72), channel_id=1, source_target_pairs={{8,0},{9,1},{12,4},{13,5},{10,2},{11,3},{14,6},{15,7},{24,16},{25,... | collective-permute-start | bytes 1093640 | tf_op jit(solution)/shard_map/ppermute | solution.py:908
  25.1 21.9 %collective-permute-start.3 = (bf16[1424,128]{1,0:T(8,128)(2,1)S(1)}, bf16[1424,128]{1,0:T(8,128)(2,1)S(1)}, u32[]{:S(2)}, u32[]{:S(2)}) collective-permute-start(bf16[1424,128]{1,0:T(8,128)(2,1)S(1)} %get-tuple-element.50), channel_id=1, source_target_pairs={{0,8},{1,9},{4,12},{5,13},{2,10},{3,11},{6,14},{7,15},{16,24},{17,... | collective-permute-start | bytes 1093640 | tf_op jit(solution)/shard_map/ppermute | solution.py:908
  51.3 13.0 %collective-permute-start.9 = (bf16[608,128]{1,0:T(8,128)(2,1)S(1)}, bf16[608,128]{1,0:T(8,128)(2,1)S(1)}, u32[]{:S(2)}, u32[]{:S(2)}) collective-permute-start(bf16[608,128]{1,0:T(8,128)(2,1)S(1)} %get-tuple-element.75), channel_id=1, source_target_pairs={{8,0},{9,1},{12,4},{13,5},{10,2},{11,3},{14,6},{15,7},{24,16},{25,... | collective-permute-start | bytes 466952 | tf_op jit(solution)/shard_map/ppermute | solution.py:908
  52.6 12.3 %collective-permute-start.8 = (bf16[608,128]{1,0:T(8,128)(2,1)S(1)}, bf16[608,128]{1,0:T(8,128)(2,1)S(1)}, u32[]{:S(2)}, u32[]{:S(2)}) collective-permute-start(bf16[608,128]{1,0:T(8,128)(2,1)S(1)} %get-tuple-element.75), channel_id=1, source_target_pairs={{4,0},{5,1},{8,4},{9,5},{12,8},{13,9},{6,2},{7,3},{10,6},{11,7},{1... | collective-permute-start | bytes 466952 | tf_op jit(solution)/shard_map/ppermute | solution.py:908
  57.9 12.0 %collective-permute-start.6 = (bf16[2,4,256,128]{3,2,1,0:T(8,128)(2,1)S(1)}, bf16[2,4,256,128]{3,2,1,0:T(8,128)(2,1)S(1)}, u32[]{:S(2)}, u32[]{:S(2)}) collective-permute-start(bf16[2,4,256,128]{3,2,1,0:T(8,128)(2,1)S(1)} %get-tuple-element.69), channel_id=1, source_target_pairs={{0,1},{1,0},{4,5},{5,4},{8,9},{9,8},{12,13},{13,12},{2,3},{3,2},{6... | collective-permute-start | bytes 1572872 | tf_op jit(solution)/shard_map/ppermute | solution.py:908
  69.9 2.0 %collective-permute-start.10 = (bf16[2,4,256,128]{3,2,1,0:T(8,128)(2,1)S(1)}, bf16[2,4,256,128]{3,2,1,0:T(8,128)(2,1)S(1)}, u32[]{:S(2)}, u32[]{:S(2)}) collective-permute-start(bf16[2,4,256,128]{3,2,1,0:T(8,128)(2,1)S(1)} %get-tuple-element.81), channel_id=1, source_target_pairs={{0,1},{1,0},{4,5},{5,4},{8,9},{9,8},{12,13},{13,12},{2,3},{3,2},{6... | collective-permute-start | bytes 1572872 | tf_op jit(solution)/shard_map/ppermute | solution.py:908
